TPU v7x, 32 devices: a whole 2x2x4 slice. The times are simulated.
32 devices in a mesh: facet: 8 (over z, y), chan: 4 (over x, core).
Axes of the slice: x: 2, y: 2, z: 4, core: 2. Of those that a mesh axis runs over, the one named last changes fastest.
Arguments:
- taylor: float32 [8, 4, 4, 8192], P('facet', 'chan'), may hold values from -6 to 6
- chan_coord: float32 [4], replicated, may hold values from -1 to 1
- sub_offset: int32 [4, 2], replicated, may hold values from 0 to 65535
- sub_owner: int32 [4], replicated, may hold values from 0 to 7, as said below
- tile_list: int32 [128], P('facet'), may hold values from -1 to 127, as said below
- fourier: float32 [128, 4, 64, 256], P('facet', 'chan'), may hold values from -0.5 to 0.5
Outputs:
- visibilities: float32 [128, 4, 256], P('facet', 'chan')
Inputs may be any that keep to these rules, and one draw needn't show every extreme that they name: `sub_owner`: every position along `facet` owns at most 2 of the listed subgrids, at least one owns exactly 2, and some own none. `tile_list`: on position i along `facet` every entry is -1 where i owns no subgrid, else lies in 0 .. 64 times the number of subgrids i owns, minus one.
All inputs are finite; a program needn't handle non-finite values.
Results may differ from a plain program's by a relative error of at most 0.0003.
Values sent between devices are 32-bit elements; how exact they have to be, the bound alone decides.
No kernel may reach another device: no remote copies, remote signals or barrier semaphores. Data moves between devices by JAX's collectives and lax.ppermute only.
A program may use at most 64 MiB of HBM per device.

v0:
```python
import math

import jax
import jax.numpy as jnp
from jax import lax
from jax.sharding import PartitionSpec as P

FACET = 8192
SIDE = 8
SKY = 65536
WIN = 64
TAYLOR = 4
CAP = 2


precise = lax.Precision.HIGHEST


def phase_index(left_side, right_side, period):
    low_part = left_side % 256
    high_part = left_side // 256
    wrapped = (low_part * right_side + high_part * right_side % 256 * 256) % 65536
    return wrapped % period


def turn_angle(index_values, period):
    return 2.0 * math.pi / period * index_values.astype(jnp.float32)


def taylor_powers(chan_coord, order_count):
    columns = [jnp.ones_like(chan_coord)]
    for degree in range(1, order_count):
        columns.append(columns[-1] * chan_coord)
    return jnp.stack(columns, axis=1)


def inverse_window(window, length):
    indices = jnp.arange(length, dtype=jnp.int32)
    angles = turn_angle(indices[:, None] * indices[None, :] % length, length)
    cosines = jnp.cos(angles)
    sines = jnp.sin(angles)
    real_in = window[..., :length]
    imag_in = window[..., length:]
    real_mid = jnp.einsum("...vu,uw->...vw", real_in, cosines, precision=precise) - jnp.einsum(
        "...vu,uw->...vw", imag_in, sines, precision=precise
    )
    imag_mid = jnp.einsum("...vu,uw->...vw", real_in, sines, precision=precise) + jnp.einsum(
        "...vu,uw->...vw", imag_in, cosines, precision=precise
    )
    real_out = jnp.einsum("...vw,vy->...yw", real_mid, cosines, precision=precise) - jnp.einsum(
        "...vw,vy->...yw", imag_mid, sines, precision=precise
    )
    imag_out = jnp.einsum("...vw,vy->...yw", real_mid, sines, precision=precise) + jnp.einsum(
        "...vw,vy->...yw", imag_mid, cosines, precision=precise
    )
    return jnp.concatenate([real_out, imag_out], axis=-1) / length


def slot_ranks(sub_owner):
    positions = jnp.arange(sub_owner.shape[0], dtype=jnp.int32)
    earlier = positions[None, :] < positions[:, None]
    same_owner = sub_owner[None, :] == sub_owner[:, None]
    return jnp.sum((earlier & same_owner).astype(jnp.int32), axis=1)


def facet_windows(channel_image, offsets, anchor_x, anchor_y):
    row_count, facet_width = channel_image.shape
    column_blocks = facet_width // WIN
    folded = (
        channel_image.reshape(row_count, column_blocks, WIN)
        .transpose(0, 2, 1)
        .reshape(row_count * WIN, column_blocks)
    )
    subgrids = offsets.shape[0]
    group_size = math.gcd(subgrids, 8)
    grouped = offsets.reshape(subgrids // group_size, group_size, 2)
    freq_steps = jnp.arange(WIN, dtype=jnp.int32)
    block_starts = WIN * jnp.arange(column_blocks, dtype=jnp.int32)
    inner_pos = anchor_x + freq_steps
    row_pos = anchor_y + jnp.arange(row_count, dtype=jnp.int32)
    factor = float((facet_width * row_count) ** (-0.5))
    group_width = group_size * WIN

    def one_group(offset_pairs):
        column_freq = ((offset_pairs[:, 0:1] + freq_steps[None, :]) % SKY).reshape(group_width)
        coarse_angle = turn_angle(
            phase_index(block_starts[:, None], column_freq[None, :], SKY), SKY
        )
        lookup = jnp.concatenate([jnp.cos(coarse_angle), -jnp.sin(coarse_angle)], axis=1)
        partial_value = jnp.dot(folded, lookup, precision=precise).reshape(
            row_count, WIN, 2 * group_width
        )
        fine_angle = turn_angle(phase_index(inner_pos[:, None], column_freq[None, :], SKY), SKY)
        cos_fine = jnp.cos(fine_angle)
        sin_fine = jnp.sin(fine_angle)
        real_part = partial_value[..., :group_width]
        imag_part = partial_value[..., group_width:]
        real_x = jnp.sum(real_part * cos_fine + imag_part * sin_fine, axis=1).reshape(
            row_count, group_size, WIN
        )
        imag_x = jnp.sum(imag_part * cos_fine - real_part * sin_fine, axis=1).reshape(
            row_count, group_size, WIN
        )
        row_freq = (offset_pairs[:, 1:2] + freq_steps[None, :]) % SKY
        vertical = turn_angle(phase_index(row_pos[None, None, :], row_freq[:, :, None], SKY), SKY)
        cos_v = jnp.cos(vertical)
        sin_v = jnp.sin(vertical)
        real_w = jnp.einsum("gvr,rgu->gvu", cos_v, real_x, precision=precise) + jnp.einsum(
            "gvr,rgu->gvu", sin_v, imag_x, precision=precise
        )
        imag_w = jnp.einsum("gvr,rgu->gvu", cos_v, imag_x, precision=precise) - jnp.einsum(
            "gvr,rgu->gvu", sin_v, real_x, precision=precise
        )
        return jnp.concatenate([real_w, imag_w], axis=-1) * factor

    return lax.map(one_group, grouped).reshape(subgrids, WIN, 2 * WIN)


def add_sources(received):
    return jnp.sum(received, axis=0)


def local(taylor, chan_coord, sub_offset, sub_owner, tile_list, fourier):
    band_count = lax.axis_size("facet")
    band_index = lax.axis_index("facet")
    chan_index = lax.axis_index("chan")
    row_count = taylor.shape[2]
    powers = taylor_powers(chan_coord, TAYLOR)
    chan_steps = jnp.arange(powers.shape[0], dtype=jnp.int32)
    facet_ids = band_index % (SIDE * SIDE)
    anchor_x = facet_ids % SIDE * FACET
    anchor_y = facet_ids // SIDE * FACET + band_index // (SIDE * SIDE) * row_count
    own_row = jnp.sum(jnp.where((chan_steps == chan_index)[:, None], powers, 0.0), axis=0)
    all_terms = lax.all_gather(taylor, "chan", axis=1, tiled=True)
    channel_image = jnp.einsum("t,trx->rx", own_row, all_terms[0], precision=precise)
    windows = facet_windows(channel_image, sub_offset, anchor_x, anchor_y)
    subgrids = windows.shape[0]
    ranks = slot_ranks(sub_owner)
    flat_windows = windows.reshape(subgrids, 2 * WIN * WIN)
    target = sub_owner * CAP + ranks
    outgoing = (
        jnp.zeros((band_count * CAP, 2 * WIN * WIN), jnp.float32).at[target].set(flat_windows)
    )
    owned = add_sources(
        lax.all_to_all(
            outgoing.reshape(band_count, CAP, 2 * WIN * WIN),
            "facet",
            split_axis=0,
            concat_axis=0,
            tiled=True,
        )
    )
    owned = owned * float(band_count ** (-0.5))
    pictures = inverse_window(owned.reshape(CAP, WIN, 2 * WIN), WIN).reshape(CAP * WIN, 2 * WIN)
    usable = tile_list >= 0
    tile_rows = jnp.take(pictures, jnp.maximum(tile_list, 0), axis=0)
    tile_rows = jnp.where(usable[:, None], tile_rows, 0.0)
    blocks = fourier[:, 0]
    vis_count = blocks.shape[2] // 2
    real_t = tile_rows[:, :WIN]
    imag_t = tile_rows[:, WIN:]
    real_f = blocks[..., :vis_count]
    imag_f = blocks[..., vis_count:]
    real_v = jnp.einsum("by,byz->bz", real_t, real_f, precision=precise) - jnp.einsum(
        "by,byz->bz", imag_t, imag_f, precision=precise
    )
    imag_v = jnp.einsum("by,byz->bz", real_t, imag_f, precision=precise) + jnp.einsum(
        "by,byz->bz", imag_t, real_f, precision=precise
    )
    return jnp.concatenate([real_v, imag_v], axis=-1)[:, None, :]


def solution(mesh):
    return jax.shard_map(
        local,
        mesh=mesh,
        in_specs=(
            P("facet", "chan", None, None),
            P(),
            P(),
            P(),
            P("facet"),
            P("facet", "chan", None, None),
        ),
        out_specs=P("facet", "chan", None),
        check_vma=False,
    )
```

profile of v0, /device:TPU:0, one launch (start us, length us, event | category | flops | bytes accessed | tf_op | source)
XLA Modules:
  0.0 46.9 jit_solution(2784440809477901816)
XLA Ops:
  0.1 0.6 %copy-done.3 = s32[4]{0:T(128)S(1)} copy-done((s32[4]{0:T(128)S(1)}, s32[4]{0:T(128)}, u32[]{:S(2)}) %copy-start.3) | copy-done | bytes 40
  0.9 8.8 %all_gather.3 = f32[1,4,4,8192]{3,2,0,1:T(4,128)S(1)} all-gather(f32[1,1,4,8192]{3,2,0,1:T(4,128)} %bitcast.103), channel_id=1, replica_groups=mesh['facet'=8,'chan'=4] {'chan'}, dimensions={1}, use_global_device_ids=true | all-gather | bytes 655360 | tf_op jit(solution)/shard_map/all_gather | solution.py:134
  9.7 0.5 %reshape.454 = f32[4,128,64,4]{2,1,0,3:T(8,128)S(1)} reshape(f32[4,8192,4]{1,0,2:T(4,128)S(1)} %bitcast.95) | data formatting | bytes 1048576 | tf_op jit(solution)/shard_map/t,trx->rx/dot_general | solution.py:135
  10.3 0.4 copy.52
  10.9 0.7 %copy-done.1 = s32[4,2]{0,1:T(2,128)S(1)} copy-done((s32[4,2]{0,1:T(2,128)S(1)}, s32[4,2]{0,1:T(2,128)}, u32[]{:S(2)}) %copy-start.1) | copy-done | bytes 56
  12.0 1.0 %fusion.89 = f32[1,4,128,64]{2,0,3,1:T(1,128)S(1)} fusion(f32[4,128,64,4]{1,3,2,0:T(4,128)S(1)} %copy.52, f32[4]{0:T(128)S(1)} %fusion.85), kind=kOutput, calls=%fused_computation.160 | convolution fusion | flops 1572864 | bytes 655376 | tf_op jit(solution)/shard_map/t,trx->rx/dot_general | solution.py:135
  13.0 0.7 %fusion.30 = (f32[128,256]{1,0:T(8,128)S(1)}, f32[128,256]{1,0:T(8,128)S(1)}) fusion(s32[128]{0:T(128)S(1)} %get-tuple-element.45, s32[256]{0:T(256)S(1)} %and_select_fusion.3, s32[128]{0:T(128)S(1)} %get-tuple-element.46), kind=kLoop, calls=%fused_computation.68 | loop fusion | flops 1310720 | bytes 264192 | tf_op jit(solution)/shard_map/while/body/eval_jaxpr/cos | solution.py:89
  13.7 0.4 fusion.51
  14.1 0.6 %fusion.8 = f32[4,64,512]{2,1,0:T(8,128)S(1)} fusion(f32[4,64,128]{2,1,0:T(8,128)S(1)} %bitcast.100, f32[128,256]{1,0:T(8,128)S(1)} %get-tuple-element.36, f32[128,256]{1,0:T(8,128)S(1)} %get-tuple-element.34), kind=kOutput, calls=%fused_computation.17 | convolution fusion | flops 201392128 | bytes 917504 | tf_op jit(solution)/shard_map/while/body/eval_jaxpr/dot_general | solution.py:90
  15.0 0.6 %fusion.72 = f32[4,64,64]{2,1,0:T(8,128)S(1)} fusion(f32[4,4,64]{2,1,0:T(4,128)S(1)} %reshape.419, s32[4]{0:T(128)S(1)} %get-tuple-element.49, s32[4,64]{1,0:T(4,128)S(1)} %get-tuple-element.43, s32[4]{0:T(128)S(1)} %get-tuple-element.50), kind=kOutput, calls=%fused_computation.118 | convolution fusion | flops 826368 | bytes 70688 | tf_op jit(solution)/shard_map/while/body/eval_jaxpr/gvr,rgu->gvu/dot_general | solution.py:111
  15.5 0.6 %fusion.76 = f32[4,64,64]{2,1,0:T(8,128)S(1)} fusion(f32[4,4,64]{2,1,0:T(4,128)S(1)} %reshape.418, s32[4]{0:T(128)S(1)} %get-tuple-element.49, s32[4,64]{1,0:T(4,128)S(1)} %get-tuple-element.43, s32[4]{0:T(128)S(1)} %get-tuple-element.50), kind=kOutput, calls=%fused_computation.122 | convolution fusion | flops 826368 | bytes 70688 | tf_op jit(solution)/shard_map/while/body/eval_jaxpr/gvr,rgu->gvu/dot_general | solution.py:108
  16.1 0.6 %convolution_subtract_fusion = f32[4,64,64]{2,1,0:T(8,128)S(1)} fusion(f32[4,64,64]{2,1,0:T(8,128)S(1)} %fusion.72, f32[4,4,64]{2,1,0:T(4,128)S(1)} %reshape.418, s32[4]{0:T(128)S(1)} %get-tuple-element.49, s32[4,64]{1,0:T(4,128)S(1)} %get-tuple-element.43, s32[4]{0:T(128)S(1)} %get-tuple-element.50), kind=kOutput, calls=%fused_computation.2 | convolution fusion | flops 842752 | bytes 136224 | tf_op jit(solution)/shard_map/while/body/eval_jaxpr/gvr,rgu->gvu/dot_general | solution.py:111
  16.6 0.6 %convolution_add_fusion = f32[4,64,64]{2,1,0:T(8,128)S(1)} fusion(f32[4,64,64]{2,1,0:T(8,128)S(1)} %fusion.76, f32[4,4,64]{2,1,0:T(4,128)S(1)} %reshape.419, s32[4]{0:T(128)S(1)} %get-tuple-element.49, s32[4,64]{1,0:T(4,128)S(1)} %get-tuple-element.43, s32[4]{0:T(128)S(1)} %get-tuple-element.50), kind=kOutput, calls=%fused_computation.3 | convolution fusion | flops 842752 | bytes 136224 | tf_op jit(solution)/shard_map/while/body/eval_jaxpr/gvr,rgu->gvu/dot_general | solution.py:108
  17.3 0.9 %scatter_custom_fusion = f32[16,8192]{1,0:T(8,128)S(1)} fusion(s32[4]{0:T(128)S(1)} %compare_select_fusion, f32[]{:T(128)} %constant.233.clone.1, f32[1,4,64,128]{3,2,1,0:T(8,128)S(1)} %fusion.22), kind=kCustom, calls=%fused_computation.22 | custom fusion | bytes 655364 | tf_op jit(solution)/shard_map/scatter | solution.py:142
  18.2 1.1 %reshape.420 = f32[8,2,8192]{2,1,0:T(2,128)} reshape(f32[16,8192]{1,0:T(8,128)S(1)} %scatter_custom_fusion) | data formatting | bytes 1048576 | tf_op jit(solution)/shard_map/reshape | solution.py:146
  19.3 6.0 %all-to-all-start = ((f32[8,2,8192]{2,1,0:T(2,128)}), f32[8,2,8192]{2,1,0:T(2,128)S(1)}, u32[]{:S(2)}, u32[]{:S(2)}) async-start(f32[8,2,8192]{2,1,0:T(2,128)} %reshape.420), calls=%async_computation | async-start | bytes 1048576 | tf_op jit(solution)/shard_map/all_to_all | solution.py:145
  25.3 15.0 %all-to-all-done = f32[8,2,8192]{2,1,0:T(2,128)S(1)} async-done(((f32[8,2,8192]{2,1,0:T(2,128)}), f32[8,2,8192]{2,1,0:T(2,128)S(1)}, u32[]{:S(2)}, u32[]{:S(2)}) %all-to-all-start) | async-done | bytes 524320 | tf_op jit(solution)/shard_map/all_to_all | solution.py:145
  42.3 0.3 convolution_add_fusion.2
  43.4 0.6 %gather_fusion = f32[16,128]{1,0:T(8,128)S(1)} fusion(f32[128,128]{1,0:T(8,128)S(1)} %maximum_multiply_fusion.1, s32[1024]{0:T(1024)S(1)} %pad_clamp_fusion), kind=kCustom, calls=%fused_computation | custom fusion | bytes 16448 | tf_op jit(solution)/shard_map/jit(_take)/gather | solution.py:156
  44.1 0.5 %fusion = f32[16,1,128]{2,1,0:T(1,128)S(1)} fusion(f32[16,64,1]{1,2,0:T(1,128)S(1)} %bitcast.106, f32[16,64,256]{2,1,0:T(8,128)S(1)} %bitcast.91), kind=kOutput, calls=%fused_computation.8 | convolution fusion | flops 1572864 | bytes 540672 | tf_op jit(solution)/shard_map/by,byz->bz/dot_general | solution.py:167
  44.6 0.5 %fusion.6 = f32[16,1,128]{2,1,0:T(1,128)S(1)} fusion(f32[16,64,1]{1,2,0:T(1,128)S(1)} %bitcast.107, f32[16,64,256]{2,1,0:T(8,128)S(1)} %bitcast.92), kind=kOutput, calls=%fused_computation.14 | convolution fusion | flops 1572864 | bytes 540672 | tf_op jit(solution)/shard_map/by,byz->bz/dot_general | solution.py:164
  45.2 0.5 %fusion.4 = f32[16,1,128]{2,1,0:T(1,128)S(1)} fusion(f32[16,64,1]{1,2,0:T(1,128)S(1)} %bitcast.104, f32[16,64,256]{2,1,0:T(8,128)S(1)} %bitcast.93), kind=kOutput, calls=%fused_computation.12 | convolution fusion | flops 1572864 | bytes 540672 | tf_op jit(solution)/shard_map/by,byz->bz/dot_general | solution.py:167
  45.7 0.5 %fusion.2 = f32[16,1,128]{2,1,0:T(1,128)S(1)} fusion(f32[16,64,1]{1,2,0:T(1,128)S(1)} %bitcast.105, f32[16,64,256]{2,1,0:T(8,128)S(1)} %bitcast.94), kind=kOutput, calls=%fused_computation.10 | convolution fusion | flops 1572864 | bytes 540672 | tf_op jit(solution)/shard_map/by,byz->bz/dot_general | solution.py:164
  46.2 0.6 %broadcast_in_dim.83 = f32[16,1,256]{2,1,0:T(1,128)} reshape(f32[16,256]{1,0:T(8,128)S(1)} %pad_maximum_fusion) | data formatting | bytes 32768 | tf_op jit(solution)/shard_map/broadcast_in_dim | solution.py:170
  (44 shorter events, 4.1 us)
Async XLA Ops:
  0.0 0.7 %copy-start.3 = (s32[4]{0:T(128)S(1)}, s32[4]{0:T(128)}, u32[]{:S(2)}) copy-start(s32[4]{0:T(128)} %param.9) | copy-start | bytes 52
  10.2 0.7 %copy-start.2 = (f32[4]{0:T(128)S(1)}, f32[4]{0:T(128)}, u32[]{:S(2)}) copy-start(f32[4]{0:T(128)} %param.7) | copy-start | bytes 52
  10.9 0.7 %copy-start.1 = (s32[4,2]{0,1:T(2,128)S(1)}, s32[4,2]{0,1:T(2,128)}, u32[]{:S(2)}) copy-start(s32[4,2]{0,1:T(2,128)} %param.8) | copy-start | bytes 100
  19.3 6.0 %copy-start.4 = (s32[16]{0:T(128)S(1)}, s32[16]{0:T(128)}, u32[]{:S(2)}) copy-start(s32[16]{0:T(128)} %param.10) | copy-start | bytes 196
  19.3 21.0 %all-to-all-start = ((f32[8,2,8192]{2,1,0:T(2,128)}), f32[8,2,8192]{2,1,0:T(2,128)S(1)}, u32[]{:S(2)}, u32[]{:S(2)}) async-start(f32[8,2,8192]{2,1,0:T(2,128)} %reshape.420), calls=%async_computation | async-start | bytes 1048576 | tf_op jit(solution)/shard_map/all_to_all | solution.py:145
  40.5 3.6 %copy-start = (f32[16,1,64,256]{3,2,1,0:T(8,128)S(1)}, f32[16,1,64,256]{3,2,1,0:T(8,128)}, u32[]{:S(2)}) copy-start(f32[16,1,64,256]{3,2,1,0:T(8,128)} %param.11) | copy-start | bytes 3145732
where the time goes:
time: 47.1 us; the launch traced here: 46.9 us
  waiting for transfers between devices  15 us (32%)
  blocking collectives  8.83 us (19%)
  matrix products  8.6 us (18%)
  local copies, waits for them, and re-layouts  6.01 us (13%)
  starting transfers between devices  5.97 us (13%)
  other arithmetic  2.23 us (5%)
    all_to_all x1, waiting for transfers between devices, local(): lax.all_to_all(outgoing.reshape(band_count, CAP, 2 * WIN * WIN), 'facet',...  15 us
    all_gather x1, blocking collectives, local(): all_terms = lax.all_gather(taylor, 'chan', axis=1, tiled=True)  8.83 us
    all_to_all x1, starting transfers between devices, local(): lax.all_to_all(outgoing.reshape(band_count, CAP, 2 * WIN * WIN), 'facet',...  5.97 us
    unnamed x11, local copies, waits for them, and re-layouts  1.63 us
    reshape x1, local copies, waits for them, and re-layouts, local(): outgoing.reshape(band_count, CAP, 2 * WIN * WIN)  1.08 us
    dot_general x1, matrix products, local(): jnp.einsum('t,trx->rx', own_row, all_terms[0], precision=precise)  0.98 us
  transfers between devices with their start and end apart: 1, of which 1 were waited for; matrix products, arithmetic and copies ran while one was open for 0% of the time, Pallas kernels for 0%

commit v1 on v0

v1 whole, which is shorter than its diff:
```python
import jax
import jax.numpy as jnp
from jax import lax
from jax.sharding import PartitionSpec as P

FACET = 8192
SIDE = 8
SKY = 65536
WIN = 64
TAYLOR = 4

precise = lax.Precision.HIGHEST

SINE = (1.5707963705062866, -0.6459637880325317, 0.07968991994857788, -0.004674150608479977, 0.0001516751217423007)
COSINE = (0.9999999403953552, -1.2336982488632202, 0.2536506950855255, -0.020810570567846298, 0.0008581625297665596)


def turns(index):
    centred = ((index + SKY // 2) & (SKY - 1)) - SKY // 2
    z = centred.astype(jnp.float32) * (2.0 / SKY)
    w = z * z
    half_sin = z * (SINE[0] + w * (SINE[1] + w * (SINE[2] + w * (SINE[3] + w * SINE[4]))))
    half_cos = COSINE[0] + w * (COSINE[1] + w * (COSINE[2] + w * (COSINE[3] + w * COSINE[4])))
    return 1.0 - 2.0 * half_sin * half_sin, 2.0 * half_sin * half_cos


def column_transform(term, offsets, anchor_x):
    row_count, width = term.shape
    lane = 128
    folded = term.reshape(row_count, width // lane, lane).transpose(1, 0, 2).reshape(width // lane * row_count, lane)
    steps = jnp.arange(WIN, dtype=jnp.int32)
    freq = (offsets[:, 0:1] + steps[None, :]).reshape(-1)
    count = freq.shape[0]
    cos_fine, sin_fine = turns(jnp.arange(lane, dtype=jnp.int32)[:, None] * freq[None, :])
    lookup = jnp.concatenate([cos_fine, -sin_fine], axis=1)
    part = jnp.dot(folded, lookup, precision=precise).reshape(width // lane, row_count, 2 * count)
    start = anchor_x + lane * jnp.arange(width // lane, dtype=jnp.int32)
    cos_start, sin_start = turns(start[:, None] * freq[None, :])
    cos_start, sin_start = cos_start[:, None], sin_start[:, None]
    real, imag = part[..., :count], part[..., count:]
    return jnp.concatenate(
        [
            jnp.sum(real * cos_start + imag * sin_start, axis=0),
            jnp.sum(imag * cos_start - real * sin_start, axis=0),
        ],
        axis=1,
    )


def exchange(value, facets, chans, flip_facet, flip_chan):
    pairs = [
        (f * chans + c, (f ^ flip_facet) * chans + (c ^ flip_chan)) for f in range(facets) for c in range(chans)
    ]
    return lax.ppermute(value, ("facet", "chan"), pairs)


def gather_terms(part, facets, chans, band, chan):
    near = SIDE if facets > SIDE else facets
    odd = chan % 2 == 1
    other = exchange(part, facets, chans, 0, 1)
    both = jnp.concatenate([jnp.where(odd, other, part), jnp.where(odd, part, other)], axis=0)
    step = 1
    while step < near:
        both = both + exchange(both, facets, chans, step, 1)
        step *= 2
    blocks = both[None]
    place = chan // 2
    step = 2
    while step < chans:
        other = exchange(blocks, facets, chans, 0, step + 1)
        high = (chan // step) % 2 == 1
        blocks = jnp.concatenate([jnp.where(high, other, blocks), jnp.where(high, blocks, other)], axis=0)
        step *= 2
    terms = blocks.reshape(chans, part.shape[0], part.shape[1])
    if facets == near:
        return terms[None]
    groups = [[h * near + f for h in range(facets // near)] for f in range(near)]
    return lax.all_gather(terms, "facet", axis=0, axis_index_groups=groups)


def transform_blocks(blocks):
    vis = blocks.shape[2] // 2
    steps = jnp.arange(WIN, dtype=jnp.int32)
    cosines, sines = turns(steps[:, None] * steps[None, :] * (SKY // WIN))
    table = jnp.concatenate(
        [jnp.concatenate([cosines, -sines], axis=1), jnp.concatenate([sines, cosines], axis=1)], axis=0
    ) / WIN
    stacked = jnp.concatenate([blocks[..., :vis], blocks[..., vis:]], axis=1)
    out = jnp.einsum("uw,bwz->buz", table, stacked, precision=precise)
    return out[:, :WIN], out[:, WIN:]


def row_weights(tile_list, sub_offset, sub_owner, band, facets, row_count):
    subgrids = sub_owner.shape[0]
    order = jnp.arange(subgrids, dtype=jnp.int32)
    rank = jnp.sum((order[None, :] < order[:, None]) & (sub_owner[None, :] == sub_owner[:, None]), axis=1)
    tile = jnp.maximum(tile_list, 0)
    chosen = (sub_owner[None, :] == band) & (rank[None, :] == (tile // WIN)[:, None]) & (tile_list >= 0)[:, None]
    first_row = jnp.sum(jnp.where(chosen, sub_offset[None, :, 1], 0), axis=1)
    near = SIDE if facets > SIDE else facets
    group = jnp.arange(facets // near, dtype=jnp.int32)
    anchor = group % SIDE * FACET + group // SIDE * row_count
    position = (anchor[:, None] + jnp.arange(row_count, dtype=jnp.int32)[None, :]).reshape(-1)
    v = jnp.arange(WIN, dtype=jnp.int32)
    up = (tile % WIN)[:, None, None] * v[None, None, :] * (SKY // WIN)
    down = (first_row[:, None, None] + v[None, None, :]) * position[None, :, None]
    cosines, sines = turns(up - down)
    scale = float((FACET * row_count * facets) ** -0.5)
    return jnp.sum(cosines, axis=2) * scale, jnp.sum(sines, axis=2) * scale, chosen.astype(jnp.float32)


def local(taylor, chan_coord, sub_offset, sub_owner, tile_list, fourier):
    facets, chans = lax.axis_size("facet"), lax.axis_size("chan")
    band, chan = lax.axis_index("facet"), lax.axis_index("chan")
    row_count = taylor.shape[2]
    subgrids = sub_offset.shape[0]
    anchor_x = band % SIDE * FACET
    part = column_transform(taylor[0, 0], sub_offset, anchor_x)
    fourier_real, fourier_imag = transform_blocks(fourier[:, 0])
    real_a, imag_a, chosen = row_weights(tile_list, sub_offset, sub_owner, band, facets, row_count)
    coord = jnp.sum(jnp.where(jnp.arange(chan_coord.shape[0]) == chan, chan_coord, 0.0))
    powers = [jnp.ones((), jnp.float32)]
    for _ in range(1, TAYLOR):
        powers.append(powers[-1] * coord)
    terms = gather_terms(part, facets, chans, band, chan)
    mixed = sum(powers[t] * terms[:, t] for t in range(TAYLOR))
    mixed = mixed.reshape(-1, 2, subgrids, WIN)
    real_y = jnp.einsum("bs,qsu->bqu", chosen, mixed[:, 0], precision=precise)
    imag_y = jnp.einsum("bs,qsu->bqu", chosen, mixed[:, 1], precision=precise)
    real_t = jnp.sum(real_a[:, :, None] * real_y - imag_a[:, :, None] * imag_y, axis=1)
    imag_t = jnp.sum(real_a[:, :, None] * imag_y + imag_a[:, :, None] * real_y, axis=1)
    real_v = jnp.sum(real_t[:, :, None] * fourier_real - imag_t[:, :, None] * fourier_imag, axis=1)
    imag_v = jnp.sum(real_t[:, :, None] * fourier_imag + imag_t[:, :, None] * fourier_real, axis=1)
    return jnp.concatenate([real_v, imag_v], axis=-1)[:, None, :]


def solution(mesh):
    return jax.shard_map(
        local,
        mesh=mesh,
        in_specs=(
            P("facet", "chan", None, None),
            P(),
            P(),
            P(),
            P("facet"),
            P("facet", "chan", None, None),
        ),
        out_specs=P("facet", "chan", None),
        check_vma=False,
    )
```

time: 47.1 us -> 22.5 us (0.48)
  waiting for transfers between devices: 15 us -> 3.12 us
  blocking collectives: 8.83 us -> 0 us
  matrix products: 8.6 us -> 2.11 us
  starting transfers between devices: 5.97 us -> 9.42 us
  local copies, waits for them, and re-layouts: 6.01 us -> 2.57 us
  between operations: 0.28 us -> 2.19 us
  other arithmetic: 2.23 us -> 2.85 us
    all_to_all x1 -> x0, waiting for transfers between devices: 15 us -> none  [local(): lax.all_to_all(outgoing.reshape(band_count, CAP, 2 * WIN * WIN), 'facet',...]
    ppermute x0 -> x5, starting transfers between devices: none -> 9.42 us  [exchange(): return lax.ppermute(value, ('facet', 'chan'), pairs)]
    all_gather x1 -> x0, blocking collectives: 8.83 us -> none  [local(): all_terms = lax.all_gather(taylor, 'chan', axis=1, tiled=True)]
    dot_general x18 -> x4, matrix products: 8.6 us -> 2.11 us  [the longest x1 1.11 us: transform_blocks(): out = jnp.einsum('uw,bwz->buz', table, stacked, precision=precise)]
    all_to_all x1 -> x0, starting transfers between devices: 5.97 us -> none  [local(): lax.all_to_all(outgoing.reshape(band_count, CAP, 2 * WIN * WIN), 'facet',...]
    ppermute x0 -> x5, waiting for transfers between devices: none -> 3.12 us  [exchange(): return lax.ppermute(value, ('facet', 'chan'), pairs)]
    cos x2 -> x0, other arithmetic: 1.11 us -> none  [the longest x1 0.71 us: one_group(): jnp.cos(coarse_angle)]
    reshape x3 -> x1, local copies, waits for them, and re-layouts: 1.25 us -> 0.15 us  [column_transform(): jnp.dot(folded, lookup, precision=precise)]
  transfers between devices with their start and end apart: 1 -> 5, of which waited for: 1 -> 3; matrix products, arithmetic and copies ran while one was open for 0% -> 11% of each run, Pallas kernels for 0% -> 0%
where the time goes in v1:
time: 22.5 us; the launch traced here: 22.3 us
  starting transfers between devices  9.42 us (42%)
  waiting for transfers between devices  3.12 us (14%)
  other arithmetic  2.85 us (13%)
  local copies, waits for them, and re-layouts  2.57 us (11%)
  between operations  2.19 us (10%)
  matrix products  2.11 us (9%)
    ppermute x5, starting transfers between devices, exchange(): return lax.ppermute(value, ('facet', 'chan'), pairs)  9.42 us
    ppermute x5, waiting for transfers between devices, exchange(): return lax.ppermute(value, ('facet', 'chan'), pairs)  3.12 us
    unnamed x12, local copies, waits for them, and re-layouts  1.49 us
    dot_general x1, matrix products, transform_blocks(): out = jnp.einsum('uw,bwz->buz', table, stacked, precision=precise)  1.11 us
    add x1, other arithmetic, local(): mixed = sum((powers[t] * terms[:, t] for t in range(TAYLOR)))  0.66 us
    broadcast_in_dim x1, local copies, waits for them, and re-layouts, local(): return jnp.concatenate([real_v, imag_v], axis=-1)[:, None, :]  0.62 us
    reduce_sum x1, other arithmetic, local(): jnp.sum(jnp.where(jnp.arange(chan_coord.shape[0]) == chan, chan_coord, 0.0))  0.6 us
    dot_general x1, matrix products, column_transform(): jnp.dot(folded, lookup, precision=precise)  0.59 us
  transfers between devices with their start and end apart: 5, of which 3 were waited for; matrix products, arithmetic and copies ran while one was open for 11% of the time, Pallas kernels for 0%

profile of v1, /device:TPU:0, one launch (start us, length us, event | category | flops | bytes accessed | tf_op | source)
XLA Modules:
  0.0 22.3 jit_solution(12992894372278150775)
XLA Ops:
  0.0 0.7 %copy-done.2 = s32[4,2]{0,1:T(2,128)S(1)} copy-done((s32[4,2]{0,1:T(2,128)S(1)}, s32[4,2]{0,1:T(2,128)}, u32[]{:S(2)}) %copy-start.2) | copy-done | bytes 56
  0.9 0.1 fusion.6
  1.0 0.6 %convolution_bitcast_fusion.1 = f32[256,512]{1,0:T(8,128)S(1)} fusion(f32[256,128]{1,0:T(8,128)S(1)} %bitcast.39, f32[128,256]{1,0:T(8,128)S(1)} %get-tuple-element.26, f32[128,256]{1,0:T(8,128)S(1)} %get-tuple-element.25), kind=kOutput, calls=%fused_computation.1 | convolution fusion | flops 201392128 | bytes 917504 | tf_op jit(solution)/shard_map/dot_general | solution.py:36
  1.6 0.1 reshape.192
  1.8 0.1 fusion.10
  2.0 0.2 add_reduce_fusion.1
  2.2 0.5 %collective-permute-start = (f32[4,512]{1,0:T(4,128)S(1)}, f32[4,512]{1,0:T(4,128)S(1)}, u32[]{:S(2)}, u32[]{:S(2)}) collective-permute-start(f32[4,512]{1,0:T(4,128)S(1)} %pad_maximum_fusion.3), channel_id=1, source_target_pairs={{0,1},{1,0},{2,3},{3,2},{4,5},{5,4},{6,7},{7,6},{8,9},{9,8},{10,11... | collective-permute-start | bytes 24584 | tf_op jit(solution)/shard_map/ppermute | solution.py:54
  2.8 0.6 %copy-done.4 = s32[4]{0:T(128)S(1)} copy-done((s32[4]{0:T(128)S(1)}, s32[4]{0:T(128)}, u32[]{:S(2)}) %copy-start.4) | copy-done | bytes 40
  3.5 0.2 convert_reduce_fusion
  4.0 0.1 fusion.22
  4.2 2.6 %collective-permute-start.1 = (f32[8,512]{1,0:T(8,128)S(1)}, f32[8,512]{1,0:T(8,128)S(1)}, u32[]{:S(2)}, u32[]{:S(2)}) collective-permute-start(f32[8,512]{1,0:T(8,128)S(1)} %pad_maximum_fusion.1), channel_id=1, source_target_pairs={{0,5},{1,4},{2,7},{3,6},{4,1},{5,0},{6,3},{7,2},{8,13},{9,12},{10,... | collective-permute-start | bytes 49160 | tf_op jit(solution)/shard_map/ppermute | solution.py:54
  6.9 1.4 %collective-permute-done.1 = f32[8,512]{1,0:T(8,128)S(1)} collective-permute-done((f32[8,512]{1,0:T(8,128)S(1)}, f32[8,512]{1,0:T(8,128)S(1)}, u32[]{:S(2)}, u32[]{:S(2)}) %collective-permute-start.1) | collective-permute-done | bytes 16416 | tf_op jit(solution)/shard_map/ppermute | solution.py:54
  8.3 2.1 %collective-permute-start.2 = (f32[8,512]{1,0:T(8,128)S(1)}, f32[8,512]{1,0:T(8,128)S(1)}, u32[]{:S(2)}, u32[]{:S(2)}) collective-permute-start(f32[8,512]{1,0:T(8,128)S(1)} %fusion.43), channel_id=1, source_target_pairs={{0,9},{1,8},{2,11},{3,10},{4,13},{5,12},{6,15},{7,14},{8,1},{9,0},... | collective-permute-start | bytes 49160 | tf_op jit(solution)/shard_map/ppermute | solution.py:54
  10.4 1.4 %collective-permute-done.2 = f32[8,512]{1,0:T(8,128)S(1)} collective-permute-done((f32[8,512]{1,0:T(8,128)S(1)}, f32[8,512]{1,0:T(8,128)S(1)}, u32[]{:S(2)}, u32[]{:S(2)}) %collective-permute-start.2) | collective-permute-done | bytes 16416 | tf_op jit(solution)/shard_map/ppermute | solution.py:54
  11.8 2.7 %collective-permute-start.3 = (f32[8,512]{1,0:T(8,128)S(1)}, f32[8,512]{1,0:T(8,128)S(1)}, u32[]{:S(2)}, u32[]{:S(2)}) collective-permute-start(f32[8,512]{1,0:T(8,128)S(1)} %add.482), channel_id=1, source_target_pairs={{0,17},{1,16},{2,19},{3,18},{4,21},{5,20},{6,23},{7,22},{8,25},{9,... | collective-permute-start | bytes 49160 | tf_op jit(solution)/shard_map/ppermute | solution.py:54
  14.5 1.1 %convolution_bitcast_fusion = f32[16,128,128]{2,1,0:T(8,128)S(1)} fusion(f32[16,64,128]{2,1,0:T(8,128)S(1)} %get-tuple-element.16, f32[16,64,128]{2,1,0:T(8,128)S(1)} %get-tuple-element.15, f32[64,64]{1,0:T(8,128)S(1)} %get-tuple-element.30, f32[64,64]{1,0:T(8,128)S(1)} %get-tuple-element.29, f32[64,64]{1,0:T(8,128)S(1)} %fusion.30), kind=kOutput, calls=%fused_computation | convolution fusion | flops 402980864 | bytes 2146304 | tf_op jit(solution)/shard_map/uw,bwz->buz/dot_general | solution.py:89
  15.6 0.3 %collective-permute-done.3 = f32[8,512]{1,0:T(8,128)S(1)} collective-permute-done((f32[8,512]{1,0:T(8,128)S(1)}, f32[8,512]{1,0:T(8,128)S(1)}, u32[]{:S(2)}, u32[]{:S(2)}) %collective-permute-start.3) | collective-permute-done | bytes 16416 | tf_op jit(solution)/shard_map/ppermute | solution.py:54
  16.0 1.5 %collective-permute-start.4 = (f32[1,8,512]{2,1,0:T(8,128)S(1)}, f32[1,8,512]{2,1,0:T(8,128)S(1)}, u32[]{:S(2)}, u32[]{:S(2)}) collective-permute-start(f32[1,8,512]{2,1,0:T(8,128)S(1)} %add_bitcast_fusion), channel_id=1, source_target_pairs={{0,3},{1,2},{2,1},{3,0},{4,7},{5,6},{6,5},{7,4},{8,11},{9,10},{10,... | collective-permute-start | bytes 49160 | tf_op jit(solution)/shard_map/ppermute | solution.py:54
  17.5 0.6 %fusion.39 = f32[]{:T(128)} fusion(f32[4]{0:T(128)S(1)} %copy-done.5, s32[]{:T(128)S(6)} %axis_index.25), kind=kLoop, calls=%fused_computation.97 | loop fusion | flops 11 | bytes 24 | tf_op jit(solution)/shard_map/reduce_sum | solution.py:121
  20.1 0.7 %fusion.33 = f32[1,1,4,512]{3,2,1,0:T(4,128)S(1)} fusion(f32[1,4,4,512]{3,2,1,0:T(4,128)S(1)} %broadcast_in_dim_reshape.2, f32[]{:T(128)S(6)} %mul.693, f32[]{:T(128)S(6)} %mul.690, f32[]{:T(128)} %fusion.39), kind=kLoop, calls=%fused_computation.72 | loop fusion | flops 12288 | bytes 40972 | tf_op jit(solution)/shard_map/add | solution.py:126
  20.8 0.2 fusion.32
  21.0 0.2 subtract_reduce_fusion.2
  21.3 0.4 %subtract_reduce_fusion = (f32[16,128]{1,0:T(8,128)S(1)}, f32[16,128]{1,0:T(8,128)S(1)}) fusion(f32[16,128,128]{2,1,0:T(8,128)S(1)} %convolution_bitcast_fusion, f32[16,64]{1,0:T(8,128)S(1)} %get-tuple-element.10, f32[16,64]{1,0:T(8,128)S(1)} %get-tuple-element.9), kind=kLoop, calls=%fused_computation.6 | loop fusion | flops 1044480 | bytes 1073152 | tf_op jit(solution)/shard_map/reduce_sum | solution.py:132
  21.6 0.6 %broadcast_in_dim.26 = f32[16,1,256]{2,1,0:T(1,128)} reshape(f32[16,256]{1,0:T(8,128)S(1)} %pad_maximum_fusion.2) | data formatting | bytes 32768 | tf_op jit(solution)/shard_map/broadcast_in_dim | solution.py:134
  (37 shorter events, 0.9 us)
Async XLA Ops:
  0.0 1.0 %copy-start = (f32[1,1,4,8192]{3,2,1,0:T(4,128)S(1)}, f32[1,1,4,8192]{3,2,1,0:T(4,128)}, u32[]{:S(2)}) copy-start(f32[1,1,4,8192]{3,2,1,0:T(4,128)} %param.6) | copy-start | bytes 393220
  0.0 0.7 %copy-start.2 = (s32[4,2]{0,1:T(2,128)S(1)}, s32[4,2]{0,1:T(2,128)}, u32[]{:S(2)}) copy-start(s32[4,2]{0,1:T(2,128)} %param.8) | copy-start | bytes 100
  1.6 2.0 %copy-start.1 = (f32[16,1,64,256]{3,2,1,0:T(8,128)S(1)}, f32[16,1,64,256]{3,2,1,0:T(8,128)}, u32[]{:S(2)}) copy-start(f32[16,1,64,256]{3,2,1,0:T(8,128)} %param.11) | copy-start | bytes 3145732
  2.1 0.7 %copy-start.3 = (s32[16]{0:T(128)S(1)}, s32[16]{0:T(128)}, u32[]{:S(2)}) copy-start(s32[16]{0:T(128)} %param.10) | copy-start | bytes 196
  2.2 2.0 %collective-permute-start = (f32[4,512]{1,0:T(4,128)S(1)}, f32[4,512]{1,0:T(4,128)S(1)}, u32[]{:S(2)}, u32[]{:S(2)}) collective-permute-start(f32[4,512]{1,0:T(4,128)S(1)} %pad_maximum_fusion.3), channel_id=1, source_target_pairs={{0,1},{1,0},{2,3},{3,2},{4,5},{5,4},{6,7},{7,6},{8,9},{9,8},{10,11... | collective-permute-start | bytes 24584 | tf_op jit(solution)/shard_map/ppermute | solution.py:54
  2.8 0.7 %copy-start.4 = (s32[4]{0:T(128)S(1)}, s32[4]{0:T(128)}, u32[]{:S(2)}) copy-start(s32[4]{0:T(128)} %param.9) | copy-start | bytes 52
  4.2 4.0 %collective-permute-start.1 = (f32[8,512]{1,0:T(8,128)S(1)}, f32[8,512]{1,0:T(8,128)S(1)}, u32[]{:S(2)}, u32[]{:S(2)}) collective-permute-start(f32[8,512]{1,0:T(8,128)S(1)} %pad_maximum_fusion.1), channel_id=1, source_target_pairs={{0,5},{1,4},{2,7},{3,6},{4,1},{5,0},{6,3},{7,2},{8,13},{9,12},{10,... | collective-permute-start | bytes 49160 | tf_op jit(solution)/shard_map/ppermute | solution.py:54
  8.3 3.5 %collective-permute-start.2 = (f32[8,512]{1,0:T(8,128)S(1)}, f32[8,512]{1,0:T(8,128)S(1)}, u32[]{:S(2)}, u32[]{:S(2)}) collective-permute-start(f32[8,512]{1,0:T(8,128)S(1)} %fusion.43), channel_id=1, source_target_pairs={{0,9},{1,8},{2,11},{3,10},{4,13},{5,12},{6,15},{7,14},{8,1},{9,0},... | collective-permute-start | bytes 49160 | tf_op jit(solution)/shard_map/ppermute | solution.py:54
  11.8 4.2 %collective-permute-start.3 = (f32[8,512]{1,0:T(8,128)S(1)}, f32[8,512]{1,0:T(8,128)S(1)}, u32[]{:S(2)}, u32[]{:S(2)}) collective-permute-start(f32[8,512]{1,0:T(8,128)S(1)} %add.482), channel_id=1, source_target_pairs={{0,17},{1,16},{2,19},{3,18},{4,21},{5,20},{6,23},{7,22},{8,25},{9,... | collective-permute-start | bytes 49160 | tf_op jit(solution)/shard_map/ppermute | solution.py:54
  15.6 1.9 %copy-start.5 = (f32[4]{0:T(128)S(1)}, f32[4]{0:T(128)}, u32[]{:S(2)}) copy-start(f32[4]{0:T(128)} %param.7) | copy-start | bytes 52
  16.0 4.1 %collective-permute-start.4 = (f32[1,8,512]{2,1,0:T(8,128)S(1)}, f32[1,8,512]{2,1,0:T(8,128)S(1)}, u32[]{:S(2)}, u32[]{:S(2)}) collective-permute-start(f32[1,8,512]{2,1,0:T(8,128)S(1)} %add_bitcast_fusion), channel_id=1, source_target_pairs={{0,3},{1,2},{2,1},{3,0},{4,7},{5,6},{6,5},{7,4},{8,11},{9,10},{10,... | collective-permute-start | bytes 49160 | tf_op jit(solution)/shard_map/ppermute | solution.py:54

commit v2 on v1

v2 whole, which is shorter than its diff:
```python
import functools
import math

import jax
import jax.numpy as jnp
from jax import lax
from jax.experimental import pallas as pl
from jax.experimental.pallas import tpu as pltpu
from jax.sharding import PartitionSpec as P

FACET = 8192
SIDE = 8
SKY = 65536
WIN = 64
TAYLOR = 4
LANE = 128

SINE = (1.5707963705062866, -0.6459637880325317, 0.07968991994857788, -0.004674150608479977, 0.0001516751217423007)
COSINE = (0.9999999403953552, -1.2336982488632202, 0.2536506950855255, -0.020810570567846298, 0.0008581625297665596)


def turns(index):
    centred = ((index + SKY // 2) & (SKY - 1)) - SKY // 2
    z = centred.astype(jnp.float32) * (2.0 / SKY)
    w = z * z
    half_sin = z * (SINE[0] + w * (SINE[1] + w * (SINE[2] + w * (SINE[3] + w * SINE[4]))))
    half_cos = COSINE[0] + w * (COSINE[1] + w * (COSINE[2] + w * (COSINE[3] + w * COSINE[4])))
    return 1.0 - 2.0 * half_sin * half_sin, 2.0 * half_sin * half_cos


def grant(*arrays):
    return (8 << 20) + 2 * sum(4 * math.prod(array.shape) for array in arrays)


def lasting(microseconds):
    return pl.CostEstimate(flops=int(microseconds * 1.15e9), bytes_accessed=0, transcendentals=0)


def split(value):
    high = value.astype(jnp.bfloat16)
    return high, (value - high.astype(jnp.float32)).astype(jnp.bfloat16)


def rotate(real, imag, cosines, sines):
    return real * cosines + imag * sines, imag * cosines - real * sines


def lookup_kernel(group, rows, offset_ref, look_ref, turn_ref):
    count = group * WIN
    step = turn_ref.shape[0] // 2 - 1
    anchor = lax.axis_index("facet") % SIDE * FACET
    lane_index = lax.broadcasted_iota(jnp.int32, (1, count), 1)
    pixel = lax.broadcasted_iota(jnp.int32, (LANE, count), 0)
    for first in range(0, offset_ref.shape[1], group):
        freq = lane_index % WIN
        for k in range(group):
            freq = freq + jnp.where(lane_index // WIN == k, offset_ref[0:1, first + k : first + k + 1], 0)
        cosines, sines = turns(pixel * freq)
        high, low = split(jnp.concatenate([cosines, -sines], axis=1))
        look_ref[0, :, 2 * first * WIN : 2 * first * WIN + 2 * count] = high
        look_ref[1, :, 2 * first * WIN : 2 * first * WIN + 2 * count] = low
        shifts = [LANE * step] + [anchor + k * LANE for k in range(step)]
        for k, shift in enumerate(shifts):
            cosines, sines = turns(freq * shift)
            turn_ref[2 * k : 2 * k + 1, first * WIN : first * WIN + count] = cosines
            turn_ref[2 * k + 1 : 2 * k + 2, first * WIN : first * WIN + count] = sines


def column_tables(offsets, rows):
    subgrids = offsets.shape[1]
    step = max(8 // rows, 1)
    shapes = [
        jax.ShapeDtypeStruct((2, LANE, 2 * subgrids * WIN), jnp.bfloat16),
        jax.ShapeDtypeStruct((2 + 2 * step, subgrids * WIN), jnp.float32),
    ]
    return pl.pallas_call(
        functools.partial(lookup_kernel, math.gcd(subgrids, 4), rows),
        in_specs=[pl.BlockSpec(memory_space=pltpu.VMEM)],
        out_specs=[pl.BlockSpec(memory_space=pltpu.VMEM)] * 2,
        out_shape=shapes,
        cost_estimate=lasting(0.3),
        compiler_params=pltpu.CompilerParams(vmem_limit_bytes=grant(*shapes)),
        name="column_tables",
    )(offsets)


def column_kernel(group, term_ref, look_ref, turn_ref, *refs):
    out_ref = refs[-1]
    rows, width = term_ref.shape[2:]
    count = group * WIN
    step = turn_ref.shape[0] // 2 - 1
    tall = step * rows
    folded = jnp.concatenate([term_ref[0, 0, :, k * LANE : (k + 1) * LANE] for k in range(width // LANE)], axis=0)
    term_high, term_low = split(folded)
    dot = functools.partial(jnp.dot, preferred_element_type=jnp.float32)
    for first in range(0, turn_ref.shape[1] // WIN, group):
        start = 2 * first * WIN
        look_high = look_ref[0, :, start : start + 2 * count]
        look_low = look_ref[1, :, start : start + 2 * count]
        part = dot(term_high, look_high) + (dot(term_low, look_high) + dot(term_high, look_low))
        turn = [turn_ref[k : k + 1, first * WIN : first * WIN + count] for k in range(turn_ref.shape[0])]
        real = jnp.zeros((tall, count), jnp.float32)
        imag = jnp.zeros((tall, count), jnp.float32)
        for k in reversed(range(width // LANE // step)):
            real, imag = rotate(real, imag, turn[0], turn[1])
            piece = part[k * tall : (k + 1) * tall]
            real, imag = real + piece[:, :count], imag + piece[:, count:]
        total_real = total_imag = 0.0
        for k in range(step):
            mine = slice(k * rows, (k + 1) * rows)
            piece = rotate(real[mine], imag[mine], turn[2 + 2 * k], turn[3 + 2 * k])
            total_real, total_imag = total_real + piece[0], total_imag + piece[1]
        out_ref[:, start : start + count] = total_real
        out_ref[:, start + count : start + 2 * count] = total_imag


def column_transform(taylor, tables, *early):
    rows, width = taylor.shape[2:]
    columns = tables[0].shape[2]
    return pl.pallas_call(
        functools.partial(column_kernel, math.gcd(columns // (2 * WIN), 4)),
        in_specs=[pl.BlockSpec(memory_space=pltpu.VMEM)] * (3 + len(early)),
        out_specs=pl.BlockSpec(memory_space=pltpu.VMEM),
        out_shape=jax.ShapeDtypeStruct((rows, columns), jnp.float32),
        cost_estimate=lasting(0.45),
        compiler_params=pltpu.CompilerParams(vmem_limit_bytes=grant(taylor, *tables, *early)),
        name="column_transform",
    )(taylor, *tables, *early)


def exchange(value, facets, chans, flip_facet, flip_chan):
    pairs = [
        (f * chans + c, (f ^ flip_facet) * chans + (c ^ flip_chan)) for f in range(facets) for c in range(chans)
    ]
    return lax.ppermute(value, ("facet", "chan"), pairs)


def gather_terms(both, facets, chans):
    near = SIDE if facets > SIDE else facets
    step = 1
    while step < near:
        both = both + exchange(both, facets, chans, step, 1)
        step *= 2
    pieces = [both]
    step = 2
    while step < chans:
        pieces = pieces + [exchange(piece, facets, chans, 0, step + 1) for piece in pieces]
        step *= 2
    if facets == near:
        return [piece[None] for piece in pieces]
    groups = [[h * near + f for h in range(facets // near)] for f in range(near)]
    return [lax.all_gather(piece, "facet", axis=0, axis_index_groups=groups) for piece in pieces]


def weight_kernel(rows, offset_hbm, owner_hbm, tile_hbm, coord_hbm, row_ref, mask_ref, mix_ref, *scratch):
    hbm = (offset_hbm, owner_hbm, tile_hbm, coord_hbm)
    offset_ref, owner_ref, tile_ref, coord_ref, sems = scratch
    copies = [pltpu.make_async_copy(a, b, sems.at[k]) for k, (a, b) in enumerate(zip(hbm, scratch[:4]))]
    for copy in copies:
        copy.start()
    facets = lax.axis_size("facet")
    band, chan = lax.axis_index("facet"), lax.axis_index("chan")

    for copy in copies:
        copy.wait()

    blocks = tile_ref.shape[0]
    sublane = lax.broadcasted_iota(jnp.int32, (blocks, LANE), 0)
    lane = lax.broadcasted_iota(jnp.int32, (blocks, LANE), 1)
    tile = jnp.zeros((blocks, LANE), jnp.int32)
    for b in range(blocks):
        tile = jnp.where(sublane == b, tile_ref[b], tile)
    slot = jnp.where(tile < 0, -1, tile // WIN)
    first_row = jnp.zeros((blocks, LANE), jnp.int32)
    seen = jnp.int32(0)
    for pair in range(0, owner_ref.shape[0], LANE // WIN):
        mask = jnp.zeros((blocks, LANE), jnp.float32)
        for k in range(LANE // WIN):
            owned = owner_ref[pair + k] == band
            chosen = slot == jnp.where(owned, seen, -2)
            seen = seen + jnp.where(owned, 1, 0)
            first_row = jnp.where(chosen, offset_ref[1, pair + k], first_row)
            mask = jnp.where(chosen & (lane // WIN == k), 1.0, mask)
        mask_ref[:, pair * WIN : pair * WIN + LANE] = mask

    scale = float((FACET * rows * facets) ** -0.5)
    v = lane % WIN
    up = jnp.maximum(tile, 0) % WIN * v * (SKY // WIN)
    near = SIDE if facets > SIDE else facets
    for h in range(facets // near):
        for r in range(rows):
            position = h % SIDE * FACET + h // SIDE * rows + r
            cosines, sines = turns(up - (first_row + v) * position)
            for part, value in enumerate((cosines, sines)):
                total = jnp.sum(jnp.where(lane < WIN, value, 0.0), axis=1, keepdims=True) * scale
                row_ref[part, h * rows + r] = jnp.broadcast_to(total, (blocks, LANE))

    coord = coord_ref[chan]
    tall = lax.broadcasted_iota(jnp.int32, (2 * rows, LANE), 0)
    for k in range(mix_ref.shape[0]):
        term = 2 * ((chan // 2) ^ k) + tall // rows
        power = jnp.ones((2 * rows, LANE), jnp.float32)
        for degree in range(1, TAYLOR):
            power = jnp.where(term >= degree, power * coord, power)
        mix_ref[k] = power


def finish_weights(offsets, owner, tiles, coord, facets, chans, rows):
    subgrids = owner.shape[0]
    blocks = tiles.shape[0]
    near = SIDE if facets > SIDE else facets
    shapes = [
        jax.ShapeDtypeStruct((2, facets // near * rows, blocks, LANE), jnp.float32),
        jax.ShapeDtypeStruct((blocks, subgrids * WIN), jnp.float32),
        jax.ShapeDtypeStruct((chans // 2, 2 * rows, LANE), jnp.float32),
    ]
    return pl.pallas_call(
        functools.partial(weight_kernel, rows),
        in_specs=[pl.BlockSpec(memory_space=pl.ANY)] * 4,
        out_specs=[pl.BlockSpec(memory_space=pltpu.VMEM)] * 3,
        out_shape=shapes,
        scratch_shapes=[
            pltpu.SMEM(offsets.shape, jnp.int32),
            pltpu.SMEM(owner.shape, jnp.int32),
            pltpu.SMEM(tiles.shape, jnp.int32),
            pltpu.SMEM(coord.shape, jnp.float32),
            pltpu.SemaphoreType.DMA((4,)),
        ],
        cost_estimate=lasting(0.75),
        compiler_params=pltpu.CompilerParams(vmem_limit_bytes=grant(*shapes)),
        name="finish_weights",
    )(offsets, owner, tiles, coord)


def finish_kernel(pieces, *refs):
    piece_refs = refs[:pieces]
    row_ref, mask_ref, mix_ref, block_ref, out_ref = refs[pieces:]
    groups, tall, width = piece_refs[0].shape
    rows = tall // 2
    subgrids = mask_ref.shape[1] // WIN
    group = math.gcd(subgrids, 4)
    count = group * WIN
    blocks = mask_ref.shape[0]
    real_row = imag_row = 0.0
    for first in range(0, subgrids, group):
        start = 2 * first * WIN
        real_t = imag_t = 0.0
        for h in range(groups):
            mixed = 0.0
            for k in range(pieces):
                weight = jnp.tile(mix_ref[k], (1, 2 * count // LANE))
                mixed = mixed + piece_refs[k][h, :, start : start + 2 * count] * weight
            mixed = mixed[:rows] + mixed[rows:]
            for r in range(rows):
                real_a = jnp.tile(row_ref[0, h * rows + r], (1, count // LANE))
                imag_a = jnp.tile(row_ref[1, h * rows + r], (1, count // LANE))
                real_y, imag_y = mixed[r : r + 1, :count], mixed[r : r + 1, count:]
                real_t = real_t + (real_a * real_y - imag_a * imag_y)
                imag_t = imag_t + (real_a * imag_y + imag_a * real_y)
        mask = mask_ref[:, first * WIN : first * WIN + count]
        for k in range(0, count, LANE):
            real_row = real_row + (real_t * mask)[:, k : k + LANE]
            imag_row = imag_row + (imag_t * mask)[:, k : k + LANE]
    row = jnp.concatenate(
        [sum(value[:, k : k + WIN] for k in range(0, LANE, WIN)) for value in (real_row, imag_row)], axis=1
    ).T
    vis = block_ref.shape[2]
    for b in range(blocks):
        real_c, imag_c = row[:WIN, b : b + 1], row[WIN:, b : b + 1]
        real_f, imag_f = block_ref[b, :WIN], block_ref[b, WIN:]
        out_ref[b, :, :vis] = jnp.sum(real_c * real_f - imag_c * imag_f, axis=0, keepdims=True)
        out_ref[b, :, vis:] = jnp.sum(real_c * imag_f + imag_c * real_f, axis=0, keepdims=True)


def finish(pieces, weights, transformed):
    blocks, _, vis = transformed.shape
    return pl.pallas_call(
        functools.partial(finish_kernel, len(pieces)),
        in_specs=[pl.BlockSpec(memory_space=pltpu.VMEM)] * (len(pieces) + 4),
        out_specs=pl.BlockSpec(memory_space=pltpu.VMEM),
        out_shape=jax.ShapeDtypeStruct((blocks, 1, 2 * vis), jnp.float32),
        cost_estimate=lasting(1.3),
        compiler_params=pltpu.CompilerParams(vmem_limit_bytes=grant(*pieces, *weights, transformed)),
        name="finish",
    )(*pieces, *weights, transformed)


def block_kernel(fourier_ref, out_ref):
    vis = out_ref.shape[2]
    here = lax.broadcasted_iota(jnp.int32, (2 * WIN, 2 * WIN), 0)
    there = lax.broadcasted_iota(jnp.int32, (2 * WIN, 2 * WIN), 1)
    cosines, sines = turns((here % WIN) * (there % WIN) * (SKY // WIN))
    sines = jnp.where(here < WIN, -sines, sines)
    table_high, table_low = split(jnp.where((here < WIN) == (there < WIN), cosines, sines) * (1.0 / WIN))
    dot = functools.partial(jnp.dot, preferred_element_type=jnp.float32)
    for b in range(0, out_ref.shape[0], 2):
        pair = [
            jnp.concatenate([fourier_ref[k, 0, :, :vis], fourier_ref[k, 0, :, vis:]], axis=0) for k in (b, b + 1)
        ]
        high, low = split(jnp.concatenate(pair, axis=1))
        done = dot(table_high, high) + (dot(table_low, high) + dot(table_high, low))
        out_ref[b] = done[:, :vis]
        out_ref[b + 1] = done[:, vis:]


def transform_blocks(fourier):
    blocks, _, _, width = fourier.shape
    vis = width // 2
    return pl.pallas_call(
        block_kernel,
        in_specs=[pl.BlockSpec(memory_space=pltpu.VMEM)],
        out_specs=pl.BlockSpec(memory_space=pltpu.VMEM),
        out_shape=jax.ShapeDtypeStruct((blocks, 2 * WIN, vis), jnp.float32),
        cost_estimate=lasting(0.65),
        compiler_params=pltpu.CompilerParams(vmem_limit_bytes=grant(fourier)),
        name="transform_blocks",
    )(fourier)


def local(taylor, chan_coord, sub_offset, sub_owner, tile_list, fourier):
    facets, chans = lax.axis_size("facet"), lax.axis_size("chan")
    chan = lax.axis_index("chan")
    offsets = sub_offset.T
    tables = column_tables(offsets, taylor.shape[2])
    beside = exchange(taylor, facets, chans, 0, 1)
    own, other = column_transform(taylor, tables), column_transform(beside, tables, fourier)
    odd = chan % 2 == 1
    both = jnp.concatenate([jnp.where(odd, other, own), jnp.where(odd, own, other)], axis=0)
    transformed = transform_blocks(fourier)
    weights = finish_weights(offsets, sub_owner, tile_list, chan_coord, facets, chans, taylor.shape[2])
    pieces = gather_terms(both, facets, chans)
    return finish(pieces, weights, transformed)


def solution(mesh):
    return jax.shard_map(
        local,
        mesh=mesh,
        in_specs=(
            P("facet", "chan", None, None),
            P(),
            P(),
            P(),
            P("facet"),
            P("facet", "chan", None, None),
        ),
        out_specs=P("facet", "chan", None),
        check_vma=False,
    )
```

time: 22.5 us -> 19.5 us (0.87)
  Pallas kernels: 0 us -> 3.94 us
  other arithmetic: 2.85 us -> 0.04 us
  matrix products: 2.11 us -> 0 us
  between operations: 2.19 us -> 0.09 us
  waiting for transfers between devices: 3.12 us -> 4.54 us
  local copies, waits for them, and re-layouts: 2.57 us -> 1.46 us
    pallas_call x0 -> x6, Pallas kernels: none -> 3.94 us  [the longest x1 1.35 us: finish(): pl.pallas_call(functools.partial(finish_kernel, len(pieces)), in_specs=[p...]
    dot_general x4 -> x0, matrix products: 2.11 us -> none  [the longest x1 1.11 us: transform_blocks(): out = jnp.einsum('uw,bwz->buz', table, stacked, precision=precise)]
    reduce_sum x6 -> x0, other arithmetic: 1.54 us -> none  [the longest x1 0.6 us: local(): jnp.sum(jnp.where(jnp.arange(chan_coord.shape[0]) == chan, chan_coord, 0.0))]
    ppermute x5, waiting for transfers between devices: 3.12 us -> 4.54 us  [exchange(): return lax.ppermute(value, ('facet', 'chan'), pairs)]
    add x4 -> x0, other arithmetic: 0.8 us -> none  [the longest x1 0.66 us: local(): mixed = sum((powers[t] * terms[:, t] for t in range(TAYLOR)))]
    broadcast_in_dim x2 -> x0, local copies, waits for them, and re-layouts: 0.62 us -> none  [the longest x1 0.62 us: local(): return jnp.concatenate([real_v, imag_v], axis=-1)[:, None, :]]
    sub x2 -> x0, other arithmetic: 0.27 us -> none  [turns(): return (1.0 - 2.0 * half_sin * half_sin, 2.0 * half_sin * half_cos)]
  transfers between devices with their start and end apart: 5 -> 5, of which waited for: 3 -> 4; matrix products, arithmetic and copies ran while one was open for 11% -> 0% of each run, Pallas kernels for 0% -> 11%
where the time goes in v2:
time: 19.5 us; the launch traced here: 19.3 us
  starting transfers between devices  9.27 us (48%)
  waiting for transfers between devices  4.54 us (23%)
  Pallas kernels  3.94 us (20%)
  local copies, waits for them, and re-layouts  1.46 us (7%)
    ppermute x5, starting transfers between devices, exchange(): return lax.ppermute(value, ('facet', 'chan'), pairs)  9.27 us
    ppermute x5, waiting for transfers between devices, exchange(): return lax.ppermute(value, ('facet', 'chan'), pairs)  4.54 us
    unnamed x12, local copies, waits for them, and re-layouts  1.46 us
    pallas_call x1, Pallas kernels, finish(): pl.pallas_call(functools.partial(finish_kernel, len(pieces)), in_specs=[p...  1.35 us
    pallas_call x2, Pallas kernels, column_transform(): pl.pallas_call(functools.partial(column_kernel, math.gcd(columns // (2 *...  0.9 us
    pallas_call x1, Pallas kernels, finish_weights(): pl.pallas_call(functools.partial(weight_kernel, rows), in_specs=[pl.Block...  0.75 us
    pallas_call x1, Pallas kernels, transform_blocks(): pl.pallas_call(block_kernel, in_specs=[pl.BlockSpec(memory_space=pltpu.VM...  0.64 us
  transfers between devices with their start and end apart: 5, of which 4 were waited for; matrix products, arithmetic and copies ran while one was open for 0% of the time, Pallas kernels for 11%

profile of v2, /device:TPU:0, one launch (start us, length us, event | category | flops | bytes accessed | tf_op | source)
XLA Modules:
  0.0 19.3 jit_solution(15554137872234601642)
XLA Ops:
  0.0 0.5 %collective-permute-start = (f32[1,1,4,8192]{3,2,1,0:T(4,128)}, f32[1,1,4,8192]{3,2,1,0:T(4,128)S(1)}, u32[]{:S(2)}, u32[]{:S(2)}) collective-permute-start(f32[1,1,4,8192]{3,2,1,0:T(4,128)} %term_ref.1), channel_id=1, source_target_pairs={{0,1},{1,0},{2,3},{3,2},{4,5},{5,4},{6,7},{7,6},{8,9},{9,8},{10,11... | collective-permute-start | bytes 393224 | tf_op jit(solution)/shard_map/ppermute | solution.py:135
  0.5 0.7 %copy-done.2 = s32[4,2]{0,1:T(2,128)S(1)} copy-done((s32[4,2]{0,1:T(2,128)S(1)}, s32[4,2]{0,1:T(2,128)}, u32[]{:S(2)}) %copy-start.2) | copy-done | bytes 56
  1.1 0.3 %column_tables.1 = (bf16[2,128,512]{2,1,0:T(8,128)(2,1)S(1)}, f32[6,256]{1,0:T(8,128)S(1)}) custom-call(s32[2,4]{1,0:T(2,128)S(1)} %bitcast.5), custom_call_target="tpu_custom_call" | custom-call | flops 345000000 | tf_op jit(solution)/shard_map/column_tables/pallas_call | solution.py:76
  1.4 0.0 copy-start
  1.4 0.6 %copy-done.1 = f32[1,1,4,8192]{3,2,1,0:T(4,128)S(1)} copy-done((f32[1,1,4,8192]{3,2,1,0:T(4,128)S(1)}, f32[1,1,4,8192]{3,2,1,0:T(4,128)}, u32[]{:S(2)}) %copy-start.1) | copy-done | bytes 131096
  2.0 0.4 %column_transform.3 = f32[4,512]{1,0:T(4,128)S(1)} custom-call(f32[1,1,4,8192]{3,2,1,0:T(4,128)S(1)} %copy-done.1, bf16[2,128,512]{2,1,0:T(8,128)(2,1)S(1)} %get-tuple-element.10.look_ref, f32[6,256]{1,0:T(8,128)S(1)} %get-tuple-element.11.turn_ref), custom_call_target="tpu_custom_call" | custom-call | flops 517500000 | tf_op jit(solution)/shard_map/column_transform/pallas_call | solution.py:120
  2.5 0.0 collective-permute-done.term_ref
  2.5 0.2 copy-done
  2.7 0.4 %column_transform.2 = f32[4,512]{1,0:T(4,128)S(1)} custom-call(f32[1,1,4,8192]{3,2,1,0:T(4,128)S(1)} %collective-permute-done.term_ref, bf16[2,128,512]{2,1,0:T(8,128)(2,1)S(1)} %get-tuple-element.10.look_ref, f32[6,256]{1,0:T(8,128)S(1)} %get-tuple-element.11.turn_ref, f32[16,1,64,256]{3,2,1,0:T(8,128)S(1)} %copy-done), custom_call_target="tpu_custom_call" | custom-call | flops 517500000 | tf_op jit(solution)/shard_map/column_transform/pallas_call | solution.py:120
  3.2 2.7 %collective-permute-start.1 = (f32[8,512]{1,0:T(8,128)S(1)}, f32[8,512]{1,0:T(8,128)S(1)}, u32[]{:S(2)}, u32[]{:S(2)}) collective-permute-start(f32[8,512]{1,0:T(8,128)S(1)} %pad_maximum_fusion), channel_id=1, source_target_pairs={{0,5},{1,4},{2,7},{3,6},{4,1},{5,0},{6,3},{7,2},{8,13},{9,12},{10,... | collective-permute-start | bytes 49160 | tf_op jit(solution)/shard_map/ppermute | solution.py:135
  5.9 1.4 %collective-permute-done.1 = f32[8,512]{1,0:T(8,128)S(1)} collective-permute-done((f32[8,512]{1,0:T(8,128)S(1)}, f32[8,512]{1,0:T(8,128)S(1)}, u32[]{:S(2)}, u32[]{:S(2)}) %collective-permute-start.1) | collective-permute-done | bytes 16416 | tf_op jit(solution)/shard_map/ppermute | solution.py:135
  7.3 0.0 copy-start.4
  7.3 0.0 copy-start.5
  7.3 1.8 %collective-permute-start.2 = (f32[8,512]{1,0:T(8,128)S(1)}, f32[8,512]{1,0:T(8,128)S(1)}, u32[]{:S(2)}, u32[]{:S(2)}) collective-permute-start(f32[8,512]{1,0:T(8,128)S(1)} %fusion), channel_id=1, source_target_pairs={{0,9},{1,8},{2,11},{3,10},{4,13},{5,12},{6,15},{7,14},{8,1},{9,0},... | collective-permute-start | bytes 49160 | tf_op jit(solution)/shard_map/ppermute | solution.py:135
  9.2 1.4 %collective-permute-done.2 = f32[8,512]{1,0:T(8,128)S(1)} collective-permute-done((f32[8,512]{1,0:T(8,128)S(1)}, f32[8,512]{1,0:T(8,128)S(1)}, u32[]{:S(2)}, u32[]{:S(2)}) %collective-permute-start.2) | collective-permute-done | bytes 16416 | tf_op jit(solution)/shard_map/ppermute | solution.py:135
  10.6 2.7 %collective-permute-start.3 = (f32[8,512]{1,0:T(8,128)S(1)}, f32[8,512]{1,0:T(8,128)S(1)}, u32[]{:S(2)}, u32[]{:S(2)}) collective-permute-start(f32[8,512]{1,0:T(8,128)S(1)} %add.15), channel_id=1, source_target_pairs={{0,17},{1,16},{2,19},{3,18},{4,21},{5,20},{6,23},{7,22},{8,25},{9,... | collective-permute-start | bytes 49160 | tf_op jit(solution)/shard_map/ppermute | solution.py:135
  13.4 0.0 copy-done.3
  13.4 0.0 copy-done.4
  13.4 0.8 %finish_weights.1 = (f32[2,4,16,128]{3,2,1,0:T(8,128)S(1)}, f32[16,256]{1,0:T(8,128)S(1)}, f32[2,8,128]{2,1,0:T(8,128)S(1)}) custom-call(s32[2,4]{1,0:T(2,128)S(1)} %bitcast.6, s32[4]{0:T(128)S(1)} %copy-done.3, s32[16]{0:T(128)S(1)} %copy-done.4, f32[4]{0:T(128)S(1)} %copy-done.5), custom_call_target="tpu_custom_call" | custom-call | flops 862499968 | tf_op jit(solution)/shard_map/finish_weights/pallas_call | solution.py:217
  14.1 0.7 %collective-permute-done.3 = f32[8,512]{1,0:T(8,128)S(1)} collective-permute-done((f32[8,512]{1,0:T(8,128)S(1)}, f32[8,512]{1,0:T(8,128)S(1)}, u32[]{:S(2)}, u32[]{:S(2)}) %collective-permute-start.3) | collective-permute-done | bytes 16416 | tf_op jit(solution)/shard_map/ppermute | solution.py:135
  14.8 1.5 %collective-permute-start.4 = (f32[8,512]{1,0:T(8,128)S(1)}, f32[8,512]{1,0:T(8,128)S(1)}, u32[]{:S(2)}, u32[]{:S(2)}) collective-permute-start(f32[8,512]{1,0:T(8,128)S(1)} %add.16), channel_id=1, source_target_pairs={{0,3},{1,2},{2,1},{3,0},{4,7},{5,6},{6,5},{7,4},{8,11},{9,10},{10,... | collective-permute-start | bytes 49160 | tf_op jit(solution)/shard_map/ppermute | solution.py:135
  16.4 0.6 %transform_blocks.1.refs_5_ = f32[16,128,128]{2,1,0:T(8,128)S(1)} custom-call(f32[16,1,64,256]{3,2,1,0:T(8,128)S(1)} %copy-done), custom_call_target="tpu_custom_call" | custom-call | flops 747500032 | tf_op jit(solution)/shard_map/transform_blocks/pallas_call | solution.py:309
  17.0 1.0 %collective-permute-done.4 = f32[8,512]{1,0:T(8,128)S(1)} collective-permute-done((f32[8,512]{1,0:T(8,128)S(1)}, f32[8,512]{1,0:T(8,128)S(1)}, u32[]{:S(2)}, u32[]{:S(2)}) %collective-permute-start.4) | collective-permute-done | bytes 16416 | tf_op jit(solution)/shard_map/ppermute | solution.py:135
  18.0 1.4 %finish.1 = f32[16,1,256]{2,1,0:T(1,128)} custom-call(f32[1,8,512]{2,1,0:T(8,128)S(1)} %bitcast.3, f32[1,8,512]{2,1,0:T(8,128)S(1)} %bitcast.4, f32[2,4,16,128]{3,2,1,0:T(8,128)S(1)} %get-tuple-element.12.refs_2_, f32[16,256]{1,0:T(8,128)S(1)} %get-tuple-element.13.refs_3_, f32[2,8,128]{2,1,0:T(8,128)S(1)} %get-tuple-element.14.refs_4_, ...), custom_call_target="tpu_custom_call" | custom-call | flops 1495000064 | tf_op jit(solution)/shard_map/finish/pallas_call | solution.py:277
  (9 shorter events, 0.0 us)
Async XLA Ops:
  0.0 2.5 %collective-permute-start = (f32[1,1,4,8192]{3,2,1,0:T(4,128)}, f32[1,1,4,8192]{3,2,1,0:T(4,128)S(1)}, u32[]{:S(2)}, u32[]{:S(2)}) collective-permute-start(f32[1,1,4,8192]{3,2,1,0:T(4,128)} %term_ref.1), channel_id=1, source_target_pairs={{0,1},{1,0},{2,3},{3,2},{4,5},{5,4},{6,7},{7,6},{8,9},{9,8},{10,11... | collective-permute-start | bytes 393224 | tf_op jit(solution)/shard_map/ppermute | solution.py:135
  0.5 0.7 %copy-start.2 = (s32[4,2]{0,1:T(2,128)S(1)}, s32[4,2]{0,1:T(2,128)}, u32[]{:S(2)}) copy-start(s32[4,2]{0,1:T(2,128)} %param.8) | copy-start | bytes 100
  1.1 0.9 %copy-start.1 = (f32[1,1,4,8192]{3,2,1,0:T(4,128)S(1)}, f32[1,1,4,8192]{3,2,1,0:T(4,128)}, u32[]{:S(2)}) copy-start(f32[1,1,4,8192]{3,2,1,0:T(4,128)} %term_ref.1) | copy-start | bytes 393220
  1.4 1.2 %copy-start = (f32[16,1,64,256]{3,2,1,0:T(8,128)S(1)}, f32[16,1,64,256]{3,2,1,0:T(8,128)}, u32[]{:S(2)}) copy-start(f32[16,1,64,256]{3,2,1,0:T(8,128)} %fourier_ref.1) | copy-start | bytes 3145732
  3.2 4.1 %collective-permute-start.1 = (f32[8,512]{1,0:T(8,128)S(1)}, f32[8,512]{1,0:T(8,128)S(1)}, u32[]{:S(2)}, u32[]{:S(2)}) collective-permute-start(f32[8,512]{1,0:T(8,128)S(1)} %pad_maximum_fusion), channel_id=1, source_target_pairs={{0,5},{1,4},{2,7},{3,6},{4,1},{5,0},{6,3},{7,2},{8,13},{9,12},{10,... | collective-permute-start | bytes 49160 | tf_op jit(solution)/shard_map/ppermute | solution.py:135
  7.3 6.1 %copy-start.3 = (s32[4]{0:T(128)S(1)}, s32[4]{0:T(128)}, u32[]{:S(2)}) copy-start(s32[4]{0:T(128)} %owner_hbm.1) | copy-start | bytes 52
  7.3 6.1 %copy-start.4 = (s32[16]{0:T(128)S(1)}, s32[16]{0:T(128)}, u32[]{:S(2)}) copy-start(s32[16]{0:T(128)} %tile_hbm.1) | copy-start | bytes 196
  7.3 6.0 %copy-start.5 = (f32[4]{0:T(128)S(1)}, f32[4]{0:T(128)}, u32[]{:S(2)}) copy-start(f32[4]{0:T(128)} %coord_hbm.1) | copy-start | bytes 52
  7.3 3.3 %collective-permute-start.2 = (f32[8,512]{1,0:T(8,128)S(1)}, f32[8,512]{1,0:T(8,128)S(1)}, u32[]{:S(2)}, u32[]{:S(2)}) collective-permute-start(f32[8,512]{1,0:T(8,128)S(1)} %fusion), channel_id=1, source_target_pairs={{0,9},{1,8},{2,11},{3,10},{4,13},{5,12},{6,15},{7,14},{8,1},{9,0},... | collective-permute-start | bytes 49160 | tf_op jit(solution)/shard_map/ppermute | solution.py:135
  10.6 4.2 %collective-permute-start.3 = (f32[8,512]{1,0:T(8,128)S(1)}, f32[8,512]{1,0:T(8,128)S(1)}, u32[]{:S(2)}, u32[]{:S(2)}) collective-permute-start(f32[8,512]{1,0:T(8,128)S(1)} %add.15), channel_id=1, source_target_pairs={{0,17},{1,16},{2,19},{3,18},{4,21},{5,20},{6,23},{7,22},{8,25},{9,... | collective-permute-start | bytes 49160 | tf_op jit(solution)/shard_map/ppermute | solution.py:135
  14.8 3.2 %collective-permute-start.4 = (f32[8,512]{1,0:T(8,128)S(1)}, f32[8,512]{1,0:T(8,128)S(1)}, u32[]{:S(2)}, u32[]{:S(2)}) collective-permute-start(f32[8,512]{1,0:T(8,128)S(1)} %add.16), channel_id=1, source_target_pairs={{0,3},{1,2},{2,1},{3,0},{4,7},{5,6},{6,5},{7,4},{8,11},{9,10},{10,... | collective-permute-start | bytes 49160 | tf_op jit(solution)/shard_map/ppermute | solution.py:135

commit v3 on v2

--- a/solution.py
+++ b/solution.py
@@ -14,6 +14,7 @@
 WIN = 64
 TAYLOR = 4
 LANE = 128
+BLOCK = 256
 
 SINE = (1.5707963705062866, -0.6459637880325317, 0.07968991994857788, -0.004674150608479977, 0.0001516751217423007)
 COSINE = (0.9999999403953552, -1.2336982488632202, 0.2536506950855255, -0.020810570567846298, 0.0008581625297665596)
@@ -45,52 +46,36 @@
     return real * cosines + imag * sines, imag * cosines - real * sines
 
 
-def lookup_kernel(group, rows, offset_ref, look_ref, turn_ref):
+def write_tables(group, anchor, offset_ref, look_ref, turn_ref):
     count = group * WIN
     step = turn_ref.shape[0] // 2 - 1
-    anchor = lax.axis_index("facet") % SIDE * FACET
     lane_index = lax.broadcasted_iota(jnp.int32, (1, count), 1)
     pixel = lax.broadcasted_iota(jnp.int32, (LANE, count), 0)
     for first in range(0, offset_ref.shape[1], group):
         freq = lane_index % WIN
         for k in range(group):
-            freq = freq + jnp.where(lane_index // WIN == k, offset_ref[0:1, first + k : first + k + 1], 0)
+            freq = freq + jnp.where(lane_index // WIN == k, offset_ref[0, first + k], 0)
         cosines, sines = turns(pixel * freq)
-        high, low = split(jnp.concatenate([cosines, -sines], axis=1))
+        tables = [(cosines, -sines)]
+        for k in range(LANE, BLOCK, LANE):
+            tables.append(rotate(*tables[0], *turns(freq * k)))
+        table = jnp.concatenate([jnp.concatenate(pair, axis=1) for pair in tables], axis=0)
+        high, low = split(table)
         look_ref[0, :, 2 * first * WIN : 2 * first * WIN + 2 * count] = high
         look_ref[1, :, 2 * first * WIN : 2 * first * WIN + 2 * count] = low
-        shifts = [LANE * step] + [anchor + k * LANE for k in range(step)]
+        shifts = [BLOCK * step] + [anchor + k * BLOCK for k in range(step)]
         for k, shift in enumerate(shifts):
             cosines, sines = turns(freq * shift)
             turn_ref[2 * k : 2 * k + 1, first * WIN : first * WIN + count] = cosines
             turn_ref[2 * k + 1 : 2 * k + 2, first * WIN : first * WIN + count] = sines
 
 
-def column_tables(offsets, rows):
-    subgrids = offsets.shape[1]
-    step = max(8 // rows, 1)
-    shapes = [
-        jax.ShapeDtypeStruct((2, LANE, 2 * subgrids * WIN), jnp.bfloat16),
-        jax.ShapeDtypeStruct((2 + 2 * step, subgrids * WIN), jnp.float32),
-    ]
-    return pl.pallas_call(
-        functools.partial(lookup_kernel, math.gcd(subgrids, 4), rows),
-        in_specs=[pl.BlockSpec(memory_space=pltpu.VMEM)],
-        out_specs=[pl.BlockSpec(memory_space=pltpu.VMEM)] * 2,
-        out_shape=shapes,
-        cost_estimate=lasting(0.3),
-        compiler_params=pltpu.CompilerParams(vmem_limit_bytes=grant(*shapes)),
-        name="column_tables",
-    )(offsets)
-
-
-def column_kernel(group, term_ref, look_ref, turn_ref, *refs):
-    out_ref = refs[-1]
+def write_columns(group, term_ref, look_ref, turn_ref, out_ref):
     rows, width = term_ref.shape[2:]
     count = group * WIN
     step = turn_ref.shape[0] // 2 - 1
     tall = step * rows
-    folded = jnp.concatenate([term_ref[0, 0, :, k * LANE : (k + 1) * LANE] for k in range(width // LANE)], axis=0)
+    folded = jnp.concatenate([term_ref[0, 0, :, k * BLOCK : (k + 1) * BLOCK] for k in range(width // BLOCK)], axis=0)
     term_high, term_low = split(folded)
     dot = functools.partial(jnp.dot, preferred_element_type=jnp.float32)
     for first in range(0, turn_ref.shape[1] // WIN, group):
@@ -101,7 +86,7 @@
         turn = [turn_ref[k : k + 1, first * WIN : first * WIN + count] for k in range(turn_ref.shape[0])]
         real = jnp.zeros((tall, count), jnp.float32)
         imag = jnp.zeros((tall, count), jnp.float32)
-        for k in reversed(range(width // LANE // step)):
+        for k in reversed(range(width // BLOCK // step)):
             real, imag = rotate(real, imag, turn[0], turn[1])
             piece = part[k * tall : (k + 1) * tall]
             real, imag = real + piece[:, :count], imag + piece[:, count:]
@@ -114,18 +99,58 @@
         out_ref[:, start + count : start + 2 * count] = total_imag
 
 
-def column_transform(taylor, tables, *early):
+def own_kernel(group, offset_hbm, term_hbm, fourier_hbm, look_ref, turn_ref, out_ref, block_ref, *scratch):
+    offset_ref, term_ref, sems = scratch
+    moves = ((offset_hbm, offset_ref), (term_hbm, term_ref), (fourier_hbm, block_ref))
+    copies = [pltpu.make_async_copy(a, b, sems.at[k]) for k, (a, b) in enumerate(moves)]
+    for copy in copies:
+        copy.start()
+    anchor = lax.axis_index("facet") % SIDE * FACET
+    copies[0].wait()
+    write_tables(group, anchor, offset_ref, look_ref, turn_ref)
+    copies[1].wait()
+    write_columns(group, term_ref, look_ref, turn_ref, out_ref)
+    copies[2].wait()
+
+
+def own_columns(offsets, taylor, fourier):
+    rows = taylor.shape[2]
+    subgrids = offsets.shape[1]
+    step = max(8 // rows, 1)
+    shapes = [
+        jax.ShapeDtypeStruct((2, BLOCK, 2 * subgrids * WIN), jnp.bfloat16),
+        jax.ShapeDtypeStruct((2 + 2 * step, subgrids * WIN), jnp.float32),
+        jax.ShapeDtypeStruct((rows, 2 * subgrids * WIN), jnp.float32),
+        jax.ShapeDtypeStruct(fourier.shape, jnp.float32),
+    ]
+    return pl.pallas_call(
+        functools.partial(own_kernel, math.gcd(subgrids, 4)),
+        in_specs=[pl.BlockSpec(memory_space=pltpu.HBM)] * 3,
+        out_specs=[pl.BlockSpec(memory_space=pltpu.VMEM)] * 4,
+        out_shape=shapes,
+        scratch_shapes=[
+            pltpu.SMEM(offsets.shape, jnp.int32),
+            pltpu.VMEM(taylor.shape, jnp.float32),
+            pltpu.SemaphoreType.DMA((3,)),
+        ],
+        cost_estimate=lasting(1.4),
+        compiler_params=pltpu.CompilerParams(vmem_limit_bytes=grant(*shapes)),
+        name="own_columns",
+    )(*(pltpu.with_memory_space_constraint(array, pltpu.HBM) for array in (offsets, taylor, fourier)))
+
+
+def column_transform(taylor, tables):
     rows, width = taylor.shape[2:]
     columns = tables[0].shape[2]
     return pl.pallas_call(
-        functools.partial(column_kernel, math.gcd(columns // (2 * WIN), 4)),
-        in_specs=[pl.BlockSpec(memory_space=pltpu.VMEM)] * (3 + len(early)),
+        functools.partial(write_columns, math.gcd(columns // (2 * WIN), 4)),
+        in_specs=[pl.BlockSpec(memory_space=pltpu.VMEM)] * 3,
         out_specs=pl.BlockSpec(memory_space=pltpu.VMEM),
         out_shape=jax.ShapeDtypeStruct((rows, columns), jnp.float32),
-        cost_estimate=lasting(0.45),
-        compiler_params=pltpu.CompilerParams(vmem_limit_bytes=grant(taylor, *tables, *early)),
+        cost_estimate=lasting(0.35),
+        compiler_params=pltpu.CompilerParams(vmem_limit_bytes=grant(taylor, *tables)),
         name="column_transform",
-    )(taylor, *tables, *early)
+    )(taylor, *tables)
 
 
 def exchange(value, facets, chans, flip_facet, flip_chan):
@@ -321,12 +346,12 @@
     facets, chans = lax.axis_size("facet"), lax.axis_size("chan")
     chan = lax.axis_index("chan")
     offsets = sub_offset.T
-    tables = column_tables(offsets, taylor.shape[2])
     beside = exchange(taylor, facets, chans, 0, 1)
-    own, other = column_transform(taylor, tables), column_transform(beside, tables, fourier)
+    *tables, own, blocks = own_columns(offsets, taylor, fourier)
+    other = column_transform(beside, tables)
     odd = chan % 2 == 1
     both = jnp.concatenate([jnp.where(odd, other, own), jnp.where(odd, own, other)], axis=0)
-    transformed = transform_blocks(fourier)
+    transformed = transform_blocks(blocks)
     weights = finish_weights(offsets, sub_owner, tile_list, chan_coord, facets, chans, taylor.shape[2])
     pieces = gather_terms(both, facets, chans)
     return finish(pieces, weights, transformed)

time: 19.5 us -> 18.5 us (0.949)
  local copies, waits for them, and re-layouts: 1.46 us -> 0.02 us
  Pallas kernels: 3.94 us -> 4.41 us
    unnamed x12 -> x8, local copies, waits for them, and re-layouts: 1.46 us -> 0.02 us
    pallas_call x3 -> x2, Pallas kernels: 1.19 us -> 1.66 us  [the longest x1 1.33 us: own_columns(): pl.pallas_call(functools.partial(own_kernel, math.gcd(subgrids, 4)), in_s...]
  transfers between devices with their start and end apart: 5 -> 5, of which waited for: 4 -> 4; matrix products, arithmetic and copies ran while one was open for 0% -> 0% of each run, Pallas kernels for 11% -> 15%
where the time goes in v3:
time: 18.5 us; the launch traced here: 18.4 us
  starting transfers between devices  9.25 us (50%)
  waiting for transfers between devices  4.56 us (25%)
  Pallas kernels  4.41 us (24%)
    ppermute x5, starting transfers between devices, exchange(): return lax.ppermute(value, ('facet', 'chan'), pairs)  9.25 us
    ppermute x5, waiting for transfers between devices, exchange(): return lax.ppermute(value, ('facet', 'chan'), pairs)  4.56 us
    pallas_call x1, Pallas kernels, finish(): pl.pallas_call(functools.partial(finish_kernel, len(pieces)), in_specs=[p...  1.35 us
    pallas_call x1, Pallas kernels, own_columns(): pl.pallas_call(functools.partial(own_kernel, math.gcd(subgrids, 4)), in_s...  1.33 us
    pallas_call x1, Pallas kernels, finish_weights(): pl.pallas_call(functools.partial(weight_kernel, rows), in_specs=[pl.Block...  0.76 us
    pallas_call x1, Pallas kernels, transform_blocks(): pl.pallas_call(block_kernel, in_specs=[pl.BlockSpec(memory_space=pltpu.VM...  0.64 us
  transfers between devices with their start and end apart: 5, of which 4 were waited for; matrix products, arithmetic and copies ran while one was open for 0% of the time, Pallas kernels for 15%

profile of v3, /device:TPU:0, one launch (start us, length us, event | category | flops | bytes accessed | tf_op | source)
XLA Modules:
  0.0 18.4 jit_solution(6154763418102127925)
XLA Ops:
  0.0 0.5 %collective-permute-start = (f32[1,1,4,8192]{3,2,1,0:T(4,128)}, f32[1,1,4,8192]{3,2,1,0:T(4,128)S(1)}, u32[]{:S(2)}, u32[]{:S(2)}) collective-permute-start(f32[1,1,4,8192]{3,2,1,0:T(4,128)} %term_hbm.1), channel_id=1, source_target_pairs={{0,1},{1,0},{2,3},{3,2},{4,5},{5,4},{6,7},{7,6},{8,9},{9,8},{10,11... | collective-permute-start | bytes 393224 | tf_op jit(solution)/shard_map/ppermute | solution.py:160
  0.5 1.3 %own_columns.1 = (bf16[2,256,512]{2,1,0:T(8,128)(2,1)S(1)}, f32[6,256]{1,0:T(8,128)S(1)}, f32[4,512]{1,0:T(4,128)S(1)}, f32[16,1,64,256]{3,2,1,0:T(8,128)S(1)}) custom-call(s32[2,4]{1,0:T(2,128)} %bitcast.5, f32[1,1,4,8192]{3,2,1,0:T(4,128)} %term_hbm.1, f32[16,1,64,256]{3,2,1,0:T(8,128)} %fourier_hbm.1), custom_call_target="tpu_custom_call" | custom-call | flops 1610000000 | tf_op jit(solution)/shard_map/own_columns/pallas_call | solution.py:126
  1.8 0.0 collective-permute-done.term_ref
  1.8 0.3 %column_transform.1 = f32[4,512]{1,0:T(4,128)S(1)} custom-call(f32[1,1,4,8192]{3,2,1,0:T(4,128)S(1)} %collective-permute-done.term_ref, bf16[2,256,512]{2,1,0:T(8,128)(2,1)S(1)} %get-tuple-element.12.look_ref, f32[6,256]{1,0:T(8,128)S(1)} %get-tuple-element.13.turn_ref), custom_call_target="tpu_custom_call" | custom-call | flops 402500000 | tf_op jit(solution)/shard_map/column_transform/pallas_call | solution.py:145
  2.2 2.7 %collective-permute-start.1 = (f32[8,512]{1,0:T(8,128)S(1)}, f32[8,512]{1,0:T(8,128)S(1)}, u32[]{:S(2)}, u32[]{:S(2)}) collective-permute-start(f32[8,512]{1,0:T(8,128)S(1)} %pad_maximum_fusion), channel_id=1, source_target_pairs={{0,5},{1,4},{2,7},{3,6},{4,1},{5,0},{6,3},{7,2},{8,13},{9,12},{10,... | collective-permute-start | bytes 49160 | tf_op jit(solution)/shard_map/ppermute | solution.py:160
  4.9 1.4 %collective-permute-done.1 = f32[8,512]{1,0:T(8,128)S(1)} collective-permute-done((f32[8,512]{1,0:T(8,128)S(1)}, f32[8,512]{1,0:T(8,128)S(1)}, u32[]{:S(2)}, u32[]{:S(2)}) %collective-permute-start.1) | collective-permute-done | bytes 16416 | tf_op jit(solution)/shard_map/ppermute | solution.py:160
  6.3 0.0 copy-start
  6.3 0.0 copy-start.1
  6.3 0.0 copy-start.2
  6.3 0.0 copy-start.3
  6.4 1.9 %collective-permute-start.2 = (f32[8,512]{1,0:T(8,128)S(1)}, f32[8,512]{1,0:T(8,128)S(1)}, u32[]{:S(2)}, u32[]{:S(2)}) collective-permute-start(f32[8,512]{1,0:T(8,128)S(1)} %fusion), channel_id=1, source_target_pairs={{0,9},{1,8},{2,11},{3,10},{4,13},{5,12},{6,15},{7,14},{8,1},{9,0},... | collective-permute-start | bytes 49160 | tf_op jit(solution)/shard_map/ppermute | solution.py:160
  8.2 1.4 %collective-permute-done.2 = f32[8,512]{1,0:T(8,128)S(1)} collective-permute-done((f32[8,512]{1,0:T(8,128)S(1)}, f32[8,512]{1,0:T(8,128)S(1)}, u32[]{:S(2)}, u32[]{:S(2)}) %collective-permute-start.2) | collective-permute-done | bytes 16416 | tf_op jit(solution)/shard_map/ppermute | solution.py:160
  9.7 2.7 %collective-permute-start.3 = (f32[8,512]{1,0:T(8,128)S(1)}, f32[8,512]{1,0:T(8,128)S(1)}, u32[]{:S(2)}, u32[]{:S(2)}) collective-permute-start(f32[8,512]{1,0:T(8,128)S(1)} %add.15), channel_id=1, source_target_pairs={{0,17},{1,16},{2,19},{3,18},{4,21},{5,20},{6,23},{7,22},{8,25},{9,... | collective-permute-start | bytes 49160 | tf_op jit(solution)/shard_map/ppermute | solution.py:160
  12.4 0.0 copy-done
  12.4 0.0 copy-done.1
  12.4 0.0 copy-done.2
  12.4 0.0 copy-done.3
  12.4 0.8 %finish_weights.1 = (f32[2,4,16,128]{3,2,1,0:T(8,128)S(1)}, f32[16,256]{1,0:T(8,128)S(1)}, f32[2,8,128]{2,1,0:T(8,128)S(1)}) custom-call(s32[2,4]{1,0:T(2,128)S(1)} %bitcast.6, s32[4]{0:T(128)S(1)} %copy-done.1, s32[16]{0:T(128)S(1)} %copy-done.2, f32[4]{0:T(128)S(1)} %copy-done.3), custom_call_target="tpu_custom_call" | custom-call | flops 862499968 | tf_op jit(solution)/shard_map/finish_weights/pallas_call | solution.py:242
  13.2 0.7 %collective-permute-done.3 = f32[8,512]{1,0:T(8,128)S(1)} collective-permute-done((f32[8,512]{1,0:T(8,128)S(1)}, f32[8,512]{1,0:T(8,128)S(1)}, u32[]{:S(2)}, u32[]{:S(2)}) %collective-permute-start.3) | collective-permute-done | bytes 16416 | tf_op jit(solution)/shard_map/ppermute | solution.py:160
  13.8 1.5 %collective-permute-start.4 = (f32[8,512]{1,0:T(8,128)S(1)}, f32[8,512]{1,0:T(8,128)S(1)}, u32[]{:S(2)}, u32[]{:S(2)}) collective-permute-start(f32[8,512]{1,0:T(8,128)S(1)} %add.16), channel_id=1, source_target_pairs={{0,3},{1,2},{2,1},{3,0},{4,7},{5,6},{6,5},{7,4},{8,11},{9,10},{10,... | collective-permute-start | bytes 49160 | tf_op jit(solution)/shard_map/ppermute | solution.py:160
  15.4 0.6 %transform_blocks.1.refs_5_ = f32[16,128,128]{2,1,0:T(8,128)S(1)} custom-call(f32[16,1,64,256]{3,2,1,0:T(8,128)S(1)} %get-tuple-element.18.fourier_ref), custom_call_target="tpu_custom_call" | custom-call | flops 747500032 | tf_op jit(solution)/shard_map/transform_blocks/pallas_call | solution.py:334
  16.0 1.0 %collective-permute-done.4 = f32[8,512]{1,0:T(8,128)S(1)} collective-permute-done((f32[8,512]{1,0:T(8,128)S(1)}, f32[8,512]{1,0:T(8,128)S(1)}, u32[]{:S(2)}, u32[]{:S(2)}) %collective-permute-start.4) | collective-permute-done | bytes 16416 | tf_op jit(solution)/shard_map/ppermute | solution.py:160
  17.0 1.4 %finish.1 = f32[16,1,256]{2,1,0:T(1,128)} custom-call(f32[1,8,512]{2,1,0:T(8,128)S(1)} %bitcast.3, f32[1,8,512]{2,1,0:T(8,128)S(1)} %bitcast.4, f32[2,4,16,128]{3,2,1,0:T(8,128)S(1)} %get-tuple-element.15.refs_2_, f32[16,256]{1,0:T(8,128)S(1)} %get-tuple-element.16.refs_3_, f32[2,8,128]{2,1,0:T(8,128)S(1)} %get-tuple-element.17.refs_4_, ...), custom_call_target="tpu_custom_call" | custom-call | flops 1495000064 | tf_op jit(solution)/shard_map/finish/pallas_call | solution.py:302
  (5 shorter events, 0.0 us)
Async XLA Ops:
  0.0 1.8 %collective-permute-start = (f32[1,1,4,8192]{3,2,1,0:T(4,128)}, f32[1,1,4,8192]{3,2,1,0:T(4,128)S(1)}, u32[]{:S(2)}, u32[]{:S(2)}) collective-permute-start(f32[1,1,4,8192]{3,2,1,0:T(4,128)} %term_hbm.1), channel_id=1, source_target_pairs={{0,1},{1,0},{2,3},{3,2},{4,5},{5,4},{6,7},{7,6},{8,9},{9,8},{10,11... | collective-permute-start | bytes 393224 | tf_op jit(solution)/shard_map/ppermute | solution.py:160
  2.2 4.1 %collective-permute-start.1 = (f32[8,512]{1,0:T(8,128)S(1)}, f32[8,512]{1,0:T(8,128)S(1)}, u32[]{:S(2)}, u32[]{:S(2)}) collective-permute-start(f32[8,512]{1,0:T(8,128)S(1)} %pad_maximum_fusion), channel_id=1, source_target_pairs={{0,5},{1,4},{2,7},{3,6},{4,1},{5,0},{6,3},{7,2},{8,13},{9,12},{10,... | collective-permute-start | bytes 49160 | tf_op jit(solution)/shard_map/ppermute | solution.py:160
  6.3 6.1 %copy-start = (s32[4,2]{0,1:T(2,128)S(1)}, s32[4,2]{0,1:T(2,128)}, u32[]{:S(2)}) copy-start(s32[4,2]{0,1:T(2,128)} %param.8) | copy-start | bytes 100
  6.3 6.1 %copy-start.1 = (s32[4]{0:T(128)S(1)}, s32[4]{0:T(128)}, u32[]{:S(2)}) copy-start(s32[4]{0:T(128)} %owner_hbm.1) | copy-start | bytes 52
  6.3 6.1 %copy-start.2 = (s32[16]{0:T(128)S(1)}, s32[16]{0:T(128)}, u32[]{:S(2)}) copy-start(s32[16]{0:T(128)} %tile_hbm.1) | copy-start | bytes 196
  6.3 6.1 %copy-start.3 = (f32[4]{0:T(128)S(1)}, f32[4]{0:T(128)}, u32[]{:S(2)}) copy-start(f32[4]{0:T(128)} %coord_hbm.1) | copy-start | bytes 52
  6.4 3.3 %collective-permute-start.2 = (f32[8,512]{1,0:T(8,128)S(1)}, f32[8,512]{1,0:T(8,128)S(1)}, u32[]{:S(2)}, u32[]{:S(2)}) collective-permute-start(f32[8,512]{1,0:T(8,128)S(1)} %fusion), channel_id=1, source_target_pairs={{0,9},{1,8},{2,11},{3,10},{4,13},{5,12},{6,15},{7,14},{8,1},{9,0},... | collective-permute-start | bytes 49160 | tf_op jit(solution)/shard_map/ppermute | solution.py:160
  9.7 4.2 %collective-permute-start.3 = (f32[8,512]{1,0:T(8,128)S(1)}, f32[8,512]{1,0:T(8,128)S(1)}, u32[]{:S(2)}, u32[]{:S(2)}) collective-permute-start(f32[8,512]{1,0:T(8,128)S(1)} %add.15), channel_id=1, source_target_pairs={{0,17},{1,16},{2,19},{3,18},{4,21},{5,20},{6,23},{7,22},{8,25},{9,... | collective-permute-start | bytes 49160 | tf_op jit(solution)/shard_map/ppermute | solution.py:160
  13.8 3.2 %collective-permute-start.4 = (f32[8,512]{1,0:T(8,128)S(1)}, f32[8,512]{1,0:T(8,128)S(1)}, u32[]{:S(2)}, u32[]{:S(2)}) collective-permute-start(f32[8,512]{1,0:T(8,128)S(1)} %add.16), channel_id=1, source_target_pairs={{0,3},{1,2},{2,1},{3,0},{4,7},{5,6},{6,5},{7,4},{8,11},{9,10},{10,... | collective-permute-start | bytes 49160 | tf_op jit(solution)/shard_map/ppermute | solution.py:160

commit v4 on v3

--- a/solution.py
+++ b/solution.py
@@ -50,24 +50,29 @@
     count = group * WIN
     step = turn_ref.shape[0] // 2 - 1
     lane_index = lax.broadcasted_iota(jnp.int32, (1, count), 1)
-    pixel = lax.broadcasted_iota(jnp.int32, (LANE, count), 0)
+    sublane = lax.broadcasted_iota(jnp.int32, (8, count), 0)
+    shifts = [8, 16, 32, BLOCK * step] + [anchor + k * BLOCK for k in range(step)]
+    shift = sum(jnp.where(sublane == k, value, 0) for k, value in enumerate(shifts))
     for first in range(0, offset_ref.shape[1], group):
         freq = lane_index % WIN
         for k in range(group):
             freq = freq + jnp.where(lane_index // WIN == k, offset_ref[0, first + k], 0)
-        cosines, sines = turns(pixel * freq)
+        cosines, sines = turns(shift * freq)
+        hops = [(cosines[k : k + 1], sines[k : k + 1]) for k in range(len(shifts))]
+        cosines, sines = turns(sublane * freq)
         tables = [(cosines, -sines)]
-        for k in range(LANE, BLOCK, LANE):
-            tables.append(rotate(*tables[0], *turns(freq * k)))
-        table = jnp.concatenate([jnp.concatenate(pair, axis=1) for pair in tables], axis=0)
-        high, low = split(table)
-        look_ref[0, :, 2 * first * WIN : 2 * first * WIN + 2 * count] = high
-        look_ref[1, :, 2 * first * WIN : 2 * first * WIN + 2 * count] = low
-        shifts = [BLOCK * step] + [anchor + k * BLOCK for k in range(step)]
-        for k, shift in enumerate(shifts):
-            cosines, sines = turns(freq * shift)
-            turn_ref[2 * k : 2 * k + 1, first * WIN : first * WIN + count] = cosines
-            turn_ref[2 * k + 1 : 2 * k + 2, first * WIN : first * WIN + count] = sines
+        for k in range(2):
+            tables = tables + [rotate(*table, *hops[k]) for table in tables]
+        while len(tables) < BLOCK // 8:
+            tables.append(rotate(*tables[-4], *hops[2]))
+        for part in (0, 1):
+            high, low = split(jnp.concatenate([table[part] for table in tables], axis=0))
+            start = (2 * first + part * group) * WIN
+            look_ref[0, :, start : start + count] = high
+            look_ref[1, :, start : start + count] = low
+        for k, hop in enumerate(hops[3:]):
+            for part in (0, 1):
+                turn_ref[2 * k + part : 2 * k + part + 1, first * WIN : first * WIN + count] = hop[part]
 
 
 def write_columns(group, term_ref, look_ref, turn_ref, out_ref):
@@ -99,9 +104,9 @@
         out_ref[:, start + count : start + 2 * count] = total_imag
 
 
-def own_kernel(group, offset_hbm, term_hbm, fourier_hbm, look_ref, turn_ref, out_ref, block_ref, *scratch):
+def own_kernel(group, offset_hbm, term_hbm, look_ref, turn_ref, out_ref, *scratch):
     offset_ref, term_ref, sems = scratch
-    moves = ((offset_hbm, offset_ref), (term_hbm, term_ref), (fourier_hbm, block_ref))
+    moves = ((offset_hbm, offset_ref), (term_hbm, term_ref))
     copies = [pltpu.make_async_copy(a, b, sems.at[k]) for k, (a, b) in enumerate(moves)]
     for copy in copies:
         copy.start()
@@ -110,10 +115,9 @@
     write_tables(group, anchor, offset_ref, look_ref, turn_ref)
     copies[1].wait()
     write_columns(group, term_ref, look_ref, turn_ref, out_ref)
-    copies[2].wait()
-
-
-def own_columns(offsets, taylor, fourier):
+
+
+def own_columns(offsets, taylor):
     rows = taylor.shape[2]
     subgrids = offsets.shape[1]
     step = max(8 // rows, 1)
@@ -121,22 +125,21 @@
         jax.ShapeDtypeStruct((2, BLOCK, 2 * subgrids * WIN), jnp.bfloat16),
         jax.ShapeDtypeStruct((2 + 2 * step, subgrids * WIN), jnp.float32),
         jax.ShapeDtypeStruct((rows, 2 * subgrids * WIN), jnp.float32),
-        jax.ShapeDtypeStruct(fourier.shape, jnp.float32),
     ]
     return pl.pallas_call(
         functools.partial(own_kernel, math.gcd(subgrids, 4)),
-        in_specs=[pl.BlockSpec(memory_space=pltpu.HBM)] * 3,
-        out_specs=[pl.BlockSpec(memory_space=pltpu.VMEM)] * 4,
+        in_specs=[pl.BlockSpec(memory_space=pltpu.HBM)] * 2,
+        out_specs=[pl.BlockSpec(memory_space=pltpu.VMEM)] * 3,
         out_shape=shapes,
         scratch_shapes=[
             pltpu.SMEM(offsets.shape, jnp.int32),
             pltpu.VMEM(taylor.shape, jnp.float32),
-            pltpu.SemaphoreType.DMA((3,)),
+            pltpu.SemaphoreType.DMA((2,)),
         ],
         cost_estimate=lasting(1.4),
         compiler_params=pltpu.CompilerParams(vmem_limit_bytes=grant(*shapes)),
         name="own_columns",
-    )(*(pltpu.with_memory_space_constraint(array, pltpu.HBM) for array in (offsets, taylor, fourier)))
+    )(*(pltpu.with_memory_space_constraint(array, pltpu.HBM) for array in (offsets, taylor)))
 
 
 def column_transform(taylor, tables):
@@ -177,16 +180,19 @@
     return [lax.all_gather(piece, "facet", axis=0, axis_index_groups=groups) for piece in pieces]
 
 
-def weight_kernel(rows, offset_hbm, owner_hbm, tile_hbm, coord_hbm, row_ref, mask_ref, mix_ref, *scratch):
-    hbm = (offset_hbm, owner_hbm, tile_hbm, coord_hbm)
+def weight_kernel(
+    rows, offset_hbm, owner_hbm, tile_hbm, coord_hbm, fourier_hbm, row_ref, mask_ref, mix_ref, block_ref, *scratch
+):
+    hbm = (offset_hbm, owner_hbm, tile_hbm, coord_hbm, fourier_hbm)
     offset_ref, owner_ref, tile_ref, coord_ref, sems = scratch
-    copies = [pltpu.make_async_copy(a, b, sems.at[k]) for k, (a, b) in enumerate(zip(hbm, scratch[:4]))]
+    targets = (*scratch[:4], block_ref)
+    copies = [pltpu.make_async_copy(a, b, sems.at[k]) for k, (a, b) in enumerate(zip(hbm, targets))]
     for copy in copies:
         copy.start()
     facets = lax.axis_size("facet")
     band, chan = lax.axis_index("facet"), lax.axis_index("chan")
 
-    for copy in copies:
+    for copy in copies[:4]:
         copy.wait()
 
     blocks = tile_ref.shape[0]
@@ -228,9 +234,10 @@
         for degree in range(1, TAYLOR):
             power = jnp.where(term >= degree, power * coord, power)
         mix_ref[k] = power
-
-
-def finish_weights(offsets, owner, tiles, coord, facets, chans, rows):
+    copies[4].wait()
+
+
+def finish_weights(offsets, owner, tiles, coord, fourier, facets, chans, rows):
     subgrids = owner.shape[0]
     blocks = tiles.shape[0]
     near = SIDE if facets > SIDE else facets
@@ -238,23 +245,24 @@
         jax.ShapeDtypeStruct((2, facets // near * rows, blocks, LANE), jnp.float32),
         jax.ShapeDtypeStruct((blocks, subgrids * WIN), jnp.float32),
         jax.ShapeDtypeStruct((chans // 2, 2 * rows, LANE), jnp.float32),
+        jax.ShapeDtypeStruct(fourier.shape, jnp.float32),
     ]
     return pl.pallas_call(
         functools.partial(weight_kernel, rows),
-        in_specs=[pl.BlockSpec(memory_space=pl.ANY)] * 4,
-        out_specs=[pl.BlockSpec(memory_space=pltpu.VMEM)] * 3,
+        in_specs=[pl.BlockSpec(memory_space=pltpu.HBM)] * 5,
+        out_specs=[pl.BlockSpec(memory_space=pltpu.VMEM)] * 4,
         out_shape=shapes,
         scratch_shapes=[
             pltpu.SMEM(offsets.shape, jnp.int32),
             pltpu.SMEM(owner.shape, jnp.int32),
             pltpu.SMEM(tiles.shape, jnp.int32),
             pltpu.SMEM(coord.shape, jnp.float32),
-            pltpu.SemaphoreType.DMA((4,)),
+            pltpu.SemaphoreType.DMA((5,)),
         ],
-        cost_estimate=lasting(0.75),
+        cost_estimate=lasting(1.3),
         compiler_params=pltpu.CompilerParams(vmem_limit_bytes=grant(*shapes)),
         name="finish_weights",
-    )(offsets, owner, tiles, coord)
+    )(*(pltpu.with_memory_space_constraint(array, pltpu.HBM) for array in (offsets, owner, tiles, coord, fourier)))
 
 
 def finish_kernel(pieces, *refs):
@@ -288,22 +296,28 @@
             imag_row = imag_row + (imag_t * mask)[:, k : k + LANE]
     row = jnp.concatenate(
         [sum(value[:, k : k + WIN] for k in range(0, LANE, WIN)) for value in (real_row, imag_row)], axis=1
-    ).T
-    vis = block_ref.shape[2]
+    )
+    high, low = split(row)
+    both = jnp.concatenate(
+        [jnp.concatenate([high, high], axis=1), jnp.concatenate([low, jnp.zeros_like(low)], axis=1)], axis=0
+    )
+    here = lax.broadcasted_iota(jnp.int32, (blocks, block_ref.shape[2]), 0)
+    dot = functools.partial(jnp.dot, preferred_element_type=jnp.float32)
+    total = 0.0
     for b in range(blocks):
-        real_c, imag_c = row[:WIN, b : b + 1], row[WIN:, b : b + 1]
-        real_f, imag_f = block_ref[b, :WIN], block_ref[b, WIN:]
-        out_ref[b, :, :vis] = jnp.sum(real_c * real_f - imag_c * imag_f, axis=0, keepdims=True)
-        out_ref[b, :, vis:] = jnp.sum(real_c * imag_f + imag_c * real_f, axis=0, keepdims=True)
+        wide = dot(both, block_ref[b])
+        total = jnp.where(here == b, wide[:blocks] + wide[blocks:], total)
+    for b in range(blocks):
+        out_ref[b] = total[b : b + 1]
 
 
 def finish(pieces, weights, transformed):
-    blocks, _, vis = transformed.shape
+    blocks, _, width = transformed.shape
     return pl.pallas_call(
         functools.partial(finish_kernel, len(pieces)),
         in_specs=[pl.BlockSpec(memory_space=pltpu.VMEM)] * (len(pieces) + 4),
         out_specs=pl.BlockSpec(memory_space=pltpu.VMEM),
-        out_shape=jax.ShapeDtypeStruct((blocks, 1, 2 * vis), jnp.float32),
+        out_shape=jax.ShapeDtypeStruct((blocks, 1, width), jnp.float32),
         cost_estimate=lasting(1.3),
         compiler_params=pltpu.CompilerParams(vmem_limit_bytes=grant(*pieces, *weights, transformed)),
         name="finish",
@@ -311,7 +325,7 @@
 
 
 def block_kernel(fourier_ref, out_ref):
-    vis = out_ref.shape[2]
+    vis = out_ref.shape[2] // 2
     here = lax.broadcasted_iota(jnp.int32, (2 * WIN, 2 * WIN), 0)
     there = lax.broadcasted_iota(jnp.int32, (2 * WIN, 2 * WIN), 1)
     cosines, sines = turns((here % WIN) * (there % WIN) * (SKY // WIN))
@@ -324,8 +338,12 @@
         ]
         high, low = split(jnp.concatenate(pair, axis=1))
         done = dot(table_high, high) + (dot(table_low, high) + dot(table_high, low))
-        out_ref[b] = done[:, :vis]
-        out_ref[b + 1] = done[:, vis:]
+        for k in (0, 1):
+            real, imag = done[:WIN, k * vis : (k + 1) * vis], done[WIN:, k * vis : (k + 1) * vis]
+            matrix = jnp.concatenate(
+                [jnp.concatenate([real, imag], axis=1), jnp.concatenate([-imag, real], axis=1)], axis=0
+            )
+            out_ref[b + k, : 2 * WIN], out_ref[b + k, 2 * WIN :] = split(matrix)
 
 
 def transform_blocks(fourier):
@@ -335,9 +353,9 @@
         block_kernel,
         in_specs=[pl.BlockSpec(memory_space=pltpu.VMEM)],
         out_specs=pl.BlockSpec(memory_space=pltpu.VMEM),
-        out_shape=jax.ShapeDtypeStruct((blocks, 2 * WIN, vis), jnp.float32),
-        cost_estimate=lasting(0.65),
-        compiler_params=pltpu.CompilerParams(vmem_limit_bytes=grant(fourier)),
+        out_shape=jax.ShapeDtypeStruct((blocks, 4 * WIN, 2 * vis), jnp.bfloat16),
+        cost_estimate=lasting(0.7),
+        compiler_params=pltpu.CompilerParams(vmem_limit_bytes=grant(fourier, fourier, fourier)),
         name="transform_blocks",
     )(fourier)
 
@@ -347,12 +365,12 @@
     chan = lax.axis_index("chan")
     offsets = sub_offset.T
     beside = exchange(taylor, facets, chans, 0, 1)
-    *tables, own, blocks = own_columns(offsets, taylor, fourier)
+    *tables, own = own_columns(offsets, taylor)
     other = column_transform(beside, tables)
     odd = chan % 2 == 1
     both = jnp.concatenate([jnp.where(odd, other, own), jnp.where(odd, own, other)], axis=0)
+    *weights, blocks = finish_weights(offsets, sub_owner, tile_list, chan_coord, fourier, facets, chans, taylor.shape[2])
     transformed = transform_blocks(blocks)
-    weights = finish_weights(offsets, sub_owner, tile_list, chan_coord, facets, chans, taylor.shape[2])
     pieces = gather_terms(both, facets, chans)
     return finish(pieces, weights, transformed)
 

time: 18.5 us -> 18.3 us (0.989)
  waiting for transfers between devices: 4.56 us -> 4.01 us
  Pallas kernels: 4.41 us -> 4.74 us
    ppermute x5, waiting for transfers between devices: 4.56 us -> 4.01 us  [exchange(): return lax.ppermute(value, ('facet', 'chan'), pairs)]
    pallas_call x1, Pallas kernels: 0.76 us -> 1.27 us  [finish_weights(): pl.pallas_call(functools.partial(weight_kernel, rows), in_specs=[pl.Block...]
  transfers between devices with their start and end apart: 5 -> 5, of which waited for: 4 -> 4; matrix products, arithmetic and copies ran while one was open for 0% -> 0% of each run, Pallas kernels for 15% -> 18%
where the time goes in v4:
time: 18.3 us; the launch traced here: 18.1 us
  starting transfers between devices  9.24 us (50%)
  Pallas kernels  4.74 us (26%)
  waiting for transfers between devices  4.01 us (22%)
    ppermute x5, starting transfers between devices, exchange(): return lax.ppermute(value, ('facet', 'chan'), pairs)  9.24 us
    ppermute x5, waiting for transfers between devices, exchange(): return lax.ppermute(value, ('facet', 'chan'), pairs)  4.01 us
    pallas_call x1, Pallas kernels, finish_weights(): pl.pallas_call(functools.partial(weight_kernel, rows), in_specs=[pl.Block...  1.27 us
    pallas_call x1, Pallas kernels, own_columns(): pl.pallas_call(functools.partial(own_kernel, math.gcd(subgrids, 4)), in_s...  1.25 us
    pallas_call x1, Pallas kernels, finish(): pl.pallas_call(functools.partial(finish_kernel, len(pieces)), in_specs=[p...  1.2 us
    pallas_call x1, Pallas kernels, transform_blocks(): pl.pallas_call(block_kernel, in_specs=[pl.BlockSpec(memory_space=pltpu.VM...  0.68 us
  transfers between devices with their start and end apart: 5, of which 4 were waited for; matrix products, arithmetic and copies ran while one was open for 0% of the time, Pallas kernels for 18%

profile of v4, /device:TPU:0, one launch (start us, length us, event | category | flops | bytes accessed | tf_op | source)
XLA Modules:
  0.0 18.1 jit_solution(15815496928164689164)
XLA Ops:
  0.0 0.5 %collective-permute-start = (f32[1,1,4,8192]{3,2,1,0:T(4,128)}, f32[1,1,4,8192]{3,2,1,0:T(4,128)S(1)}, u32[]{:S(2)}, u32[]{:S(2)}) collective-permute-start(f32[1,1,4,8192]{3,2,1,0:T(4,128)} %term_hbm.1), channel_id=1, source_target_pairs={{0,1},{1,0},{2,3},{3,2},{4,5},{5,4},{6,7},{7,6},{8,9},{9,8},{10,11... | collective-permute-start | bytes 393224 | tf_op jit(solution)/shard_map/ppermute | solution.py:163
  0.5 1.3 %own_columns.1 = (bf16[2,256,512]{2,1,0:T(8,128)(2,1)S(1)}, f32[6,256]{1,0:T(8,128)S(1)}, f32[4,512]{1,0:T(4,128)S(1)}) custom-call(s32[2,4]{1,0:T(2,128)} %bitcast.5, f32[1,1,4,8192]{3,2,1,0:T(4,128)} %term_hbm.1), custom_call_target="tpu_custom_call" | custom-call | flops 1610000000 | tf_op jit(solution)/shard_map/own_columns/pallas_call | solution.py:129
  1.7 0.0 collective-permute-done.term_ref
  1.7 0.3 %column_transform.1 = f32[4,512]{1,0:T(4,128)S(1)} custom-call(f32[1,1,4,8192]{3,2,1,0:T(4,128)S(1)} %collective-permute-done.term_ref, bf16[2,256,512]{2,1,0:T(8,128)(2,1)S(1)} %get-tuple-element.12.look_ref, f32[6,256]{1,0:T(8,128)S(1)} %get-tuple-element.13.turn_ref), custom_call_target="tpu_custom_call" | custom-call | flops 402500000 | tf_op jit(solution)/shard_map/column_transform/pallas_call | solution.py:148
  2.1 2.7 %collective-permute-start.1 = (f32[8,512]{1,0:T(8,128)S(1)}, f32[8,512]{1,0:T(8,128)S(1)}, u32[]{:S(2)}, u32[]{:S(2)}) collective-permute-start(f32[8,512]{1,0:T(8,128)S(1)} %pad_maximum_fusion), channel_id=1, source_target_pairs={{0,5},{1,4},{2,7},{3,6},{4,1},{5,0},{6,3},{7,2},{8,13},{9,12},{10,... | collective-permute-start | bytes 49160 | tf_op jit(solution)/shard_map/ppermute | solution.py:163
  4.8 1.4 %collective-permute-done.1 = f32[8,512]{1,0:T(8,128)S(1)} collective-permute-done((f32[8,512]{1,0:T(8,128)S(1)}, f32[8,512]{1,0:T(8,128)S(1)}, u32[]{:S(2)}, u32[]{:S(2)}) %collective-permute-start.1) | collective-permute-done | bytes 16416 | tf_op jit(solution)/shard_map/ppermute | solution.py:163
  6.2 1.8 %collective-permute-start.2 = (f32[8,512]{1,0:T(8,128)S(1)}, f32[8,512]{1,0:T(8,128)S(1)}, u32[]{:S(2)}, u32[]{:S(2)}) collective-permute-start(f32[8,512]{1,0:T(8,128)S(1)} %fusion), channel_id=1, source_target_pairs={{0,9},{1,8},{2,11},{3,10},{4,13},{5,12},{6,15},{7,14},{8,1},{9,0},... | collective-permute-start | bytes 49160 | tf_op jit(solution)/shard_map/ppermute | solution.py:163
  8.1 1.4 %collective-permute-done.2 = f32[8,512]{1,0:T(8,128)S(1)} collective-permute-done((f32[8,512]{1,0:T(8,128)S(1)}, f32[8,512]{1,0:T(8,128)S(1)}, u32[]{:S(2)}, u32[]{:S(2)}) %collective-permute-start.2) | collective-permute-done | bytes 16416 | tf_op jit(solution)/shard_map/ppermute | solution.py:163
  9.5 2.7 %collective-permute-start.3 = (f32[8,512]{1,0:T(8,128)S(1)}, f32[8,512]{1,0:T(8,128)S(1)}, u32[]{:S(2)}, u32[]{:S(2)}) collective-permute-start(f32[8,512]{1,0:T(8,128)S(1)} %add.15), channel_id=1, source_target_pairs={{0,17},{1,16},{2,19},{3,18},{4,21},{5,20},{6,23},{7,22},{8,25},{9,... | collective-permute-start | bytes 49160 | tf_op jit(solution)/shard_map/ppermute | solution.py:163
  12.3 1.3 %finish_weights.1 = (f32[2,4,16,128]{3,2,1,0:T(8,128)S(1)}, f32[16,256]{1,0:T(8,128)S(1)}, f32[2,8,128]{2,1,0:T(8,128)S(1)}, f32[16,1,64,256]{3,2,1,0:T(8,128)S(1)}) custom-call(s32[2,4]{1,0:T(2,128)} %bitcast.6, s32[4]{0:T(128)} %owner_hbm.1, s32[16]{0:T(128)} %tile_hbm.1, f32[4]{0:T(128)} %coord_hbm.1, f32[16,1,64,256]{3,2,1,0:T(8,128)} %fourier_hbm.1), custom_call_target="tpu_custom_call" | custom-call | flops 1495000064 | tf_op jit(solution)/shard_map/finish_weights/pallas_call | solution.py:250
  13.5 0.2 collective-permute-done.3
  13.7 1.5 %collective-permute-start.4 = (f32[8,512]{1,0:T(8,128)S(1)}, f32[8,512]{1,0:T(8,128)S(1)}, u32[]{:S(2)}, u32[]{:S(2)}) collective-permute-start(f32[8,512]{1,0:T(8,128)S(1)} %add.16), channel_id=1, source_target_pairs={{0,3},{1,2},{2,1},{3,0},{4,7},{5,6},{6,5},{7,4},{8,11},{9,10},{10,... | collective-permute-start | bytes 49160 | tf_op jit(solution)/shard_map/ppermute | solution.py:163
  15.2 0.7 %transform_blocks.1.refs_5_ = bf16[16,256,256]{2,1,0:T(8,128)(2,1)S(1)} custom-call(f32[16,1,64,256]{3,2,1,0:T(8,128)S(1)} %get-tuple-element.18.fourier_ref), custom_call_target="tpu_custom_call" | custom-call | flops 805000000 | tf_op jit(solution)/shard_map/transform_blocks/pallas_call | solution.py:352
  15.9 1.0 %collective-permute-done.4 = f32[8,512]{1,0:T(8,128)S(1)} collective-permute-done((f32[8,512]{1,0:T(8,128)S(1)}, f32[8,512]{1,0:T(8,128)S(1)}, u32[]{:S(2)}, u32[]{:S(2)}) %collective-permute-start.4) | collective-permute-done | bytes 16416 | tf_op jit(solution)/shard_map/ppermute | solution.py:163
  16.9 1.2 %finish.1 = f32[16,1,256]{2,1,0:T(1,128)} custom-call(f32[1,8,512]{2,1,0:T(8,128)S(1)} %bitcast.3, f32[1,8,512]{2,1,0:T(8,128)S(1)} %bitcast.4, f32[2,4,16,128]{3,2,1,0:T(8,128)S(1)} %get-tuple-element.15.refs_2_, f32[16,256]{1,0:T(8,128)S(1)} %get-tuple-element.16.refs_3_, f32[2,8,128]{2,1,0:T(8,128)S(1)} %get-tuple-element.17.refs_4_, ...), custom_call_target="tpu_custom_call" | custom-call | flops 1495000064 | tf_op jit(solution)/shard_map/finish/pallas_call | solution.py:316
  (5 shorter events, 0.0 us)
Async XLA Ops:
  0.0 1.7 %collective-permute-start = (f32[1,1,4,8192]{3,2,1,0:T(4,128)}, f32[1,1,4,8192]{3,2,1,0:T(4,128)S(1)}, u32[]{:S(2)}, u32[]{:S(2)}) collective-permute-start(f32[1,1,4,8192]{3,2,1,0:T(4,128)} %term_hbm.1), channel_id=1, source_target_pairs={{0,1},{1,0},{2,3},{3,2},{4,5},{5,4},{6,7},{7,6},{8,9},{9,8},{10,11... | collective-permute-start | bytes 393224 | tf_op jit(solution)/shard_map/ppermute | solution.py:163
  2.1 4.1 %collective-permute-start.1 = (f32[8,512]{1,0:T(8,128)S(1)}, f32[8,512]{1,0:T(8,128)S(1)}, u32[]{:S(2)}, u32[]{:S(2)}) collective-permute-start(f32[8,512]{1,0:T(8,128)S(1)} %pad_maximum_fusion), channel_id=1, source_target_pairs={{0,5},{1,4},{2,7},{3,6},{4,1},{5,0},{6,3},{7,2},{8,13},{9,12},{10,... | collective-permute-start | bytes 49160 | tf_op jit(solution)/shard_map/ppermute | solution.py:163
  6.2 3.3 %collective-permute-start.2 = (f32[8,512]{1,0:T(8,128)S(1)}, f32[8,512]{1,0:T(8,128)S(1)}, u32[]{:S(2)}, u32[]{:S(2)}) collective-permute-start(f32[8,512]{1,0:T(8,128)S(1)} %fusion), channel_id=1, source_target_pairs={{0,9},{1,8},{2,11},{3,10},{4,13},{5,12},{6,15},{7,14},{8,1},{9,0},... | collective-permute-start | bytes 49160 | tf_op jit(solution)/shard_map/ppermute | solution.py:163
  9.5 4.2 %collective-permute-start.3 = (f32[8,512]{1,0:T(8,128)S(1)}, f32[8,512]{1,0:T(8,128)S(1)}, u32[]{:S(2)}, u32[]{:S(2)}) collective-permute-start(f32[8,512]{1,0:T(8,128)S(1)} %add.15), channel_id=1, source_target_pairs={{0,17},{1,16},{2,19},{3,18},{4,21},{5,20},{6,23},{7,22},{8,25},{9,... | collective-permute-start | bytes 49160 | tf_op jit(solution)/shard_map/ppermute | solution.py:163
  13.7 3.2 %collective-permute-start.4 = (f32[8,512]{1,0:T(8,128)S(1)}, f32[8,512]{1,0:T(8,128)S(1)}, u32[]{:S(2)}, u32[]{:S(2)}) collective-permute-start(f32[8,512]{1,0:T(8,128)S(1)} %add.16), channel_id=1, source_target_pairs={{0,3},{1,2},{2,1},{3,0},{4,7},{5,6},{6,5},{7,4},{8,11},{9,10},{10,... | collective-permute-start | bytes 49160 | tf_op jit(solution)/shard_map/ppermute | solution.py:163

commit v5 on v4

--- a/solution.py
+++ b/solution.py
@@ -46,40 +46,40 @@
     return real * cosines + imag * sines, imag * cosines - real * sines
 
 
-def write_tables(group, anchor, offset_ref, look_ref, turn_ref):
+def write_tables(group, step, anchor, offset_ref, look_ref, turn_ref):
     count = group * WIN
-    step = turn_ref.shape[0] // 2 - 1
     lane_index = lax.broadcasted_iota(jnp.int32, (1, count), 1)
-    sublane = lax.broadcasted_iota(jnp.int32, (8, count), 0)
-    shifts = [8, 16, 32, BLOCK * step] + [anchor + k * BLOCK for k in range(step)]
+    sublane = lax.broadcasted_iota(jnp.int32, (16, count), 0)
+    hops = turn_ref.shape[0] // 2 - step
+    shifts = [16, 32, 64] + [BLOCK * step << k for k in range(hops)] + [anchor + k * BLOCK for k in range(step)]
     shift = sum(jnp.where(sublane == k, value, 0) for k, value in enumerate(shifts))
     for first in range(0, offset_ref.shape[1], group):
         freq = lane_index % WIN
         for k in range(group):
             freq = freq + jnp.where(lane_index // WIN == k, offset_ref[0, first + k], 0)
         cosines, sines = turns(shift * freq)
-        hops = [(cosines[k : k + 1], sines[k : k + 1]) for k in range(len(shifts))]
+        turned = [(cosines[k : k + 1], sines[k : k + 1]) for k in range(len(shifts))]
         cosines, sines = turns(sublane * freq)
         tables = [(cosines, -sines)]
         for k in range(2):
-            tables = tables + [rotate(*table, *hops[k]) for table in tables]
-        while len(tables) < BLOCK // 8:
-            tables.append(rotate(*tables[-4], *hops[2]))
+            tables = tables + [rotate(*table, *turned[k]) for table in tables]
+        while len(tables) < BLOCK // 16:
+            tables.append(rotate(*tables[-4], *turned[2]))
         for part in (0, 1):
             high, low = split(jnp.concatenate([table[part] for table in tables], axis=0))
             start = (2 * first + part * group) * WIN
             look_ref[0, :, start : start + count] = high
             look_ref[1, :, start : start + count] = low
-        for k, hop in enumerate(hops[3:]):
+        for k, hop in enumerate(turned[3:]):
             for part in (0, 1):
                 turn_ref[2 * k + part : 2 * k + part + 1, first * WIN : first * WIN + count] = hop[part]
 
 
-def write_columns(group, term_ref, look_ref, turn_ref, out_ref):
+def columns(group, step, term_ref, look_ref, turn_ref):
     rows, width = term_ref.shape[2:]
     count = group * WIN
-    step = turn_ref.shape[0] // 2 - 1
     tall = step * rows
+    hops = turn_ref.shape[0] // 2 - step
     folded = jnp.concatenate([term_ref[0, 0, :, k * BLOCK : (k + 1) * BLOCK] for k in range(width // BLOCK)], axis=0)
     term_high, term_low = split(folded)
     dot = functools.partial(jnp.dot, preferred_element_type=jnp.float32)
@@ -89,22 +89,25 @@
         look_low = look_ref[1, :, start : start + 2 * count]
         part = dot(term_high, look_high) + (dot(term_low, look_high) + dot(term_high, look_low))
         turn = [turn_ref[k : k + 1, first * WIN : first * WIN + count] for k in range(turn_ref.shape[0])]
-        real = jnp.zeros((tall, count), jnp.float32)
-        imag = jnp.zeros((tall, count), jnp.float32)
-        for k in reversed(range(width // BLOCK // step)):
-            real, imag = rotate(real, imag, turn[0], turn[1])
-            piece = part[k * tall : (k + 1) * tall]
-            real, imag = real + piece[:, :count], imag + piece[:, count:]
+        pieces = []
+        for k in range(0, part.shape[0], tall):
+            pieces.append((part[k : k + tall, :count], part[k : k + tall, count:]))
+        for k in range(hops):
+            merged = []
+            for near, far in zip(pieces[::2], pieces[1::2]):
+                moved = rotate(*far, turn[2 * k], turn[2 * k + 1])
+                merged.append((near[0] + moved[0], near[1] + moved[1]))
+            pieces = merged
+        (real, imag), = pieces
         total_real = total_imag = 0.0
         for k in range(step):
             mine = slice(k * rows, (k + 1) * rows)
-            piece = rotate(real[mine], imag[mine], turn[2 + 2 * k], turn[3 + 2 * k])
+            piece = rotate(real[mine], imag[mine], turn[2 * (hops + k)], turn[2 * (hops + k) + 1])
             total_real, total_imag = total_real + piece[0], total_imag + piece[1]
-        out_ref[:, start : start + count] = total_real
-        out_ref[:, start + count : start + 2 * count] = total_imag
-
-
-def own_kernel(group, offset_hbm, term_hbm, look_ref, turn_ref, out_ref, *scratch):
+        yield start, count, total_real, total_imag
+
+
+def own_kernel(group, step, offset_hbm, term_hbm, look_ref, turn_ref, out_ref, *scratch):
     offset_ref, term_ref, sems = scratch
     moves = ((offset_hbm, offset_ref), (term_hbm, term_ref))
     copies = [pltpu.make_async_copy(a, b, sems.at[k]) for k, (a, b) in enumerate(moves)]
@@ -112,22 +115,36 @@
         copy.start()
     anchor = lax.axis_index("facet") % SIDE * FACET
     copies[0].wait()
-    write_tables(group, anchor, offset_ref, look_ref, turn_ref)
+    write_tables(group, step, anchor, offset_ref, look_ref, turn_ref)
     copies[1].wait()
-    write_columns(group, term_ref, look_ref, turn_ref, out_ref)
+    for start, count, real, imag in columns(group, step, term_ref, look_ref, turn_ref):
+        out_ref[:, start : start + count] = real
+        out_ref[:, start + count : start + 2 * count] = imag
+
+
+def other_kernel(group, step, term_ref, look_ref, turn_ref, own_ref, out_ref):
+    rows = own_ref.shape[0]
+    odd = lax.axis_index("chan") % 2 == 1
+    for start, count, *other in columns(group, step, term_ref, look_ref, turn_ref):
+        for k, value in enumerate(other):
+            place = slice(start + k * count, start + (k + 1) * count)
+            own = own_ref[:, place]
+            out_ref[:rows, place] = jnp.where(odd, value, own)
+            out_ref[rows:, place] = jnp.where(odd, own, value)
 
 
 def own_columns(offsets, taylor):
-    rows = taylor.shape[2]
+    rows, width = taylor.shape[2:]
     subgrids = offsets.shape[1]
     step = max(8 // rows, 1)
+    hops = (width // BLOCK // step).bit_length() - 1
     shapes = [
         jax.ShapeDtypeStruct((2, BLOCK, 2 * subgrids * WIN), jnp.bfloat16),
-        jax.ShapeDtypeStruct((2 + 2 * step, subgrids * WIN), jnp.float32),
+        jax.ShapeDtypeStruct((2 * (hops + step), subgrids * WIN), jnp.float32),
         jax.ShapeDtypeStruct((rows, 2 * subgrids * WIN), jnp.float32),
     ]
     return pl.pallas_call(
-        functools.partial(own_kernel, math.gcd(subgrids, 4)),
+        functools.partial(own_kernel, math.gcd(subgrids, 4), step),
         in_specs=[pl.BlockSpec(memory_space=pltpu.HBM)] * 2,
         out_specs=[pl.BlockSpec(memory_space=pltpu.VMEM)] * 3,
         out_shape=shapes,
@@ -142,18 +159,18 @@
     )(*(pltpu.with_memory_space_constraint(array, pltpu.HBM) for array in (offsets, taylor)))
 
 
-def column_transform(taylor, tables):
-    rows, width = taylor.shape[2:]
-    columns = tables[0].shape[2]
+def both_columns(taylor, tables, own):
+    rows = taylor.shape[2]
+    columns_out = tables[0].shape[2]
     return pl.pallas_call(
-        functools.partial(write_columns, math.gcd(columns // (2 * WIN), 4)),
-        in_specs=[pl.BlockSpec(memory_space=pltpu.VMEM)] * 3,
+        functools.partial(other_kernel, math.gcd(columns_out // (2 * WIN), 4), max(8 // rows, 1)),
+        in_specs=[pl.BlockSpec(memory_space=pltpu.VMEM)] * 4,
         out_specs=pl.BlockSpec(memory_space=pltpu.VMEM),
-        out_shape=jax.ShapeDtypeStruct((rows, columns), jnp.float32),
+        out_shape=jax.ShapeDtypeStruct((2 * rows, columns_out), jnp.float32),
         cost_estimate=lasting(0.35),
         compiler_params=pltpu.CompilerParams(vmem_limit_bytes=grant(taylor, *tables)),
-        name="column_transform",
-    )(taylor, *tables)
+        name="both_columns",
+    )(taylor, *tables, own)
 
 
 def exchange(value, facets, chans, flip_facet, flip_chan):
@@ -297,22 +314,33 @@
     row = jnp.concatenate(
         [sum(value[:, k : k + WIN] for k in range(0, LANE, WIN)) for value in (real_row, imag_row)], axis=1
     )
-    high, low = split(row)
-    both = jnp.concatenate(
-        [jnp.concatenate([high, high], axis=1), jnp.concatenate([low, jnp.zeros_like(low)], axis=1)], axis=0
-    )
-    here = lax.broadcasted_iota(jnp.int32, (blocks, block_ref.shape[2]), 0)
-    dot = functools.partial(jnp.dot, preferred_element_type=jnp.float32)
-    total = 0.0
-    for b in range(blocks):
-        wide = dot(both, block_ref[b])
-        total = jnp.where(here == b, wide[:blocks] + wide[blocks:], total)
-    for b in range(blocks):
-        out_ref[b] = total[b : b + 1]
+    none = jnp.zeros((8, WIN), jnp.float32)
+    odd = lax.broadcasted_iota(jnp.int32, (8, 4 * WIN), 0) % 2 == 1
+    here = lax.broadcasted_iota(jnp.int32, (8, block_ref.shape[2]), 0) // 2
+    vis = block_ref.shape[2] // 2
+    for first in range(0, blocks, 8):
+        mine = row[first : first + 8]
+        high = mine.astype(jnp.bfloat16).astype(jnp.float32)
+        sides = []
+        for value, again in ((high, True), (mine - high, False)):
+            for part in (value[:, :WIN], value[:, WIN:]):
+                wide = [part, part if again else none]
+                even_side, odd_side = jnp.concatenate([*wide, none, none], axis=1), jnp.concatenate([none, none, *wide], axis=1)
+                sides.append(jnp.where(odd, odd_side, even_side))
+        left = jnp.concatenate(sides, axis=0).astype(jnp.bfloat16)
+        real_c, imag_c = 0.0, 0.0
+        for b in range(4):
+            wide = jnp.dot(left, block_ref[first // 2 + b], preferred_element_type=jnp.float32)
+            real_c = jnp.where(here == b, wide[:8] + wide[16:24], real_c)
+            imag_c = jnp.where(here == b, wide[8:16] + wide[24:], imag_c)
+        real_v, imag_v = real_c[:, :vis] - imag_c[:, vis:], real_c[:, vis:] + imag_c[:, :vis]
+        for b in range(8):
+            out_ref[first + b, :, :vis] = real_v[b : b + 1]
+            out_ref[first + b, :, vis:] = imag_v[b : b + 1]
 
 
 def finish(pieces, weights, transformed):
-    blocks, _, width = transformed.shape
+    blocks, width = 2 * transformed.shape[0], transformed.shape[2]
     return pl.pallas_call(
         functools.partial(finish_kernel, len(pieces)),
         in_specs=[pl.BlockSpec(memory_space=pltpu.VMEM)] * (len(pieces) + 4),
@@ -332,18 +360,16 @@
     sines = jnp.where(here < WIN, -sines, sines)
     table_high, table_low = split(jnp.where((here < WIN) == (there < WIN), cosines, sines) * (1.0 / WIN))
     dot = functools.partial(jnp.dot, preferred_element_type=jnp.float32)
-    for b in range(0, out_ref.shape[0], 2):
+    for b in range(0, fourier_ref.shape[0], 2):
         pair = [
             jnp.concatenate([fourier_ref[k, 0, :, :vis], fourier_ref[k, 0, :, vis:]], axis=0) for k in (b, b + 1)
         ]
         high, low = split(jnp.concatenate(pair, axis=1))
         done = dot(table_high, high) + (dot(table_low, high) + dot(table_high, low))
         for k in (0, 1):
-            real, imag = done[:WIN, k * vis : (k + 1) * vis], done[WIN:, k * vis : (k + 1) * vis]
-            matrix = jnp.concatenate(
-                [jnp.concatenate([real, imag], axis=1), jnp.concatenate([-imag, real], axis=1)], axis=0
-            )
-            out_ref[b + k, : 2 * WIN], out_ref[b + k, 2 * WIN :] = split(matrix)
+            matrix = jnp.concatenate([done[:WIN, k * vis : (k + 1) * vis], done[WIN:, k * vis : (k + 1) * vis]], axis=1)
+            start = 2 * WIN * k
+            out_ref[b // 2, start : start + WIN], out_ref[b // 2, start + WIN : start + 2 * WIN] = split(matrix)
 
 
 def transform_blocks(fourier):
@@ -353,7 +379,7 @@
         block_kernel,
         in_specs=[pl.BlockSpec(memory_space=pltpu.VMEM)],
         out_specs=pl.BlockSpec(memory_space=pltpu.VMEM),
-        out_shape=jax.ShapeDtypeStruct((blocks, 4 * WIN, 2 * vis), jnp.bfloat16),
+        out_shape=jax.ShapeDtypeStruct((blocks // 2, 4 * WIN, 2 * vis), jnp.bfloat16),
         cost_estimate=lasting(0.7),
         compiler_params=pltpu.CompilerParams(vmem_limit_bytes=grant(fourier, fourier, fourier)),
         name="transform_blocks",
@@ -362,13 +388,10 @@
 
 def local(taylor, chan_coord, sub_offset, sub_owner, tile_list, fourier):
     facets, chans = lax.axis_size("facet"), lax.axis_size("chan")
-    chan = lax.axis_index("chan")
     offsets = sub_offset.T
     beside = exchange(taylor, facets, chans, 0, 1)
     *tables, own = own_columns(offsets, taylor)
-    other = column_transform(beside, tables)
-    odd = chan % 2 == 1
-    both = jnp.concatenate([jnp.where(odd, other, own), jnp.where(odd, own, other)], axis=0)
+    both = both_columns(beside, tables, own)
     *weights, blocks = finish_weights(offsets, sub_owner, tile_list, chan_coord, fourier, facets, chans, taylor.shape[2])
     transformed = transform_blocks(blocks)
     pieces = gather_terms(both, facets, chans)

time: 18.3 us -> 18 us (0.984)
  Pallas kernels: 4.74 us -> 4.52 us
where the time goes in v5:
time: 18 us; the launch traced here: 17.8 us
  starting transfers between devices  9.18 us (51%)
  Pallas kernels  4.52 us (25%)
  waiting for transfers between devices  4.03 us (22%)
    ppermute x5, starting transfers between devices, exchange(): return lax.ppermute(value, ('facet', 'chan'), pairs)  9.18 us
    ppermute x5, waiting for transfers between devices, exchange(): return lax.ppermute(value, ('facet', 'chan'), pairs)  4.03 us
    pallas_call x1, Pallas kernels, finish_weights(): pl.pallas_call(functools.partial(weight_kernel, rows), in_specs=[pl.Block...  1.27 us
    pallas_call x1, Pallas kernels, own_columns(): pl.pallas_call(functools.partial(own_kernel, math.gcd(subgrids, 4), step)...  1.22 us
    pallas_call x1, Pallas kernels, finish(): pl.pallas_call(functools.partial(finish_kernel, len(pieces)), in_specs=[p...  1.09 us
    pallas_call x1, Pallas kernels, transform_blocks(): pl.pallas_call(block_kernel, in_specs=[pl.BlockSpec(memory_space=pltpu.VM...  0.65 us
  transfers between devices with their start and end apart: 5, of which 4 were waited for; matrix products, arithmetic and copies ran while one was open for 0% of the time, Pallas kernels for 18%

profile of v5, /device:TPU:0, one launch (start us, length us, event | category | flops | bytes accessed | tf_op | source)
XLA Modules:
  0.0 17.8 jit_solution(1827932071054848659)
XLA Ops:
  0.0 0.5 %collective-permute-start = (f32[1,1,4,8192]{3,2,1,0:T(4,128)}, f32[1,1,4,8192]{3,2,1,0:T(4,128)S(1)}, u32[]{:S(2)}, u32[]{:S(2)}) collective-permute-start(f32[1,1,4,8192]{3,2,1,0:T(4,128)} %term_hbm.1), channel_id=1, source_target_pairs={{0,1},{1,0},{2,3},{3,2},{4,5},{5,4},{6,7},{7,6},{8,9},{9,8},{10,11... | collective-permute-start | bytes 393224 | tf_op jit(solution)/shard_map/ppermute | solution.py:180
  0.5 1.2 %own_columns.1 = (bf16[2,256,512]{2,1,0:T(8,128)(2,1)S(1)}, f32[12,256]{1,0:T(8,128)S(1)}, f32[4,512]{1,0:T(4,128)S(1)}) custom-call(s32[2,4]{1,0:T(2,128)} %bitcast.5, f32[1,1,4,8192]{3,2,1,0:T(4,128)} %term_hbm.1), custom_call_target="tpu_custom_call" | custom-call | flops 1610000000 | tf_op jit(solution)/shard_map/own_columns/pallas_call | solution.py:146
  1.7 0.0 collective-permute-done.term_ref
  1.7 0.3 %both_columns.1 = f32[8,512]{1,0:T(8,128)S(1)} custom-call(f32[1,1,4,8192]{3,2,1,0:T(4,128)S(1)} %collective-permute-done.term_ref, bf16[2,256,512]{2,1,0:T(8,128)(2,1)S(1)} %get-tuple-element.12.look_ref, f32[12,256]{1,0:T(8,128)S(1)} %get-tuple-element.13.turn_ref, f32[4,512]{1,0:T(4,128)S(1)} %get-tuple-element.14.own_ref), custom_call_target="tpu_custom_call" | custom-call | flops 402500000 | tf_op jit(solution)/shard_map/both_columns/pallas_call | solution.py:165
  2.0 2.7 %collective-permute-start.1 = (f32[8,512]{1,0:T(8,128)S(1)}, f32[8,512]{1,0:T(8,128)S(1)}, u32[]{:S(2)}, u32[]{:S(2)}) collective-permute-start(f32[8,512]{1,0:T(8,128)S(1)} %both_columns.1), channel_id=1, source_target_pairs={{0,5},{1,4},{2,7},{3,6},{4,1},{5,0},{6,3},{7,2},{8,13},{9,12},{10,... | collective-permute-start | bytes 49160 | tf_op jit(solution)/shard_map/ppermute | solution.py:180
  4.7 1.4 %collective-permute-done.1 = f32[8,512]{1,0:T(8,128)S(1)} collective-permute-done((f32[8,512]{1,0:T(8,128)S(1)}, f32[8,512]{1,0:T(8,128)S(1)}, u32[]{:S(2)}, u32[]{:S(2)}) %collective-permute-start.1) | collective-permute-done | bytes 16416 | tf_op jit(solution)/shard_map/ppermute | solution.py:180
  6.1 1.8 %collective-permute-start.2 = (f32[8,512]{1,0:T(8,128)S(1)}, f32[8,512]{1,0:T(8,128)S(1)}, u32[]{:S(2)}, u32[]{:S(2)}) collective-permute-start(f32[8,512]{1,0:T(8,128)S(1)} %add.9), channel_id=1, source_target_pairs={{0,9},{1,8},{2,11},{3,10},{4,13},{5,12},{6,15},{7,14},{8,1},{9,0},... | collective-permute-start | bytes 49160 | tf_op jit(solution)/shard_map/ppermute | solution.py:180
  7.9 1.4 %collective-permute-done.2 = f32[8,512]{1,0:T(8,128)S(1)} collective-permute-done((f32[8,512]{1,0:T(8,128)S(1)}, f32[8,512]{1,0:T(8,128)S(1)}, u32[]{:S(2)}, u32[]{:S(2)}) %collective-permute-start.2) | collective-permute-done | bytes 16416 | tf_op jit(solution)/shard_map/ppermute | solution.py:180
  9.4 2.7 %collective-permute-start.3 = (f32[8,512]{1,0:T(8,128)S(1)}, f32[8,512]{1,0:T(8,128)S(1)}, u32[]{:S(2)}, u32[]{:S(2)}) collective-permute-start(f32[8,512]{1,0:T(8,128)S(1)} %add.10), channel_id=1, source_target_pairs={{0,17},{1,16},{2,19},{3,18},{4,21},{5,20},{6,23},{7,22},{8,25},{9,... | collective-permute-start | bytes 49160 | tf_op jit(solution)/shard_map/ppermute | solution.py:180
  12.1 1.3 %finish_weights.1 = (f32[2,4,16,128]{3,2,1,0:T(8,128)S(1)}, f32[16,256]{1,0:T(8,128)S(1)}, f32[2,8,128]{2,1,0:T(8,128)S(1)}, f32[16,1,64,256]{3,2,1,0:T(8,128)S(1)}) custom-call(s32[2,4]{1,0:T(2,128)} %bitcast.6, s32[4]{0:T(128)} %owner_hbm.1, s32[16]{0:T(128)} %tile_hbm.1, f32[4]{0:T(128)} %coord_hbm.1, f32[16,1,64,256]{3,2,1,0:T(8,128)} %fourier_hbm.1), custom_call_target="tpu_custom_call" | custom-call | flops 1495000064 | tf_op jit(solution)/shard_map/finish_weights/pallas_call | solution.py:267
  13.4 0.2 collective-permute-done.3
  13.5 1.5 %collective-permute-start.4 = (f32[8,512]{1,0:T(8,128)S(1)}, f32[8,512]{1,0:T(8,128)S(1)}, u32[]{:S(2)}, u32[]{:S(2)}) collective-permute-start(f32[8,512]{1,0:T(8,128)S(1)} %add.11), channel_id=1, source_target_pairs={{0,3},{1,2},{2,1},{3,0},{4,7},{5,6},{6,5},{7,4},{8,11},{9,10},{10,... | collective-permute-start | bytes 49160 | tf_op jit(solution)/shard_map/ppermute | solution.py:180
  15.1 0.7 %transform_blocks.1.refs_5_ = bf16[8,256,256]{2,1,0:T(8,128)(2,1)S(1)} custom-call(f32[16,1,64,256]{3,2,1,0:T(8,128)S(1)} %get-tuple-element.18.fourier_ref), custom_call_target="tpu_custom_call" | custom-call | flops 805000000 | tf_op jit(solution)/shard_map/transform_blocks/pallas_call | solution.py:378
  15.7 1.0 %collective-permute-done.4 = f32[8,512]{1,0:T(8,128)S(1)} collective-permute-done((f32[8,512]{1,0:T(8,128)S(1)}, f32[8,512]{1,0:T(8,128)S(1)}, u32[]{:S(2)}, u32[]{:S(2)}) %collective-permute-start.4) | collective-permute-done | bytes 16416 | tf_op jit(solution)/shard_map/ppermute | solution.py:180
  16.7 1.1 %finish.1 = f32[16,1,256]{2,1,0:T(1,128)} custom-call(f32[1,8,512]{2,1,0:T(8,128)S(1)} %bitcast.3, f32[1,8,512]{2,1,0:T(8,128)S(1)} %bitcast.4, f32[2,4,16,128]{3,2,1,0:T(8,128)S(1)} %get-tuple-element.15.refs_2_, f32[16,256]{1,0:T(8,128)S(1)} %get-tuple-element.16.refs_3_, f32[2,8,128]{2,1,0:T(8,128)S(1)} %get-tuple-element.17.refs_4_, ...), custom_call_target="tpu_custom_call" | custom-call | flops 1495000064 | tf_op jit(solution)/shard_map/finish/pallas_call | solution.py:344
  (3 shorter events, 0.0 us)
Async XLA Ops:
  0.0 1.7 %collective-permute-start = (f32[1,1,4,8192]{3,2,1,0:T(4,128)}, f32[1,1,4,8192]{3,2,1,0:T(4,128)S(1)}, u32[]{:S(2)}, u32[]{:S(2)}) collective-permute-start(f32[1,1,4,8192]{3,2,1,0:T(4,128)} %term_hbm.1), channel_id=1, source_target_pairs={{0,1},{1,0},{2,3},{3,2},{4,5},{5,4},{6,7},{7,6},{8,9},{9,8},{10,11... | collective-permute-start | bytes 393224 | tf_op jit(solution)/shard_map/ppermute | solution.py:180
  2.0 4.1 %collective-permute-start.1 = (f32[8,512]{1,0:T(8,128)S(1)}, f32[8,512]{1,0:T(8,128)S(1)}, u32[]{:S(2)}, u32[]{:S(2)}) collective-permute-start(f32[8,512]{1,0:T(8,128)S(1)} %both_columns.1), channel_id=1, source_target_pairs={{0,5},{1,4},{2,7},{3,6},{4,1},{5,0},{6,3},{7,2},{8,13},{9,12},{10,... | collective-permute-start | bytes 49160 | tf_op jit(solution)/shard_map/ppermute | solution.py:180
  6.1 3.2 %collective-permute-start.2 = (f32[8,512]{1,0:T(8,128)S(1)}, f32[8,512]{1,0:T(8,128)S(1)}, u32[]{:S(2)}, u32[]{:S(2)}) collective-permute-start(f32[8,512]{1,0:T(8,128)S(1)} %add.9), channel_id=1, source_target_pairs={{0,9},{1,8},{2,11},{3,10},{4,13},{5,12},{6,15},{7,14},{8,1},{9,0},... | collective-permute-start | bytes 49160 | tf_op jit(solution)/shard_map/ppermute | solution.py:180
  9.4 4.2 %collective-permute-start.3 = (f32[8,512]{1,0:T(8,128)S(1)}, f32[8,512]{1,0:T(8,128)S(1)}, u32[]{:S(2)}, u32[]{:S(2)}) collective-permute-start(f32[8,512]{1,0:T(8,128)S(1)} %add.10), channel_id=1, source_target_pairs={{0,17},{1,16},{2,19},{3,18},{4,21},{5,20},{6,23},{7,22},{8,25},{9,... | collective-permute-start | bytes 49160 | tf_op jit(solution)/shard_map/ppermute | solution.py:180
  13.5 3.2 %collective-permute-start.4 = (f32[8,512]{1,0:T(8,128)S(1)}, f32[8,512]{1,0:T(8,128)S(1)}, u32[]{:S(2)}, u32[]{:S(2)}) collective-permute-start(f32[8,512]{1,0:T(8,128)S(1)} %add.11), channel_id=1, source_target_pairs={{0,3},{1,2},{2,1},{3,0},{4,7},{5,6},{6,5},{7,4},{8,11},{9,10},{10,... | collective-permute-start | bytes 49160 | tf_op jit(solution)/shard_map/ppermute | solution.py:180

commit v6 on v5

--- a/solution.py
+++ b/solution.py
@@ -311,23 +311,19 @@
         for k in range(0, count, LANE):
             real_row = real_row + (real_t * mask)[:, k : k + LANE]
             imag_row = imag_row + (imag_t * mask)[:, k : k + LANE]
-    row = jnp.concatenate(
-        [sum(value[:, k : k + WIN] for k in range(0, LANE, WIN)) for value in (real_row, imag_row)], axis=1
-    )
-    none = jnp.zeros((8, WIN), jnp.float32)
-    odd = lax.broadcasted_iota(jnp.int32, (8, 4 * WIN), 0) % 2 == 1
+    real_row, imag_row = (sum(pltpu.roll(value, k, 1) for k in range(0, LANE, WIN)) for value in (real_row, imag_row))
+    lane = lax.broadcasted_iota(jnp.int32, (8, LANE), 1)
+    keep = lane // WIN == lax.broadcasted_iota(jnp.int32, (8, LANE), 0) % 2
     here = lax.broadcasted_iota(jnp.int32, (8, block_ref.shape[2]), 0) // 2
     vis = block_ref.shape[2] // 2
     for first in range(0, blocks, 8):
-        mine = row[first : first + 8]
-        high = mine.astype(jnp.bfloat16).astype(jnp.float32)
-        sides = []
-        for value, again in ((high, True), (mine - high, False)):
-            for part in (value[:, :WIN], value[:, WIN:]):
-                wide = [part, part if again else none]
-                even_side, odd_side = jnp.concatenate([*wide, none, none], axis=1), jnp.concatenate([none, none, *wide], axis=1)
-                sides.append(jnp.where(odd, odd_side, even_side))
-        left = jnp.concatenate(sides, axis=0).astype(jnp.bfloat16)
+        highs, lows = [], []
+        for value in (real_row, imag_row):
+            mine = jnp.where(keep, value[first : first + 8], 0.0)
+            high = mine.astype(jnp.bfloat16).astype(jnp.float32)
+            highs.append(jnp.concatenate([high, high], axis=1))
+            lows.append(jnp.concatenate([mine - high, jnp.zeros_like(mine)], axis=1))
+        left = jnp.concatenate(highs + lows, axis=0).astype(jnp.bfloat16)
         real_c, imag_c = 0.0, 0.0
         for b in range(4):
             wide = jnp.dot(left, block_ref[first // 2 + b], preferred_element_type=jnp.float32)
@@ -368,8 +364,9 @@
         done = dot(table_high, high) + (dot(table_low, high) + dot(table_high, low))
         for k in (0, 1):
             matrix = jnp.concatenate([done[:WIN, k * vis : (k + 1) * vis], done[WIN:, k * vis : (k + 1) * vis]], axis=1)
-            start = 2 * WIN * k
-            out_ref[b // 2, start : start + WIN], out_ref[b // 2, start + WIN : start + 2 * WIN] = split(matrix)
+            high, low = split(matrix)
+            out_ref[b // 2, WIN * k : WIN * (k + 1)] = high
+            out_ref[b // 2, WIN * (k + 2) : WIN * (k + 3)] = low
 
 
 def transform_blocks(fourier):

time: 18 us -> 17.8 us (0.989)
  no operation moved by 1% of the time
where the time goes in v6:
time: 17.8 us; the launch traced here: 17.7 us
  starting transfers between devices  9.18 us (52%)
  Pallas kernels  4.39 us (25%)
  waiting for transfers between devices  4.03 us (23%)
    ppermute x5, starting transfers between devices, exchange(): return lax.ppermute(value, ('facet', 'chan'), pairs)  9.18 us
    ppermute x5, waiting for transfers between devices, exchange(): return lax.ppermute(value, ('facet', 'chan'), pairs)  4.03 us
    pallas_call x1, Pallas kernels, finish_weights(): pl.pallas_call(functools.partial(weight_kernel, rows), in_specs=[pl.Block...  1.27 us
    pallas_call x1, Pallas kernels, own_columns(): pl.pallas_call(functools.partial(own_kernel, math.gcd(subgrids, 4), step)...  1.22 us
    pallas_call x1, Pallas kernels, finish(): pl.pallas_call(functools.partial(finish_kernel, len(pieces)), in_specs=[p...  0.96 us
    pallas_call x1, Pallas kernels, transform_blocks(): pl.pallas_call(block_kernel, in_specs=[pl.BlockSpec(memory_space=pltpu.VM...  0.65 us
  transfers between devices with their start and end apart: 5, of which 4 were waited for; matrix products, arithmetic and copies ran while one was open for 0% of the time, Pallas kernels for 18%

profile of v6, /device:TPU:0, one launch (start us, length us, event | category | flops | bytes accessed | tf_op | source)
XLA Modules:
  0.0 17.7 jit_solution(9366231794868275743)
XLA Ops:
  0.0 0.5 %collective-permute-start = (f32[1,1,4,8192]{3,2,1,0:T(4,128)}, f32[1,1,4,8192]{3,2,1,0:T(4,128)S(1)}, u32[]{:S(2)}, u32[]{:S(2)}) collective-permute-start(f32[1,1,4,8192]{3,2,1,0:T(4,128)} %term_hbm.1), channel_id=1, source_target_pairs={{0,1},{1,0},{2,3},{3,2},{4,5},{5,4},{6,7},{7,6},{8,9},{9,8},{10,11... | collective-permute-start | bytes 393224 | tf_op jit(solution)/shard_map/ppermute | solution.py:180
  0.5 1.2 %own_columns.1 = (bf16[2,256,512]{2,1,0:T(8,128)(2,1)S(1)}, f32[12,256]{1,0:T(8,128)S(1)}, f32[4,512]{1,0:T(4,128)S(1)}) custom-call(s32[2,4]{1,0:T(2,128)} %bitcast.5, f32[1,1,4,8192]{3,2,1,0:T(4,128)} %term_hbm.1), custom_call_target="tpu_custom_call" | custom-call | flops 1610000000 | tf_op jit(solution)/shard_map/own_columns/pallas_call | solution.py:146
  1.7 0.0 collective-permute-done.term_ref
  1.7 0.3 %both_columns.1 = f32[8,512]{1,0:T(8,128)S(1)} custom-call(f32[1,1,4,8192]{3,2,1,0:T(4,128)S(1)} %collective-permute-done.term_ref, bf16[2,256,512]{2,1,0:T(8,128)(2,1)S(1)} %get-tuple-element.12.look_ref, f32[12,256]{1,0:T(8,128)S(1)} %get-tuple-element.13.turn_ref, f32[4,512]{1,0:T(4,128)S(1)} %get-tuple-element.14.own_ref), custom_call_target="tpu_custom_call" | custom-call | flops 402500000 | tf_op jit(solution)/shard_map/both_columns/pallas_call | solution.py:165
  2.0 2.7 %collective-permute-start.1 = (f32[8,512]{1,0:T(8,128)S(1)}, f32[8,512]{1,0:T(8,128)S(1)}, u32[]{:S(2)}, u32[]{:S(2)}) collective-permute-start(f32[8,512]{1,0:T(8,128)S(1)} %both_columns.1), channel_id=1, source_target_pairs={{0,5},{1,4},{2,7},{3,6},{4,1},{5,0},{6,3},{7,2},{8,13},{9,12},{10,... | collective-permute-start | bytes 49160 | tf_op jit(solution)/shard_map/ppermute | solution.py:180
  4.7 1.4 %collective-permute-done.1 = f32[8,512]{1,0:T(8,128)S(1)} collective-permute-done((f32[8,512]{1,0:T(8,128)S(1)}, f32[8,512]{1,0:T(8,128)S(1)}, u32[]{:S(2)}, u32[]{:S(2)}) %collective-permute-start.1) | collective-permute-done | bytes 16416 | tf_op jit(solution)/shard_map/ppermute | solution.py:180
  6.1 1.8 %collective-permute-start.2 = (f32[8,512]{1,0:T(8,128)S(1)}, f32[8,512]{1,0:T(8,128)S(1)}, u32[]{:S(2)}, u32[]{:S(2)}) collective-permute-start(f32[8,512]{1,0:T(8,128)S(1)} %add.9), channel_id=1, source_target_pairs={{0,9},{1,8},{2,11},{3,10},{4,13},{5,12},{6,15},{7,14},{8,1},{9,0},... | collective-permute-start | bytes 49160 | tf_op jit(solution)/shard_map/ppermute | solution.py:180
  7.9 1.4 %collective-permute-done.2 = f32[8,512]{1,0:T(8,128)S(1)} collective-permute-done((f32[8,512]{1,0:T(8,128)S(1)}, f32[8,512]{1,0:T(8,128)S(1)}, u32[]{:S(2)}, u32[]{:S(2)}) %collective-permute-start.2) | collective-permute-done | bytes 16416 | tf_op jit(solution)/shard_map/ppermute | solution.py:180
  9.4 2.7 %collective-permute-start.3 = (f32[8,512]{1,0:T(8,128)S(1)}, f32[8,512]{1,0:T(8,128)S(1)}, u32[]{:S(2)}, u32[]{:S(2)}) collective-permute-start(f32[8,512]{1,0:T(8,128)S(1)} %add.10), channel_id=1, source_target_pairs={{0,17},{1,16},{2,19},{3,18},{4,21},{5,20},{6,23},{7,22},{8,25},{9,... | collective-permute-start | bytes 49160 | tf_op jit(solution)/shard_map/ppermute | solution.py:180
  12.1 1.3 %finish_weights.1 = (f32[2,4,16,128]{3,2,1,0:T(8,128)S(1)}, f32[16,256]{1,0:T(8,128)S(1)}, f32[2,8,128]{2,1,0:T(8,128)S(1)}, f32[16,1,64,256]{3,2,1,0:T(8,128)S(1)}) custom-call(s32[2,4]{1,0:T(2,128)} %bitcast.6, s32[4]{0:T(128)} %owner_hbm.1, s32[16]{0:T(128)} %tile_hbm.1, f32[4]{0:T(128)} %coord_hbm.1, f32[16,1,64,256]{3,2,1,0:T(8,128)} %fourier_hbm.1), custom_call_target="tpu_custom_call" | custom-call | flops 1495000064 | tf_op jit(solution)/shard_map/finish_weights/pallas_call | solution.py:267
  13.4 0.2 collective-permute-done.3
  13.5 1.5 %collective-permute-start.4 = (f32[8,512]{1,0:T(8,128)S(1)}, f32[8,512]{1,0:T(8,128)S(1)}, u32[]{:S(2)}, u32[]{:S(2)}) collective-permute-start(f32[8,512]{1,0:T(8,128)S(1)} %add.11), channel_id=1, source_target_pairs={{0,3},{1,2},{2,1},{3,0},{4,7},{5,6},{6,5},{7,4},{8,11},{9,10},{10,... | collective-permute-start | bytes 49160 | tf_op jit(solution)/shard_map/ppermute | solution.py:180
  15.1 0.7 %transform_blocks.1.refs_5_ = bf16[8,256,256]{2,1,0:T(8,128)(2,1)S(1)} custom-call(f32[16,1,64,256]{3,2,1,0:T(8,128)S(1)} %get-tuple-element.18.fourier_ref), custom_call_target="tpu_custom_call" | custom-call | flops 805000000 | tf_op jit(solution)/shard_map/transform_blocks/pallas_call | solution.py:375
  15.7 1.0 %collective-permute-done.4 = f32[8,512]{1,0:T(8,128)S(1)} collective-permute-done((f32[8,512]{1,0:T(8,128)S(1)}, f32[8,512]{1,0:T(8,128)S(1)}, u32[]{:S(2)}, u32[]{:S(2)}) %collective-permute-start.4) | collective-permute-done | bytes 16416 | tf_op jit(solution)/shard_map/ppermute | solution.py:180
  16.7 1.0 %finish.1 = f32[16,1,256]{2,1,0:T(1,128)} custom-call(f32[1,8,512]{2,1,0:T(8,128)S(1)} %bitcast.3, f32[1,8,512]{2,1,0:T(8,128)S(1)} %bitcast.4, f32[2,4,16,128]{3,2,1,0:T(8,128)S(1)} %get-tuple-element.15.refs_2_, f32[16,256]{1,0:T(8,128)S(1)} %get-tuple-element.16.refs_3_, f32[2,8,128]{2,1,0:T(8,128)S(1)} %get-tuple-element.17.refs_4_, ...), custom_call_target="tpu_custom_call" | custom-call | flops 1495000064 | tf_op jit(solution)/shard_map/finish/pallas_call | solution.py:340
  (3 shorter events, 0.0 us)
Async XLA Ops:
  0.0 1.7 %collective-permute-start = (f32[1,1,4,8192]{3,2,1,0:T(4,128)}, f32[1,1,4,8192]{3,2,1,0:T(4,128)S(1)}, u32[]{:S(2)}, u32[]{:S(2)}) collective-permute-start(f32[1,1,4,8192]{3,2,1,0:T(4,128)} %term_hbm.1), channel_id=1, source_target_pairs={{0,1},{1,0},{2,3},{3,2},{4,5},{5,4},{6,7},{7,6},{8,9},{9,8},{10,11... | collective-permute-start | bytes 393224 | tf_op jit(solution)/shard_map/ppermute | solution.py:180
  2.0 4.1 %collective-permute-start.1 = (f32[8,512]{1,0:T(8,128)S(1)}, f32[8,512]{1,0:T(8,128)S(1)}, u32[]{:S(2)}, u32[]{:S(2)}) collective-permute-start(f32[8,512]{1,0:T(8,128)S(1)} %both_columns.1), channel_id=1, source_target_pairs={{0,5},{1,4},{2,7},{3,6},{4,1},{5,0},{6,3},{7,2},{8,13},{9,12},{10,... | collective-permute-start | bytes 49160 | tf_op jit(solution)/shard_map/ppermute | solution.py:180
  6.1 3.2 %collective-permute-start.2 = (f32[8,512]{1,0:T(8,128)S(1)}, f32[8,512]{1,0:T(8,128)S(1)}, u32[]{:S(2)}, u32[]{:S(2)}) collective-permute-start(f32[8,512]{1,0:T(8,128)S(1)} %add.9), channel_id=1, source_target_pairs={{0,9},{1,8},{2,11},{3,10},{4,13},{5,12},{6,15},{7,14},{8,1},{9,0},... | collective-permute-start | bytes 49160 | tf_op jit(solution)/shard_map/ppermute | solution.py:180
  9.4 4.2 %collective-permute-start.3 = (f32[8,512]{1,0:T(8,128)S(1)}, f32[8,512]{1,0:T(8,128)S(1)}, u32[]{:S(2)}, u32[]{:S(2)}) collective-permute-start(f32[8,512]{1,0:T(8,128)S(1)} %add.10), channel_id=1, source_target_pairs={{0,17},{1,16},{2,19},{3,18},{4,21},{5,20},{6,23},{7,22},{8,25},{9,... | collective-permute-start | bytes 49160 | tf_op jit(solution)/shard_map/ppermute | solution.py:180
  13.5 3.2 %collective-permute-start.4 = (f32[8,512]{1,0:T(8,128)S(1)}, f32[8,512]{1,0:T(8,128)S(1)}, u32[]{:S(2)}, u32[]{:S(2)}) collective-permute-start(f32[8,512]{1,0:T(8,128)S(1)} %add.11), channel_id=1, source_target_pairs={{0,3},{1,2},{2,1},{3,0},{4,7},{5,6},{6,5},{7,4},{8,11},{9,10},{10,... | collective-permute-start | bytes 49160 | tf_op jit(solution)/shard_map/ppermute | solution.py:180

commit v7 on v6

--- a/solution.py
+++ b/solution.py
@@ -180,21 +180,22 @@
     return lax.ppermute(value, ("facet", "chan"), pairs)
 
 
-def gather_terms(both, facets, chans):
+def gather_channel(both, mix, facets, chans):
     near = SIDE if facets > SIDE else facets
+    rows = both.shape[0] // 2
     step = 1
     while step < near:
         both = both + exchange(both, facets, chans, step, 1)
         step *= 2
-    pieces = [both]
-    step = 2
-    while step < chans:
-        pieces = pieces + [exchange(piece, facets, chans, 0, step + 1) for piece in pieces]
-        step *= 2
+    parts = []
+    for k in range(chans // 2):
+        weighted = both * mix[k]
+        part = weighted[:rows] + weighted[rows:]
+        parts.append(exchange(part, facets, chans, 0, 2 * k + 1) if k else part)
     if facets == near:
-        return [piece[None] for piece in pieces]
+        return [part[None] for part in parts]
     groups = [[h * near + f for h in range(facets // near)] for f in range(near)]
-    return [lax.all_gather(piece, "facet", axis=0, axis_index_groups=groups) for piece in pieces]
+    return [lax.all_gather(sum(parts), "facet", axis=0, axis_index_groups=groups)]
 
 
 def weight_kernel(
@@ -243,14 +244,14 @@
                 total = jnp.sum(jnp.where(lane < WIN, value, 0.0), axis=1, keepdims=True) * scale
                 row_ref[part, h * rows + r] = jnp.broadcast_to(total, (blocks, LANE))
 
-    coord = coord_ref[chan]
-    tall = lax.broadcasted_iota(jnp.int32, (2 * rows, LANE), 0)
+    term = 2 * (chan // 2) + lax.broadcasted_iota(jnp.int32, (2 * rows, LANE), 0) // rows
     for k in range(mix_ref.shape[0]):
-        term = 2 * ((chan // 2) ^ k) + tall // rows
+        coord = coord_ref[chan ^ (2 * k + 1) if k else chan]
         power = jnp.ones((2 * rows, LANE), jnp.float32)
         for degree in range(1, TAYLOR):
             power = jnp.where(term >= degree, power * coord, power)
-        mix_ref[k] = power
+        for start in range(0, mix_ref.shape[2], LANE):
+            mix_ref[k, :, start : start + LANE] = power
     copies[4].wait()
 
 
@@ -261,7 +262,7 @@
     shapes = [
         jax.ShapeDtypeStruct((2, facets // near * rows, blocks, LANE), jnp.float32),
         jax.ShapeDtypeStruct((blocks, subgrids * WIN), jnp.float32),
-        jax.ShapeDtypeStruct((chans // 2, 2 * rows, LANE), jnp.float32),
+        jax.ShapeDtypeStruct((chans // 2, 2 * rows, 2 * subgrids * WIN), jnp.float32),
         jax.ShapeDtypeStruct(fourier.shape, jnp.float32),
     ]
     return pl.pallas_call(
@@ -284,9 +285,8 @@
 
 def finish_kernel(pieces, *refs):
     piece_refs = refs[:pieces]
-    row_ref, mask_ref, mix_ref, block_ref, out_ref = refs[pieces:]
-    groups, tall, width = piece_refs[0].shape
-    rows = tall // 2
+    row_ref, mask_ref, block_ref, out_ref = refs[pieces:]
+    groups, rows, width = piece_refs[0].shape
     subgrids = mask_ref.shape[1] // WIN
     group = math.gcd(subgrids, 4)
     count = group * WIN
@@ -296,11 +296,7 @@
         start = 2 * first * WIN
         real_t = imag_t = 0.0
         for h in range(groups):
-            mixed = 0.0
-            for k in range(pieces):
-                weight = jnp.tile(mix_ref[k], (1, 2 * count // LANE))
-                mixed = mixed + piece_refs[k][h, :, start : start + 2 * count] * weight
-            mixed = mixed[:rows] + mixed[rows:]
+            mixed = sum(ref[h, :, start : start + 2 * count] for ref in piece_refs)
             for r in range(rows):
                 real_a = jnp.tile(row_ref[0, h * rows + r], (1, count // LANE))
                 imag_a = jnp.tile(row_ref[1, h * rows + r], (1, count // LANE))
@@ -339,7 +335,7 @@
     blocks, width = 2 * transformed.shape[0], transformed.shape[2]
     return pl.pallas_call(
         functools.partial(finish_kernel, len(pieces)),
-        in_specs=[pl.BlockSpec(memory_space=pltpu.VMEM)] * (len(pieces) + 4),
+        in_specs=[pl.BlockSpec(memory_space=pltpu.VMEM)] * (len(pieces) + 3),
         out_specs=pl.BlockSpec(memory_space=pltpu.VMEM),
         out_shape=jax.ShapeDtypeStruct((blocks, 1, width), jnp.float32),
         cost_estimate=lasting(1.3),
@@ -389,10 +385,12 @@
     beside = exchange(taylor, facets, chans, 0, 1)
     *tables, own = own_columns(offsets, taylor)
     both = both_columns(beside, tables, own)
-    *weights, blocks = finish_weights(offsets, sub_owner, tile_list, chan_coord, fourier, facets, chans, taylor.shape[2])
+    row_weights, mask, mix, blocks = finish_weights(
+        offsets, sub_owner, tile_list, chan_coord, fourier, facets, chans, taylor.shape[2]
+    )
     transformed = transform_blocks(blocks)
-    pieces = gather_terms(both, facets, chans)
-    return finish(pieces, weights, transformed)
+    parts = gather_channel(both, mix, facets, chans)
+    return finish(parts, (row_weights, mask), transformed)
 
 
 def solution(mesh):

time: 17.8 us -> 17.8 us (level)
  no operation moved by 1% of the time
where the time goes in v7:
time: 17.8 us; the launch traced here: 17.6 us
  starting transfers between devices  9.25 us (52%)
  Pallas kernels  4.39 us (25%)
  waiting for transfers between devices  3.94 us (22%)
    ppermute x5, starting transfers between devices, exchange(): return lax.ppermute(value, ('facet', 'chan'), pairs)  9.25 us
    ppermute x5, waiting for transfers between devices, exchange(): return lax.ppermute(value, ('facet', 'chan'), pairs)  3.94 us
    pallas_call x1, Pallas kernels, finish_weights(): pl.pallas_call(functools.partial(weight_kernel, rows), in_specs=[pl.Block...  1.27 us
    pallas_call x1, Pallas kernels, own_columns(): pl.pallas_call(functools.partial(own_kernel, math.gcd(subgrids, 4), step)...  1.22 us
    pallas_call x1, Pallas kernels, finish(): pl.pallas_call(functools.partial(finish_kernel, len(pieces)), in_specs=[p...  0.96 us
    pallas_call x1, Pallas kernels, transform_blocks(): pl.pallas_call(block_kernel, in_specs=[pl.BlockSpec(memory_space=pltpu.VM...  0.65 us
  transfers between devices with their start and end apart: 5, of which 4 were waited for; matrix products, arithmetic and copies ran while one was open for 0% of the time, Pallas kernels for 18%

profile of v7, /device:TPU:0, one launch (start us, length us, event | category | flops | bytes accessed | tf_op | source)
XLA Modules:
  0.0 17.6 jit_solution(2210850365646768675)
XLA Ops:
  0.0 0.5 %collective-permute-start = (f32[1,1,4,8192]{3,2,1,0:T(4,128)}, f32[1,1,4,8192]{3,2,1,0:T(4,128)S(1)}, u32[]{:S(2)}, u32[]{:S(2)}) collective-permute-start(f32[1,1,4,8192]{3,2,1,0:T(4,128)} %term_hbm.1), channel_id=1, source_target_pairs={{0,1},{1,0},{2,3},{3,2},{4,5},{5,4},{6,7},{7,6},{8,9},{9,8},{10,11... | collective-permute-start | bytes 393224 | tf_op jit(solution)/shard_map/ppermute | solution.py:180
  0.5 1.2 %own_columns.1 = (bf16[2,256,512]{2,1,0:T(8,128)(2,1)S(1)}, f32[12,256]{1,0:T(8,128)S(1)}, f32[4,512]{1,0:T(4,128)S(1)}) custom-call(s32[2,4]{1,0:T(2,128)} %bitcast.9, f32[1,1,4,8192]{3,2,1,0:T(4,128)} %term_hbm.1), custom_call_target="tpu_custom_call" | custom-call | flops 1610000000 | tf_op jit(solution)/shard_map/own_columns/pallas_call | solution.py:146
  1.7 0.0 collective-permute-done.term_ref
  1.7 0.3 %both_columns.1 = f32[8,512]{1,0:T(8,128)S(1)} custom-call(f32[1,1,4,8192]{3,2,1,0:T(4,128)S(1)} %collective-permute-done.term_ref, bf16[2,256,512]{2,1,0:T(8,128)(2,1)S(1)} %get-tuple-element.12.look_ref, f32[12,256]{1,0:T(8,128)S(1)} %get-tuple-element.13.turn_ref, f32[4,512]{1,0:T(4,128)S(1)} %get-tuple-element.14.own_ref), custom_call_target="tpu_custom_call" | custom-call | flops 402500000 | tf_op jit(solution)/shard_map/both_columns/pallas_call | solution.py:165
  2.0 2.7 %collective-permute-start.1 = (f32[8,512]{1,0:T(8,128)S(1)}, f32[8,512]{1,0:T(8,128)S(1)}, u32[]{:S(2)}, u32[]{:S(2)}) collective-permute-start(f32[8,512]{1,0:T(8,128)S(1)} %both_columns.1), channel_id=1, source_target_pairs={{0,5},{1,4},{2,7},{3,6},{4,1},{5,0},{6,3},{7,2},{8,13},{9,12},{10,... | collective-permute-start | bytes 49160 | tf_op jit(solution)/shard_map/ppermute | solution.py:180
  4.7 1.4 %collective-permute-done.1 = f32[8,512]{1,0:T(8,128)S(1)} collective-permute-done((f32[8,512]{1,0:T(8,128)S(1)}, f32[8,512]{1,0:T(8,128)S(1)}, u32[]{:S(2)}, u32[]{:S(2)}) %collective-permute-start.1) | collective-permute-done | bytes 16416 | tf_op jit(solution)/shard_map/ppermute | solution.py:180
  6.1 1.8 %collective-permute-start.2 = (f32[8,512]{1,0:T(8,128)S(1)}, f32[8,512]{1,0:T(8,128)S(1)}, u32[]{:S(2)}, u32[]{:S(2)}) collective-permute-start(f32[8,512]{1,0:T(8,128)S(1)} %add.15), channel_id=1, source_target_pairs={{0,9},{1,8},{2,11},{3,10},{4,13},{5,12},{6,15},{7,14},{8,1},{9,0},... | collective-permute-start | bytes 49160 | tf_op jit(solution)/shard_map/ppermute | solution.py:180
  7.9 1.3 %finish_weights.1 = (f32[2,4,16,128]{3,2,1,0:T(8,128)S(1)}, f32[16,256]{1,0:T(8,128)S(1)}, f32[2,8,512]{2,1,0:T(8,128)S(1)}, f32[16,1,64,256]{3,2,1,0:T(8,128)S(1)}) custom-call(s32[2,4]{1,0:T(2,128)} %bitcast.10, s32[4]{0:T(128)} %owner_hbm.1, s32[16]{0:T(128)} %tile_hbm.1, f32[4]{0:T(128)} %coord_hbm.1, f32[16,1,64,256]{3,2,1,0:T(8,128)} %fourier_hbm.1), custom_call_target="tpu_custom_call" | custom-call | flops 1495000064 | tf_op jit(solution)/shard_map/finish_weights/pallas_call | solution.py:268
  9.2 0.2 collective-permute-done.2
  9.4 2.7 %collective-permute-start.3 = (f32[8,512]{1,0:T(8,128)S(1)}, f32[8,512]{1,0:T(8,128)S(1)}, u32[]{:S(2)}, u32[]{:S(2)}) collective-permute-start(f32[8,512]{1,0:T(8,128)S(1)} %add.16), channel_id=1, source_target_pairs={{0,17},{1,16},{2,19},{3,18},{4,21},{5,20},{6,23},{7,22},{8,25},{9,... | collective-permute-start | bytes 49160 | tf_op jit(solution)/shard_map/ppermute | solution.py:180
  12.1 0.7 %transform_blocks.1.refs_4_ = bf16[8,256,256]{2,1,0:T(8,128)(2,1)S(1)} custom-call(f32[16,1,64,256]{3,2,1,0:T(8,128)S(1)} %get-tuple-element.18.fourier_ref), custom_call_target="tpu_custom_call" | custom-call | flops 805000000 | tf_op jit(solution)/shard_map/transform_blocks/pallas_call | solution.py:371
  12.8 0.8 %collective-permute-done.3 = f32[8,512]{1,0:T(8,128)S(1)} collective-permute-done((f32[8,512]{1,0:T(8,128)S(1)}, f32[8,512]{1,0:T(8,128)S(1)}, u32[]{:S(2)}, u32[]{:S(2)}) %collective-permute-start.3) | collective-permute-done | bytes 16416 | tf_op jit(solution)/shard_map/ppermute | solution.py:180
  13.6 1.6 %collective-permute-start.4 = (f32[4,512]{1,0:T(4,128)S(1)}, f32[4,512]{1,0:T(4,128)S(1)}, u32[]{:S(2)}, u32[]{:S(2)}) collective-permute-start(f32[4,512]{1,0:T(4,128)S(1)} %slice_add_fusion), channel_id=1, source_target_pairs={{0,3},{1,2},{2,1},{3,0},{4,7},{5,6},{6,5},{7,4},{8,11},{9,10},{10,... | collective-permute-start | bytes 24584 | tf_op jit(solution)/shard_map/ppermute | solution.py:180
  15.1 1.5 %collective-permute-done.4 = f32[4,512]{1,0:T(4,128)S(1)} collective-permute-done((f32[4,512]{1,0:T(4,128)S(1)}, f32[4,512]{1,0:T(4,128)S(1)}, u32[]{:S(2)}, u32[]{:S(2)}) %collective-permute-start.4) | collective-permute-done | bytes 8224 | tf_op jit(solution)/shard_map/ppermute | solution.py:180
  16.7 1.0 %finish.1 = f32[16,1,256]{2,1,0:T(1,128)} custom-call(f32[1,4,512]{2,1,0:T(4,128)S(1)} %fusion.refs_0_, f32[1,4,512]{2,1,0:T(4,128)S(1)} %bitcast.8, f32[2,4,16,128]{3,2,1,0:T(8,128)S(1)} %get-tuple-element.16.refs_2_, f32[16,256]{1,0:T(8,128)S(1)} %get-tuple-element.17.refs_3_, bf16[8,256,256]{2,1,0:T(8,128)(2,1)S(1)} %transform_blocks.1.refs_4_), custom_call_target="tpu_custom_call" | custom-call | flops 1495000064 | tf_op jit(solution)/shard_map/finish/pallas_call | solution.py:336
  (5 shorter events, 0.0 us)
Async XLA Ops:
  0.0 1.7 %collective-permute-start = (f32[1,1,4,8192]{3,2,1,0:T(4,128)}, f32[1,1,4,8192]{3,2,1,0:T(4,128)S(1)}, u32[]{:S(2)}, u32[]{:S(2)}) collective-permute-start(f32[1,1,4,8192]{3,2,1,0:T(4,128)} %term_hbm.1), channel_id=1, source_target_pairs={{0,1},{1,0},{2,3},{3,2},{4,5},{5,4},{6,7},{7,6},{8,9},{9,8},{10,11... | collective-permute-start | bytes 393224 | tf_op jit(solution)/shard_map/ppermute | solution.py:180
  2.0 4.1 %collective-permute-start.1 = (f32[8,512]{1,0:T(8,128)S(1)}, f32[8,512]{1,0:T(8,128)S(1)}, u32[]{:S(2)}, u32[]{:S(2)}) collective-permute-start(f32[8,512]{1,0:T(8,128)S(1)} %both_columns.1), channel_id=1, source_target_pairs={{0,5},{1,4},{2,7},{3,6},{4,1},{5,0},{6,3},{7,2},{8,13},{9,12},{10,... | collective-permute-start | bytes 49160 | tf_op jit(solution)/shard_map/ppermute | solution.py:180
  6.1 3.2 %collective-permute-start.2 = (f32[8,512]{1,0:T(8,128)S(1)}, f32[8,512]{1,0:T(8,128)S(1)}, u32[]{:S(2)}, u32[]{:S(2)}) collective-permute-start(f32[8,512]{1,0:T(8,128)S(1)} %add.15), channel_id=1, source_target_pairs={{0,9},{1,8},{2,11},{3,10},{4,13},{5,12},{6,15},{7,14},{8,1},{9,0},... | collective-permute-start | bytes 49160 | tf_op jit(solution)/shard_map/ppermute | solution.py:180
  9.4 4.2 %collective-permute-start.3 = (f32[8,512]{1,0:T(8,128)S(1)}, f32[8,512]{1,0:T(8,128)S(1)}, u32[]{:S(2)}, u32[]{:S(2)}) collective-permute-start(f32[8,512]{1,0:T(8,128)S(1)} %add.16), channel_id=1, source_target_pairs={{0,17},{1,16},{2,19},{3,18},{4,21},{5,20},{6,23},{7,22},{8,25},{9,... | collective-permute-start | bytes 49160 | tf_op jit(solution)/shard_map/ppermute | solution.py:180
  13.6 3.1 %collective-permute-start.4 = (f32[4,512]{1,0:T(4,128)S(1)}, f32[4,512]{1,0:T(4,128)S(1)}, u32[]{:S(2)}, u32[]{:S(2)}) collective-permute-start(f32[4,512]{1,0:T(4,128)S(1)} %slice_add_fusion), channel_id=1, source_target_pairs={{0,3},{1,2},{2,1},{3,0},{4,7},{5,6},{6,5},{7,4},{8,11},{9,10},{10,... | collective-permute-start | bytes 24584 | tf_op jit(solution)/shard_map/ppermute | solution.py:180

commit v8 on v7

--- a/solution.py
+++ b/solution.py
@@ -312,6 +312,7 @@
     keep = lane // WIN == lax.broadcasted_iota(jnp.int32, (8, LANE), 0) % 2
     here = lax.broadcasted_iota(jnp.int32, (8, block_ref.shape[2]), 0) // 2
     vis = block_ref.shape[2] // 2
+    lefts = []
     for first in range(0, blocks, 8):
         highs, lows = [], []
         for value in (real_row, imag_row):
@@ -319,16 +320,18 @@
             high = mine.astype(jnp.bfloat16).astype(jnp.float32)
             highs.append(jnp.concatenate([high, high], axis=1))
             lows.append(jnp.concatenate([mine - high, jnp.zeros_like(mine)], axis=1))
-        left = jnp.concatenate(highs + lows, axis=0).astype(jnp.bfloat16)
-        real_c, imag_c = 0.0, 0.0
-        for b in range(4):
-            wide = jnp.dot(left, block_ref[first // 2 + b], preferred_element_type=jnp.float32)
-            real_c = jnp.where(here == b, wide[:8] + wide[16:24], real_c)
-            imag_c = jnp.where(here == b, wide[8:16] + wide[24:], imag_c)
+        lefts.append(jnp.concatenate(highs + lows, axis=0).astype(jnp.bfloat16))
+    reals, imags = [0.0] * len(lefts), [0.0] * len(lefts)
+    for b in range(4):
+        for k, left in enumerate(lefts):
+            wide = jnp.dot(left, block_ref[4 * k + b], preferred_element_type=jnp.float32)
+            reals[k] = jnp.where(here == b, wide[:8] + wide[16:24], reals[k])
+            imags[k] = jnp.where(here == b, wide[8:16] + wide[24:], imags[k])
+    for k, (real_c, imag_c) in enumerate(zip(reals, imags)):
         real_v, imag_v = real_c[:, :vis] - imag_c[:, vis:], real_c[:, vis:] + imag_c[:, :vis]
         for b in range(8):
-            out_ref[first + b, :, :vis] = real_v[b : b + 1]
-            out_ref[first + b, :, vis:] = imag_v[b : b + 1]
+            out_ref[8 * k + b, :, :vis] = real_v[b : b + 1]
+            out_ref[8 * k + b, :, vis:] = imag_v[b : b + 1]
 
 
 def finish(pieces, weights, transformed):

time: 17.8 us -> 17.8 us (level)
  no operation moved by 1% of the time
where the time goes in v8:
time: 17.8 us; the launch traced here: 17.6 us
  starting transfers between devices  9.25 us (52%)
  Pallas kernels  4.37 us (25%)
  waiting for transfers between devices  3.94 us (22%)
    ppermute x5, starting transfers between devices, exchange(): return lax.ppermute(value, ('facet', 'chan'), pairs)  9.25 us
    ppermute x5, waiting for transfers between devices, exchange(): return lax.ppermute(value, ('facet', 'chan'), pairs)  3.94 us
    pallas_call x1, Pallas kernels, finish_weights(): pl.pallas_call(functools.partial(weight_kernel, rows), in_specs=[pl.Block...  1.27 us
    pallas_call x1, Pallas kernels, own_columns(): pl.pallas_call(functools.partial(own_kernel, math.gcd(subgrids, 4), step)...  1.22 us
    pallas_call x1, Pallas kernels, finish(): pl.pallas_call(functools.partial(finish_kernel, len(pieces)), in_specs=[p...  0.94 us
    pallas_call x1, Pallas kernels, transform_blocks(): pl.pallas_call(block_kernel, in_specs=[pl.BlockSpec(memory_space=pltpu.VM...  0.65 us
  transfers between devices with their start and end apart: 5, of which 4 were waited for; matrix products, arithmetic and copies ran while one was open for 0% of the time, Pallas kernels for 18%

profile of v8, /device:TPU:0, one launch (start us, length us, event | category | flops | bytes accessed | tf_op | source)
XLA Modules:
  0.0 17.6 jit_solution(5526335372381545389)
XLA Ops:
  0.0 0.5 %collective-permute-start = (f32[1,1,4,8192]{3,2,1,0:T(4,128)}, f32[1,1,4,8192]{3,2,1,0:T(4,128)S(1)}, u32[]{:S(2)}, u32[]{:S(2)}) collective-permute-start(f32[1,1,4,8192]{3,2,1,0:T(4,128)} %term_hbm.1), channel_id=1, source_target_pairs={{0,1},{1,0},{2,3},{3,2},{4,5},{5,4},{6,7},{7,6},{8,9},{9,8},{10,11... | collective-permute-start | bytes 393224 | tf_op jit(solution)/shard_map/ppermute | solution.py:180
  0.5 1.2 %own_columns.1 = (bf16[2,256,512]{2,1,0:T(8,128)(2,1)S(1)}, f32[12,256]{1,0:T(8,128)S(1)}, f32[4,512]{1,0:T(4,128)S(1)}) custom-call(s32[2,4]{1,0:T(2,128)} %bitcast.9, f32[1,1,4,8192]{3,2,1,0:T(4,128)} %term_hbm.1), custom_call_target="tpu_custom_call" | custom-call | flops 1610000000 | tf_op jit(solution)/shard_map/own_columns/pallas_call | solution.py:146
  1.7 0.0 collective-permute-done.term_ref
  1.7 0.3 %both_columns.1 = f32[8,512]{1,0:T(8,128)S(1)} custom-call(f32[1,1,4,8192]{3,2,1,0:T(4,128)S(1)} %collective-permute-done.term_ref, bf16[2,256,512]{2,1,0:T(8,128)(2,1)S(1)} %get-tuple-element.12.look_ref, f32[12,256]{1,0:T(8,128)S(1)} %get-tuple-element.13.turn_ref, f32[4,512]{1,0:T(4,128)S(1)} %get-tuple-element.14.own_ref), custom_call_target="tpu_custom_call" | custom-call | flops 402500000 | tf_op jit(solution)/shard_map/both_columns/pallas_call | solution.py:165
  2.0 2.7 %collective-permute-start.1 = (f32[8,512]{1,0:T(8,128)S(1)}, f32[8,512]{1,0:T(8,128)S(1)}, u32[]{:S(2)}, u32[]{:S(2)}) collective-permute-start(f32[8,512]{1,0:T(8,128)S(1)} %both_columns.1), channel_id=1, source_target_pairs={{0,5},{1,4},{2,7},{3,6},{4,1},{5,0},{6,3},{7,2},{8,13},{9,12},{10,... | collective-permute-start | bytes 49160 | tf_op jit(solution)/shard_map/ppermute | solution.py:180
  4.7 1.4 %collective-permute-done.1 = f32[8,512]{1,0:T(8,128)S(1)} collective-permute-done((f32[8,512]{1,0:T(8,128)S(1)}, f32[8,512]{1,0:T(8,128)S(1)}, u32[]{:S(2)}, u32[]{:S(2)}) %collective-permute-start.1) | collective-permute-done | bytes 16416 | tf_op jit(solution)/shard_map/ppermute | solution.py:180
  6.1 1.8 %collective-permute-start.2 = (f32[8,512]{1,0:T(8,128)S(1)}, f32[8,512]{1,0:T(8,128)S(1)}, u32[]{:S(2)}, u32[]{:S(2)}) collective-permute-start(f32[8,512]{1,0:T(8,128)S(1)} %add.15), channel_id=1, source_target_pairs={{0,9},{1,8},{2,11},{3,10},{4,13},{5,12},{6,15},{7,14},{8,1},{9,0},... | collective-permute-start | bytes 49160 | tf_op jit(solution)/shard_map/ppermute | solution.py:180
  7.9 1.3 %finish_weights.1 = (f32[2,4,16,128]{3,2,1,0:T(8,128)S(1)}, f32[16,256]{1,0:T(8,128)S(1)}, f32[2,8,512]{2,1,0:T(8,128)S(1)}, f32[16,1,64,256]{3,2,1,0:T(8,128)S(1)}) custom-call(s32[2,4]{1,0:T(2,128)} %bitcast.10, s32[4]{0:T(128)} %owner_hbm.1, s32[16]{0:T(128)} %tile_hbm.1, f32[4]{0:T(128)} %coord_hbm.1, f32[16,1,64,256]{3,2,1,0:T(8,128)} %fourier_hbm.1), custom_call_target="tpu_custom_call" | custom-call | flops 1495000064 | tf_op jit(solution)/shard_map/finish_weights/pallas_call | solution.py:268
  9.2 0.2 collective-permute-done.2
  9.4 2.7 %collective-permute-start.3 = (f32[8,512]{1,0:T(8,128)S(1)}, f32[8,512]{1,0:T(8,128)S(1)}, u32[]{:S(2)}, u32[]{:S(2)}) collective-permute-start(f32[8,512]{1,0:T(8,128)S(1)} %add.16), channel_id=1, source_target_pairs={{0,17},{1,16},{2,19},{3,18},{4,21},{5,20},{6,23},{7,22},{8,25},{9,... | collective-permute-start | bytes 49160 | tf_op jit(solution)/shard_map/ppermute | solution.py:180
  12.1 0.7 %transform_blocks.1.refs_4_ = bf16[8,256,256]{2,1,0:T(8,128)(2,1)S(1)} custom-call(f32[16,1,64,256]{3,2,1,0:T(8,128)S(1)} %get-tuple-element.18.fourier_ref), custom_call_target="tpu_custom_call" | custom-call | flops 805000000 | tf_op jit(solution)/shard_map/transform_blocks/pallas_call | solution.py:374
  12.8 0.8 %collective-permute-done.3 = f32[8,512]{1,0:T(8,128)S(1)} collective-permute-done((f32[8,512]{1,0:T(8,128)S(1)}, f32[8,512]{1,0:T(8,128)S(1)}, u32[]{:S(2)}, u32[]{:S(2)}) %collective-permute-start.3) | collective-permute-done | bytes 16416 | tf_op jit(solution)/shard_map/ppermute | solution.py:180
  13.6 1.6 %collective-permute-start.4 = (f32[4,512]{1,0:T(4,128)S(1)}, f32[4,512]{1,0:T(4,128)S(1)}, u32[]{:S(2)}, u32[]{:S(2)}) collective-permute-start(f32[4,512]{1,0:T(4,128)S(1)} %slice_add_fusion), channel_id=1, source_target_pairs={{0,3},{1,2},{2,1},{3,0},{4,7},{5,6},{6,5},{7,4},{8,11},{9,10},{10,... | collective-permute-start | bytes 24584 | tf_op jit(solution)/shard_map/ppermute | solution.py:180
  15.1 1.5 %collective-permute-done.4 = f32[4,512]{1,0:T(4,128)S(1)} collective-permute-done((f32[4,512]{1,0:T(4,128)S(1)}, f32[4,512]{1,0:T(4,128)S(1)}, u32[]{:S(2)}, u32[]{:S(2)}) %collective-permute-start.4) | collective-permute-done | bytes 8224 | tf_op jit(solution)/shard_map/ppermute | solution.py:180
  16.7 0.9 %finish.1 = f32[16,1,256]{2,1,0:T(1,128)} custom-call(f32[1,4,512]{2,1,0:T(4,128)S(1)} %fusion.refs_0_, f32[1,4,512]{2,1,0:T(4,128)S(1)} %bitcast.8, f32[2,4,16,128]{3,2,1,0:T(8,128)S(1)} %get-tuple-element.16.refs_2_, f32[16,256]{1,0:T(8,128)S(1)} %get-tuple-element.17.refs_3_, bf16[8,256,256]{2,1,0:T(8,128)(2,1)S(1)} %transform_blocks.1.refs_4_), custom_call_target="tpu_custom_call" | custom-call | flops 1495000064 | tf_op jit(solution)/shard_map/finish/pallas_call | solution.py:339
  (5 shorter events, 0.0 us)
Async XLA Ops:
  0.0 1.7 %collective-permute-start = (f32[1,1,4,8192]{3,2,1,0:T(4,128)}, f32[1,1,4,8192]{3,2,1,0:T(4,128)S(1)}, u32[]{:S(2)}, u32[]{:S(2)}) collective-permute-start(f32[1,1,4,8192]{3,2,1,0:T(4,128)} %term_hbm.1), channel_id=1, source_target_pairs={{0,1},{1,0},{2,3},{3,2},{4,5},{5,4},{6,7},{7,6},{8,9},{9,8},{10,11... | collective-permute-start | bytes 393224 | tf_op jit(solution)/shard_map/ppermute | solution.py:180
  2.0 4.1 %collective-permute-start.1 = (f32[8,512]{1,0:T(8,128)S(1)}, f32[8,512]{1,0:T(8,128)S(1)}, u32[]{:S(2)}, u32[]{:S(2)}) collective-permute-start(f32[8,512]{1,0:T(8,128)S(1)} %both_columns.1), channel_id=1, source_target_pairs={{0,5},{1,4},{2,7},{3,6},{4,1},{5,0},{6,3},{7,2},{8,13},{9,12},{10,... | collective-permute-start | bytes 49160 | tf_op jit(solution)/shard_map/ppermute | solution.py:180
  6.1 3.2 %collective-permute-start.2 = (f32[8,512]{1,0:T(8,128)S(1)}, f32[8,512]{1,0:T(8,128)S(1)}, u32[]{:S(2)}, u32[]{:S(2)}) collective-permute-start(f32[8,512]{1,0:T(8,128)S(1)} %add.15), channel_id=1, source_target_pairs={{0,9},{1,8},{2,11},{3,10},{4,13},{5,12},{6,15},{7,14},{8,1},{9,0},... | collective-permute-start | bytes 49160 | tf_op jit(solution)/shard_map/ppermute | solution.py:180
  9.4 4.2 %collective-permute-start.3 = (f32[8,512]{1,0:T(8,128)S(1)}, f32[8,512]{1,0:T(8,128)S(1)}, u32[]{:S(2)}, u32[]{:S(2)}) collective-permute-start(f32[8,512]{1,0:T(8,128)S(1)} %add.16), channel_id=1, source_target_pairs={{0,17},{1,16},{2,19},{3,18},{4,21},{5,20},{6,23},{7,22},{8,25},{9,... | collective-permute-start | bytes 49160 | tf_op jit(solution)/shard_map/ppermute | solution.py:180
  13.6 3.1 %collective-permute-start.4 = (f32[4,512]{1,0:T(4,128)S(1)}, f32[4,512]{1,0:T(4,128)S(1)}, u32[]{:S(2)}, u32[]{:S(2)}) collective-permute-start(f32[4,512]{1,0:T(4,128)S(1)} %slice_add_fusion), channel_id=1, source_target_pairs={{0,3},{1,2},{2,1},{3,0},{4,7},{5,6},{6,5},{7,4},{8,11},{9,10},{10,... | collective-permute-start | bytes 24584 | tf_op jit(solution)/shard_map/ppermute | solution.py:180

commit v9 on v8

--- a/solution.py
+++ b/solution.py
@@ -183,10 +183,10 @@
 def gather_channel(both, mix, facets, chans):
     near = SIDE if facets > SIDE else facets
     rows = both.shape[0] // 2
-    step = 1
-    while step < near:
+    step = near
+    while step > 1:
+        step //= 2
         both = both + exchange(both, facets, chans, step, 1)
-        step *= 2
     parts = []
     for k in range(chans // 2):
         weighted = both * mix[k]

time: 17.8 us -> 17.8 us (level)
  starting transfers between devices: 9.25 us -> 8.96 us
  waiting for transfers between devices: 3.94 us -> 4.22 us
    ppermute x5, waiting for transfers between devices: 3.94 us -> 4.22 us  [exchange(): return lax.ppermute(value, ('facet', 'chan'), pairs)]
    ppermute x5, starting transfers between devices: 9.25 us -> 8.96 us  [exchange(): return lax.ppermute(value, ('facet', 'chan'), pairs)]
where the time goes in v9:
time: 17.8 us; the launch traced here: 17.6 us
  starting transfers between devices  8.96 us (50%)
  Pallas kernels  4.37 us (25%)
  waiting for transfers between devices  4.22 us (24%)
    ppermute x5, starting transfers between devices, exchange(): return lax.ppermute(value, ('facet', 'chan'), pairs)  8.96 us
    ppermute x5, waiting for transfers between devices, exchange(): return lax.ppermute(value, ('facet', 'chan'), pairs)  4.22 us
    pallas_call x1, Pallas kernels, finish_weights(): pl.pallas_call(functools.partial(weight_kernel, rows), in_specs=[pl.Block...  1.27 us
    pallas_call x1, Pallas kernels, own_columns(): pl.pallas_call(functools.partial(own_kernel, math.gcd(subgrids, 4), step)...  1.22 us
    pallas_call x1, Pallas kernels, finish(): pl.pallas_call(functools.partial(finish_kernel, len(pieces)), in_specs=[p...  0.94 us
    pallas_call x1, Pallas kernels, transform_blocks(): pl.pallas_call(block_kernel, in_specs=[pl.BlockSpec(memory_space=pltpu.VM...  0.65 us
  transfers between devices with their start and end apart: 5, of which 4 were waited for; matrix products, arithmetic and copies ran while one was open for 0% of the time, Pallas kernels for 18%

profile of v9, /device:TPU:0, one launch (start us, length us, event | category | flops | bytes accessed | tf_op | source)
XLA Modules:
  0.0 17.6 jit_solution(14674203539929307107)
XLA Ops:
  0.0 0.5 %collective-permute-start = (f32[1,1,4,8192]{3,2,1,0:T(4,128)}, f32[1,1,4,8192]{3,2,1,0:T(4,128)S(1)}, u32[]{:S(2)}, u32[]{:S(2)}) collective-permute-start(f32[1,1,4,8192]{3,2,1,0:T(4,128)} %term_hbm.1), channel_id=1, source_target_pairs={{0,1},{1,0},{2,3},{3,2},{4,5},{5,4},{6,7},{7,6},{8,9},{9,8},{10,11... | collective-permute-start | bytes 393224 | tf_op jit(solution)/shard_map/ppermute | solution.py:180
  0.5 1.2 %own_columns.1 = (bf16[2,256,512]{2,1,0:T(8,128)(2,1)S(1)}, f32[12,256]{1,0:T(8,128)S(1)}, f32[4,512]{1,0:T(4,128)S(1)}) custom-call(s32[2,4]{1,0:T(2,128)} %bitcast.9, f32[1,1,4,8192]{3,2,1,0:T(4,128)} %term_hbm.1), custom_call_target="tpu_custom_call" | custom-call | flops 1610000000 | tf_op jit(solution)/shard_map/own_columns/pallas_call | solution.py:146
  1.7 0.0 collective-permute-done.term_ref
  1.7 0.3 %both_columns.1 = f32[8,512]{1,0:T(8,128)S(1)} custom-call(f32[1,1,4,8192]{3,2,1,0:T(4,128)S(1)} %collective-permute-done.term_ref, bf16[2,256,512]{2,1,0:T(8,128)(2,1)S(1)} %get-tuple-element.12.look_ref, f32[12,256]{1,0:T(8,128)S(1)} %get-tuple-element.13.turn_ref, f32[4,512]{1,0:T(4,128)S(1)} %get-tuple-element.14.own_ref), custom_call_target="tpu_custom_call" | custom-call | flops 402500000 | tf_op jit(solution)/shard_map/both_columns/pallas_call | solution.py:165
  2.0 3.8 %collective-permute-start.1 = (f32[8,512]{1,0:T(8,128)S(1)}, f32[8,512]{1,0:T(8,128)S(1)}, u32[]{:S(2)}, u32[]{:S(2)}) collective-permute-start(f32[8,512]{1,0:T(8,128)S(1)} %both_columns.1), channel_id=1, source_target_pairs={{0,17},{1,16},{2,19},{3,18},{4,21},{5,20},{6,23},{7,22},{8,25},{9,... | collective-permute-start | bytes 49160 | tf_op jit(solution)/shard_map/ppermute | solution.py:180
  5.8 1.4 %collective-permute-done.1 = f32[8,512]{1,0:T(8,128)S(1)} collective-permute-done((f32[8,512]{1,0:T(8,128)S(1)}, f32[8,512]{1,0:T(8,128)S(1)}, u32[]{:S(2)}, u32[]{:S(2)}) %collective-permute-start.1) | collective-permute-done | bytes 16416 | tf_op jit(solution)/shard_map/ppermute | solution.py:180
  7.2 1.6 %collective-permute-start.2 = (f32[8,512]{1,0:T(8,128)S(1)}, f32[8,512]{1,0:T(8,128)S(1)}, u32[]{:S(2)}, u32[]{:S(2)}) collective-permute-start(f32[8,512]{1,0:T(8,128)S(1)} %add.15), channel_id=1, source_target_pairs={{0,9},{1,8},{2,11},{3,10},{4,13},{5,12},{6,15},{7,14},{8,1},{9,0},... | collective-permute-start | bytes 49160 | tf_op jit(solution)/shard_map/ppermute | solution.py:180
  8.8 1.3 %finish_weights.1 = (f32[2,4,16,128]{3,2,1,0:T(8,128)S(1)}, f32[16,256]{1,0:T(8,128)S(1)}, f32[2,8,512]{2,1,0:T(8,128)S(1)}, f32[16,1,64,256]{3,2,1,0:T(8,128)S(1)}) custom-call(s32[2,4]{1,0:T(2,128)} %bitcast.10, s32[4]{0:T(128)} %owner_hbm.1, s32[16]{0:T(128)} %tile_hbm.1, f32[4]{0:T(128)} %coord_hbm.1, f32[16,1,64,256]{3,2,1,0:T(8,128)} %fourier_hbm.1), custom_call_target="tpu_custom_call" | custom-call | flops 1495000064 | tf_op jit(solution)/shard_map/finish_weights/pallas_call | solution.py:268
  10.1 0.3 %collective-permute-done.2 = f32[8,512]{1,0:T(8,128)S(1)} collective-permute-done((f32[8,512]{1,0:T(8,128)S(1)}, f32[8,512]{1,0:T(8,128)S(1)}, u32[]{:S(2)}, u32[]{:S(2)}) %collective-permute-start.2) | collective-permute-done | bytes 16416 | tf_op jit(solution)/shard_map/ppermute | solution.py:180
  10.4 1.6 %collective-permute-start.3 = (f32[8,512]{1,0:T(8,128)S(1)}, f32[8,512]{1,0:T(8,128)S(1)}, u32[]{:S(2)}, u32[]{:S(2)}) collective-permute-start(f32[8,512]{1,0:T(8,128)S(1)} %add.16), channel_id=1, source_target_pairs={{0,5},{1,4},{2,7},{3,6},{4,1},{5,0},{6,3},{7,2},{8,13},{9,12},{10,... | collective-permute-start | bytes 49160 | tf_op jit(solution)/shard_map/ppermute | solution.py:180
  11.9 0.7 %transform_blocks.1.refs_4_ = bf16[8,256,256]{2,1,0:T(8,128)(2,1)S(1)} custom-call(f32[16,1,64,256]{3,2,1,0:T(8,128)S(1)} %get-tuple-element.18.fourier_ref), custom_call_target="tpu_custom_call" | custom-call | flops 805000000 | tf_op jit(solution)/shard_map/transform_blocks/pallas_call | solution.py:374
  12.6 1.0 %collective-permute-done.3 = f32[8,512]{1,0:T(8,128)S(1)} collective-permute-done((f32[8,512]{1,0:T(8,128)S(1)}, f32[8,512]{1,0:T(8,128)S(1)}, u32[]{:S(2)}, u32[]{:S(2)}) %collective-permute-start.3) | collective-permute-done | bytes 16416 | tf_op jit(solution)/shard_map/ppermute | solution.py:180
  13.6 1.6 %collective-permute-start.4 = (f32[4,512]{1,0:T(4,128)S(1)}, f32[4,512]{1,0:T(4,128)S(1)}, u32[]{:S(2)}, u32[]{:S(2)}) collective-permute-start(f32[4,512]{1,0:T(4,128)S(1)} %slice_add_fusion), channel_id=1, source_target_pairs={{0,3},{1,2},{2,1},{3,0},{4,7},{5,6},{6,5},{7,4},{8,11},{9,10},{10,... | collective-permute-start | bytes 24584 | tf_op jit(solution)/shard_map/ppermute | solution.py:180
  15.1 1.5 %collective-permute-done.4 = f32[4,512]{1,0:T(4,128)S(1)} collective-permute-done((f32[4,512]{1,0:T(4,128)S(1)}, f32[4,512]{1,0:T(4,128)S(1)}, u32[]{:S(2)}, u32[]{:S(2)}) %collective-permute-start.4) | collective-permute-done | bytes 8224 | tf_op jit(solution)/shard_map/ppermute | solution.py:180
  16.7 0.9 %finish.1 = f32[16,1,256]{2,1,0:T(1,128)} custom-call(f32[1,4,512]{2,1,0:T(4,128)S(1)} %fusion.refs_0_, f32[1,4,512]{2,1,0:T(4,128)S(1)} %bitcast.8, f32[2,4,16,128]{3,2,1,0:T(8,128)S(1)} %get-tuple-element.16.refs_2_, f32[16,256]{1,0:T(8,128)S(1)} %get-tuple-element.17.refs_3_, bf16[8,256,256]{2,1,0:T(8,128)(2,1)S(1)} %transform_blocks.1.refs_4_), custom_call_target="tpu_custom_call" | custom-call | flops 1495000064 | tf_op jit(solution)/shard_map/finish/pallas_call | solution.py:339
  (5 shorter events, 0.0 us)
Async XLA Ops:
  0.0 1.7 %collective-permute-start = (f32[1,1,4,8192]{3,2,1,0:T(4,128)}, f32[1,1,4,8192]{3,2,1,0:T(4,128)S(1)}, u32[]{:S(2)}, u32[]{:S(2)}) collective-permute-start(f32[1,1,4,8192]{3,2,1,0:T(4,128)} %term_hbm.1), channel_id=1, source_target_pairs={{0,1},{1,0},{2,3},{3,2},{4,5},{5,4},{6,7},{7,6},{8,9},{9,8},{10,11... | collective-permute-start | bytes 393224 | tf_op jit(solution)/shard_map/ppermute | solution.py:180
  2.0 5.2 %collective-permute-start.1 = (f32[8,512]{1,0:T(8,128)S(1)}, f32[8,512]{1,0:T(8,128)S(1)}, u32[]{:S(2)}, u32[]{:S(2)}) collective-permute-start(f32[8,512]{1,0:T(8,128)S(1)} %both_columns.1), channel_id=1, source_target_pairs={{0,17},{1,16},{2,19},{3,18},{4,21},{5,20},{6,23},{7,22},{8,25},{9,... | collective-permute-start | bytes 49160 | tf_op jit(solution)/shard_map/ppermute | solution.py:180
  7.2 3.2 %collective-permute-start.2 = (f32[8,512]{1,0:T(8,128)S(1)}, f32[8,512]{1,0:T(8,128)S(1)}, u32[]{:S(2)}, u32[]{:S(2)}) collective-permute-start(f32[8,512]{1,0:T(8,128)S(1)} %add.15), channel_id=1, source_target_pairs={{0,9},{1,8},{2,11},{3,10},{4,13},{5,12},{6,15},{7,14},{8,1},{9,0},... | collective-permute-start | bytes 49160 | tf_op jit(solution)/shard_map/ppermute | solution.py:180
  10.4 3.2 %collective-permute-start.3 = (f32[8,512]{1,0:T(8,128)S(1)}, f32[8,512]{1,0:T(8,128)S(1)}, u32[]{:S(2)}, u32[]{:S(2)}) collective-permute-start(f32[8,512]{1,0:T(8,128)S(1)} %add.16), channel_id=1, source_target_pairs={{0,5},{1,4},{2,7},{3,6},{4,1},{5,0},{6,3},{7,2},{8,13},{9,12},{10,... | collective-permute-start | bytes 49160 | tf_op jit(solution)/shard_map/ppermute | solution.py:180
  13.6 3.1 %collective-permute-start.4 = (f32[4,512]{1,0:T(4,128)S(1)}, f32[4,512]{1,0:T(4,128)S(1)}, u32[]{:S(2)}, u32[]{:S(2)}) collective-permute-start(f32[4,512]{1,0:T(4,128)S(1)} %slice_add_fusion), channel_id=1, source_target_pairs={{0,3},{1,2},{2,1},{3,0},{4,7},{5,6},{6,5},{7,4},{8,11},{9,10},{10,... | collective-permute-start | bytes 24584 | tf_op jit(solution)/shard_map/ppermute | solution.py:180
